TPU v7x, 256 devices: a whole 4x4x8 slice. The times are simulated.
256 devices in a mesh: chan: 64 (over z, y, core), panel: 4 (over x).
Axes of the slice: x: 4, y: 4, z: 8, core: 2. Of those that a mesh axis runs over, the one named last changes fastest.
Arguments:
- eta: bfloat16 [128, 1024, 1024], P('chan', 'panel'), as said below
- gamma: bfloat16 [128, 1024, 1024], P('chan', 'panel')
- pp_weight: float32 [128, 1024], P('chan'), may hold values from -1 to 1
- cc_weight: float32 [128, 1024], P('chan'), may hold values from -1 to 1
- live_pairs: int32 [128], P('chan'), may hold values from 256 to 1024, as said below
- forward_table: bfloat16 [128, 128], replicated, may hold values from -0.5 to 0.5
- back_table: bfloat16 [128, 128], replicated, may hold values from -0.5 to 0.5
Outputs:
- commutator: bfloat16 [128, 1024, 1024], P('chan', 'panel')
Inputs may be any that keep to these rules, and one draw needn't show every extreme that they name: eta[j] is exactly antisymmetric and gamma[j] exactly symmetric for every channel j. `live_pairs`: each value is a multiple of 256.
All inputs are finite; a program needn't handle non-finite values.
Results may differ from a plain program's by a relative error of at most 0.0067.
Values may be sent and summed in bfloat16 or wider, within the bound.
No kernel may reach another device: no remote copies, remote signals or barrier semaphores. Data moves between devices by JAX's collectives and lax.ppermute only.
A program may use at most 128 MiB of HBM per device.

v0:
```python
import jax
import jax.numpy as jnp
from jax import lax
from jax.experimental import pallas as pl
from jax.experimental.pallas import tpu as pltpu
from jax.sharding import PartitionSpec as P

BF16 = jnp.bfloat16
F32 = jnp.float32
OFFSETS = (0, 1, -2, 3, 4)
LANES = 128


def params():
    return pltpu.CompilerParams(vmem_limit_bytes=48 * 1024 * 1024)


def cost(flops, size):
    return pl.CostEstimate(flops=flops, bytes_accessed=size, transcendentals=0)


def tile_at(panel, l, offset):
    return pl.multiple_of(lax.rem(2 * panel + l + offset + 8, 8) * LANES, LANES)


def swap_blocks(x):
    lane = lax.broadcasted_iota(jnp.int32, (64, LANES), 1)
    top, bottom = x[:64], x[64:]
    low = lane < 64
    upper = jnp.where(low, top, pltpu.roll(bottom, 64, 1))
    lower = jnp.where(low, pltpu.roll(top, 64, 1), bottom)
    even = (lane[:32] & 32) == 0
    parts = []
    for half in (upper, lower):
        first, second = half[:32], half[32:]
        parts.append(jnp.where(even, first, pltpu.roll(second, 32, 1)))
        parts.append(jnp.where(even, pltpu.roll(first, 96, 1), second))
    return jnp.concatenate(parts, axis=0)


def contract_last(a, b):
    return lax.dot_general(a, b, (((1,), (1,)), ((), ())), preferred_element_type=F32)


def pack_kernel(eta_ref, gamma_ref, out_ref):
    panel = lax.axis_index("panel")
    for arr, ref in enumerate((eta_ref, gamma_ref)):
        for l in range(2):
            for t, offset in enumerate(OFFSETS):
                column = tile_at(panel, l, offset)
                rows = [ref[ch, l * 128 : (l + 1) * 128, pl.ds(column, LANES)].astype(F32).reshape(16, 8, LANES) for ch in range(2)]
                start = arr * 32 + l * 16
                out_ref[start : start + 16, t] = jnp.concatenate(rows, axis=1).astype(BF16)


def spread_kernel(forward_ref, back_ref, forward_out, back_out):
    for ref, out, shift in ((forward_ref, forward_out, 3), (back_ref, back_out, 2)):
        size = 128 << shift
        row = lax.broadcasted_iota(jnp.int32, (size, 128), 0) >> shift
        column = lax.broadcasted_iota(jnp.int32, (size, 128), 1)
        copies = jnp.where(row == column, F32(1.0), F32(0.0)).astype(BF16)
        tall = jnp.dot(copies, ref[...], preferred_element_type=F32).astype(BF16)
        mask = (1 << shift) - 1
        for start in range(0, size, 256):
            wide = contract_last(tall[start : start + 256], copies)
            row = lax.broadcasted_iota(jnp.int32, wide.shape, 0) & mask
            column = lax.broadcasted_iota(jnp.int32, wide.shape, 1) & mask
            out[start : start + 256, :] = jnp.where(row == column, wide, F32(0.0)).astype(BF16)


def recouple_kernel(table_ref, in_ref, out_ref):
    rhs = jnp.concatenate([in_ref[:, q].reshape(1024, LANES) for q in range(5)], axis=1)
    mixed = jnp.dot(table_ref[...], rhs, preferred_element_type=F32).astype(BF16)
    for q in range(5):
        out_ref[:, q] = mixed[:, q * LANES : (q + 1) * LANES].reshape(64, 16, LANES)


def tile_of(ref, arr, l, t, ch):
    start = arr * 32 + l * 16
    return ref[start : start + 16, t].astype(F32)[:, ch * 8 : ch * 8 + 8].reshape(128, LANES)


PLUS = ((1, 1), (0, 3))
MINUS = ((0, 2), (1, 2))
FAR = ((1, 3),)


def mirror_kernel(in_ref, plus_ref, minus_ref, far_ref):
    for arr in range(2):
        for ch in range(2):
            for ref, held in ((plus_ref, PLUS), (minus_ref, MINUS), (far_ref, FAR)):
                for u, (l, t) in enumerate(held):
                    ref[(arr * 2 + ch) * len(held) + u] = swap_blocks(tile_of(in_ref, arr, l, t, ch).T).astype(BF16)


def product_kernel(in_ref, plus_ref, minus_ref, far_ref, weight_ref, out_ref, scaled, plain):
    panel = lax.axis_index("panel")
    for ch in range(2):
        for l in range(2):
            weight = weight_ref[ch : ch + 1, pl.ds(tile_at(panel, l, 0), LANES)]

            def put(arr, offset, value):
                rows = pl.ds(tile_at(panel, l, offset), LANES)
                columns = slice(l * LANES, (l + 1) * LANES)
                if arr == 0:
                    scaled[ch, rows, columns] = (value * weight).astype(BF16)
                else:
                    plain[ch, rows, columns] = value.astype(BF16)

            for arr in range(2):
                base = arr * 2 + ch
                for t, offset in enumerate(OFFSETS):
                    tile = swap_blocks(tile_of(in_ref, arr, l, t, ch))
                    put(arr, offset, -tile if arr == 0 else tile)
                put(arr, 2, minus_ref[base * 2 + l].astype(F32))
                if l == 0:
                    put(arr, -1, plus_ref[base * 2].astype(F32))
                    put(arr, -3, far_ref[base].astype(F32))
                else:
                    put(arr, -1, swap_blocks(tile_of(in_ref, arr, 0, 1, ch).T))
                    put(arr, -3, plus_ref[base * 2 + 1].astype(F32))
        for owner in range(4):
            rows = slice(owner * 256, (owner + 1) * 256)
            total = contract_last(scaled[ch, rows], plain[ch]) + contract_last(plain[ch, rows], scaled[ch])
            for l in range(2):
                for t, offset in enumerate(OFFSETS):
                    column = (2 * owner + l + offset) % 8 * LANES
                    out_ref[owner, l, t, ch] = total[l * 128 : (l + 1) * 128, column : column + LANES].astype(BF16)


def sum_kernel(in_ref, out_ref):
    for l in range(2):
        low, high = [], []
        for t in range(5):
            both = []
            for ch in range(2):
                parts = [in_ref[p, l, t, ch].astype(F32) for p in range(4)]
                total = (parts[0] + parts[1]) + (parts[2] + parts[3])
                both.append(swap_blocks(total).reshape(16, 8, LANES))
            low += [both[0][:, :4], both[1][:, :4]]
            high += [both[0][:, 4:], both[1][:, 4:]]
        out_ref[l * 32 : l * 32 + 16] = jnp.concatenate(low, axis=1).astype(BF16)
        out_ref[l * 32 + 16 : l * 32 + 32] = jnp.concatenate(high, axis=1).astype(BF16)


def recouple_back_kernel(table_ref, in_ref, out_ref):
    value = in_ref[...].astype(F32)
    rhs = jnp.concatenate([value[:, q * 8 : q * 8 + 8].reshape(512, LANES) for q in range(5)], axis=1).astype(BF16)
    mixed = jnp.dot(table_ref[...], rhs, preferred_element_type=F32)
    pieces = [mixed[:, q * LANES : (q + 1) * LANES].reshape(64, 8, LANES) for q in range(5)]
    out_ref[...] = jnp.concatenate(pieces, axis=1).astype(BF16)


def back_tile(ref, l, t, ch):
    low = ref[l * 32 : l * 32 + 16].astype(F32)[:, t * 8 + ch * 4 : t * 8 + ch * 4 + 4]
    high = ref[l * 32 + 16 : l * 32 + 32].astype(F32)[:, t * 8 + ch * 4 : t * 8 + ch * 4 + 4]
    return jnp.concatenate([low, high], axis=1).reshape(128, LANES)


def back_mirror_kernel(in_ref, plus_ref, minus_ref, far_ref):
    for ch in range(2):
        for ref, held in ((plus_ref, PLUS), (minus_ref, MINUS), (far_ref, FAR)):
            for u, (l, t) in enumerate(held):
                ref[ch * len(held) + u] = back_tile(in_ref, l, t, ch).astype(BF16)


def finish_kernel(in_ref, plus_ref, minus_ref, far_ref, pp_ref, out_ref):
    panel = lax.axis_index("panel")
    for ch in range(2):
        for l in range(2):
            rows = slice(l * 128, (l + 1) * 128)

            def put(offset, value):
                columns = pl.ds(tile_at(panel, l, offset), LANES)
                out_ref[ch, rows, columns] = (pp_ref[ch, rows, columns] + value).astype(BF16)

            for t, offset in enumerate(OFFSETS):
                put(offset, back_tile(in_ref, l, t, ch).T)
            put(2, minus_ref[ch * 2 + l].astype(F32))
            if l == 0:
                put(-1, plus_ref[ch * 2].astype(F32))
                put(-3, far_ref[ch].astype(F32))
            else:
                put(-1, back_tile(in_ref, 0, 1, ch))
                put(-3, plus_ref[ch * 2 + 1].astype(F32))


def pair_kernel(eta_ref, gamma_ref, eta_all_ref, gamma_all_ref, weight_ref, out_ref):
    weight = weight_ref[0]
    own = (eta_ref[0].astype(F32) * weight).astype(BF16)
    other = (eta_all_ref[0].astype(F32) * weight).astype(BF16)
    out_ref[0] = contract_last(own, gamma_all_ref[0]) + contract_last(gamma_ref[0], other)


def pair_part(eta, gamma, eta_all, gamma_all, weight):
    step = 256
    return pl.pallas_call(
        pair_kernel,
        grid=(2, 1024 // step),
        in_specs=[
            pl.BlockSpec((1, 256, 1024), lambda c, q: (c, 0, 0)),
            pl.BlockSpec((1, 256, 1024), lambda c, q: (c, 0, 0)),
            pl.BlockSpec((1, step, 1024), lambda c, q: (c, q, 0)),
            pl.BlockSpec((1, step, 1024), lambda c, q: (c, q, 0)),
            pl.BlockSpec((1, 1, 1024), lambda c, q: (c, 0, 0)),
        ],
        out_specs=pl.BlockSpec((1, 256, step), lambda c, q: (c, 0, q)),
        out_shape=jax.ShapeDtypeStruct((2, 256, 1024), F32),
        compiler_params=params(),
        cost_estimate=cost(2 * 2 * 2 * 256 * 1024 * 1024, 12 * 1024 * 1024),
        name="pair_part",
    )(eta, gamma, eta_all, gamma_all, weight.reshape(2, 1, 1024))


def call(kernel, shapes, args, flops=0, scratch=(), name=None):
    single = not isinstance(shapes, list)
    outs = [shapes] if single else shapes
    shaped = [jax.ShapeDtypeStruct(s, BF16) for s in outs]
    size = sum(a.size * a.dtype.itemsize for a in args) + sum(2 * s.size for s in shaped)
    return pl.pallas_call(
        kernel,
        out_shape=shaped[0] if single else shaped,
        scratch_shapes=list(scratch),
        compiler_params=params(),
        cost_estimate=cost(flops, size),
        name=name,
    )(*args)


def exchange(operand, axis):
    return lax.all_to_all(operand, axis, split_axis=0, concat_axis=0, tiled=True)


def mirror(plus, minus, far):
    def step(value, by):
        return lax.ppermute(value, "panel", [(i, (i + by) % 4) for i in range(4)])

    return step(plus, 1), step(minus, 3), step(far, 2)


def shards(eta, gamma, pp_weight, cc_weight, live_pairs, forward_table, back_table):
    positions = lax.broadcasted_iota(jnp.int32, pp_weight.shape, 1)
    weight_pp = jnp.where(positions < live_pairs[:, None], pp_weight, F32(0.0))
    eta_all = lax.all_gather(eta, "panel", axis=1, tiled=True)
    gamma_all = lax.all_gather(gamma, "panel", axis=1, tiled=True)

    packed = call(pack_kernel, (64, 5, 16, LANES), (eta, gamma), name="pack")
    forward_wide, back_wide = call(spread_kernel, [(1024, 1024), (512, 512)], (forward_table, back_table), flops=600_000_000, name="spread")
    packed = exchange(packed, "chan")
    mixed = call(recouple_kernel, (64, 5, 16, LANES), (forward_wide, packed), flops=1_400_000_000, name="recouple")
    mixed = exchange(mixed, "chan")
    sends = call(mirror_kernel, [(8, 128, LANES), (8, 128, LANES), (4, 128, LANES)], (mixed,), name="mirror")
    received = mirror(*sends)
    partial = call(
        product_kernel,
        (4, 2, 5, 2, 128, LANES),
        (mixed, *received, cc_weight),
        flops=2_200_000_000,
        scratch=[pltpu.VMEM((2, 1024, 256), BF16)] * 2,
        name="product",
    )
    partial = exchange(partial, "panel")
    part = call(sum_kernel, (64, 40, LANES), (partial,), name="sum")
    part = exchange(part, "chan")
    part = call(recouple_back_kernel, (64, 40, LANES), (back_wide, part), flops=400_000_000, name="recouple_back")
    part = exchange(part, "chan")
    back_sends = call(back_mirror_kernel, [(4, 128, LANES), (4, 128, LANES), (2, 128, LANES)], (part,), name="back_mirror")
    back_received = mirror(*back_sends)
    pp_part = pair_part(eta, gamma, eta_all, gamma_all, weight_pp)
    return call(finish_kernel, (2, 256, 1024), (part, *back_received, pp_part), name="finish")


def solution(mesh):
    in_specs = (
        P("chan", "panel", None),
        P("chan", "panel", None),
        P("chan", None),
        P("chan", None),
        P("chan"),
        P(),
        P(),
    )
    out_specs = P("chan", "panel", None)
    return jax.shard_map(shards, mesh=mesh, in_specs=in_specs, out_specs=out_specs, check_vma=False)
```

profile of v0, /device:TPU:1, one launch (start us, length us, event | category | flops | bytes accessed | tf_op | source)
XLA Modules:
  0.0 239.9 jit_solution(10554548671902060191)
XLA Ops:
  9.7 1.4 pack.1
  11.1 13.3 %all-to-all-start = ((bf16[64,5,16,128]{3,2,1,0:T(8,128)(2,1)}), bf16[64,5,16,128]{3,2,1,0:T(8,128)(2,1)S(1)}, u32[]{:S(2)}, u32[]{:S(2)}) async-start(bf16[64,5,16,128]{3,2,1,0:T(8,128)(2,1)} %pack.1), calls=%async_computation | async-start | bytes 2621440 | tf_op jit(solution)/shard_map/all_to_all | solution.py:231
  25.5 1.4 copy-done.7
  26.8 31.2 %all-to-all-done.in_ref = bf16[64,5,16,128]{3,2,1,0:T(8,128)(2,1)S(1)} async-done(((bf16[64,5,16,128]{3,2,1,0:T(8,128)(2,1)}), bf16[64,5,16,128]{3,2,1,0:T(8,128)(2,1)S(1)}, u32[]{:S(2)}, u32[]{:S(2)}) %all-to-all-start) | async-done | bytes 1310752 | tf_op jit(solution)/shard_map/all_to_all | solution.py:231
  58.0 1.6 copy-done.8
  59.6 2.9 %recouple.1 = bf16[64,5,16,128]{3,2,1,0:T(8,128)(2,1)} custom-call(bf16[1024,1024]{1,0:T(8,128)(2,1)S(1)} %copy-done.8, bf16[64,5,16,128]{3,2,1,0:T(8,128)(2,1)S(1)} %all-to-all-done.in_ref), custom_call_target="tpu_custom_call" | custom-call | flops 1400000000 | bytes 4718592 | tf_op jit(solution)/shard_map/recouple/pallas_call | solution.py:220
  62.5 6.5 %all-to-all-start.1 = ((bf16[64,5,16,128]{3,2,1,0:T(8,128)(2,1)}), bf16[64,5,16,128]{3,2,1,0:T(8,128)(2,1)S(1)}, u32[]{:S(2)}, u32[]{:S(2)}) async-start(bf16[64,5,16,128]{3,2,1,0:T(8,128)(2,1)} %recouple.1), calls=%async_computation.1 | async-start | bytes 2621440 | tf_op jit(solution)/shard_map/all_to_all | solution.py:231
  69.7 32.9 %all-to-all-done.1.in_ref = bf16[64,5,16,128]{3,2,1,0:T(8,128)(2,1)S(1)} async-done(((bf16[64,5,16,128]{3,2,1,0:T(8,128)(2,1)}), bf16[64,5,16,128]{3,2,1,0:T(8,128)(2,1)S(1)}, u32[]{:S(2)}, u32[]{:S(2)}) %all-to-all-start.1) | async-done | bytes 1310752 | tf_op jit(solution)/shard_map/all_to_all | solution.py:231
  102.6 1.3 mirror.1
  103.9 1.3 collective-permute-start
  105.1 1.5 collective-permute-start.1
  106.6 1.5 collective-permute-start.2
  108.1 16.9 %collective-permute-done.2.far_ref = bf16[4,128,128]{2,1,0:T(8,128)(2,1)S(1)} collective-permute-done((bf16[4,128,128]{2,1,0:T(8,128)(2,1)S(1)}, bf16[4,128,128]{2,1,0:T(8,128)(2,1)S(1)}, u32[]{:S(2)}, u32[]{:S(2)}) %collective-permute-start.2) | collective-permute-done | bytes 131104 | tf_op jit(solution)/shard_map/ppermute | solution.py:236
  125.1 3.3 %product.1 = bf16[4,2,5,2,128,128]{5,4,3,2,1,0:T(8,128)(2,1)S(1)} custom-call(bf16[64,5,16,128]{3,2,1,0:T(8,128)(2,1)S(1)} %all-to-all-done.1.in_ref, bf16[8,128,128]{2,1,0:T(8,128)(2,1)S(1)} %collective-permute-done.plus_ref, bf16[8,128,128]{2,1,0:T(8,128)(2,1)S(1)} %collective-permute-done.1.minus_ref, ...), custom_call_target="tpu_custom_call" | custom-call | flops 2200000000 | bytes 4595712 | tf_op jit(solution)/shard_map/product/pallas_call | solution.py:220
  128.4 31.5 %all_to_all.25.in_ref = bf16[4,2,5,2,128,128]{5,4,3,2,1,0:T(8,128)(2,1)S(1)} all-to-all(bf16[4,2,5,2,128,128]{5,4,3,2,1,0:T(8,128)(2,1)S(1)} %product.1), channel_id=1, replica_groups=mesh['chan'=64,'panel'=4] {'panel'}, dimensions={0} | all-to-all | bytes 5242880 | tf_op jit(solution)/shard_map/all_to_all | solution.py:231
  159.9 1.5 sum.1
  161.4 30.9 %all_to_all.26.in_ref = bf16[64,40,128]{2,1,0:T(8,128)(2,1)S(1)} all-to-all(bf16[64,40,128]{2,1,0:T(8,128)(2,1)S(1)} %sum.1), channel_id=1, replica_groups=mesh['chan'=64,'panel'=4] {'chan'}, dimensions={0} | all-to-all | bytes 1310720 | tf_op jit(solution)/shard_map/all_to_all | solution.py:231
  192.3 1.4 recouple_back.1
  193.7 5.9 %all-to-all-start.4 = ((bf16[64,40,128]{2,1,0:T(8,128)(2,1)}), bf16[64,40,128]{2,1,0:T(8,128)(2,1)S(1)}, u32[]{:S(2)}, u32[]{:S(2)}) async-start(bf16[64,40,128]{2,1,0:T(8,128)(2,1)} %recouple_back.1), calls=%async_computation.4 | async-start | bytes 1310720 | tf_op jit(solution)/shard_map/all_to_all | solution.py:231
  199.7 20.3 %all-to-all-done.4.in_ref = bf16[64,40,128]{2,1,0:T(8,128)(2,1)S(1)} async-done(((bf16[64,40,128]{2,1,0:T(8,128)(2,1)}), bf16[64,40,128]{2,1,0:T(8,128)(2,1)S(1)}, u32[]{:S(2)}, u32[]{:S(2)}) %all-to-all-start.4) | async-done | bytes 655392 | tf_op jit(solution)/shard_map/all_to_all | solution.py:231
  220.1 1.3 collective-permute-start.5
  222.2 1.8 collective-permute-start.4
  224.0 7.6 %pair_part.1.pp_ref = f32[2,256,1024]{2,1,0:T(8,128)S(1)} custom-call(bf16[2,256,1024]{2,1,0:T(8,128)(2,1)S(1)} %copy-done.1, bf16[2,256,1024]{2,1,0:T(8,128)(2,1)S(1)} %copy-done.3, bf16[2,1024,1024]{2,1,0:T(8,128)(2,1)} %all-gather.3.cloned.1.call-done.eta_all_ref, bf16[2,1024,1024]{2,1,0:T(8,128)(2,1)} %all-gather.5.cloned.1.call-done.gamma_all_ref, ...), custom_call_target="tpu_custom_call" | custom-call | flops 2147483648 | bytes 12582912 | tf_op jit(solution)/shard_map/pair_part/pallas_call | solution.py:197
  231.6 1.5 finish.1
  (36 shorter events, 6.1 us)
Async XLA Ops:
  6.5 217.5 %all-gather.3.cloned.1.call-start = ((), (), s32[]{:S(2)}) async-start(), calls=%async_computation.5 | async-start | bytes 5242880 | tf_op jit(solution)/shard_map/all_gather | solution.py:244
  7.3 1.2 copy-start
  8.5 1.2 copy-start.2
  11.1 13.3 %copy-start.4 = (bf16[128,128]{1,0:T(8,128)(2,1)S(1)}, bf16[128,128]{1,0:T(8,128)(2,1)}, u32[]{:S(2)}) copy-start(bf16[128,128]{1,0:T(8,128)(2,1)} %forward_ref.1) | copy-start | bytes 98308
  11.1 13.3 %copy-start.5 = (bf16[128,128]{1,0:T(8,128)(2,1)S(1)}, bf16[128,128]{1,0:T(8,128)(2,1)}, u32[]{:S(2)}) copy-start(bf16[128,128]{1,0:T(8,128)(2,1)} %back_ref.1) | copy-start | bytes 98308
  11.1 46.9 %all-to-all-start = ((bf16[64,5,16,128]{3,2,1,0:T(8,128)(2,1)}), bf16[64,5,16,128]{3,2,1,0:T(8,128)(2,1)S(1)}, u32[]{:S(2)}, u32[]{:S(2)}) async-start(bf16[64,5,16,128]{3,2,1,0:T(8,128)(2,1)} %pack.1), calls=%async_computation | async-start | bytes 2621440 | tf_op jit(solution)/shard_map/all_to_all | solution.py:231
  25.5 1.4 copy-start.7
  58.0 1.6 copy-start.8
  62.5 62.6 %copy-start.6 = (f32[2,1024]{1,0:T(2,128)S(1)}, f32[2,1024]{1,0:T(2,128)}, u32[]{:S(2)}) copy-start(f32[2,1024]{1,0:T(2,128)} %weight_ref.1) | copy-start | bytes 24580
  62.5 40.1 %all-to-all-start.1 = ((bf16[64,5,16,128]{3,2,1,0:T(8,128)(2,1)}), bf16[64,5,16,128]{3,2,1,0:T(8,128)(2,1)S(1)}, u32[]{:S(2)}, u32[]{:S(2)}) async-start(bf16[64,5,16,128]{3,2,1,0:T(8,128)(2,1)} %recouple.1), calls=%async_computation.1 | async-start | bytes 2621440 | tf_op jit(solution)/shard_map/all_to_all | solution.py:231
  69.0 155.0 %all-gather.5.cloned.1.call-start = ((), (), s32[]{:S(2)}) async-start(), calls=%async_computation.6 | async-start | bytes 5242880 | tf_op jit(solution)/shard_map/all_gather | solution.py:245
  103.9 21.2 %collective-permute-start = (bf16[8,128,128]{2,1,0:T(8,128)(2,1)S(1)}, bf16[8,128,128]{2,1,0:T(8,128)(2,1)S(1)}, u32[]{:S(2)}, u32[]{:S(2)}) collective-permute-start(bf16[8,128,128]{2,1,0:T(8,128)(2,1)S(1)} %get-tuple-element.15), channel_id=1, source_target_pairs={{0,1},{1,2},{2,3},{3,0},{4,5},{5,6},{6,7},{7,4},{8,9},{9,10},{10,1... | collective-permute-start | bytes 786440 | tf_op jit(solution)/shard_map/ppermute | solution.py:236
  105.1 19.9 %collective-permute-start.1 = (bf16[8,128,128]{2,1,0:T(8,128)(2,1)S(1)}, bf16[8,128,128]{2,1,0:T(8,128)(2,1)S(1)}, u32[]{:S(2)}, u32[]{:S(2)}) collective-permute-start(bf16[8,128,128]{2,1,0:T(8,128)(2,1)S(1)} %get-tuple-element.16), channel_id=1, source_target_pairs={{0,3},{1,0},{2,1},{3,2},{4,7},{5,4},{6,5},{7,6},{8,11},{9,8},{10,9... | collective-permute-start | bytes 786440 | tf_op jit(solution)/shard_map/ppermute | solution.py:236
  106.6 18.4 %collective-permute-start.2 = (bf16[4,128,128]{2,1,0:T(8,128)(2,1)S(1)}, bf16[4,128,128]{2,1,0:T(8,128)(2,1)S(1)}, u32[]{:S(2)}, u32[]{:S(2)}) collective-permute-start(bf16[4,128,128]{2,1,0:T(8,128)(2,1)S(1)} %get-tuple-element.17), channel_id=1, source_target_pairs={{0,2},{1,3},{2,0},{3,1},{4,6},{5,7},{6,4},{7,5},{8,10},{9,11},{10,... | collective-permute-start | bytes 393224 | tf_op jit(solution)/shard_map/ppermute | solution.py:236
  161.4 38.2 %copy-start.9 = (f32[2,1024]{1,0:T(2,128)S(1)}, f32[2,1024]{1,0:T(2,128)}, u32[]{:S(2)}) copy-start(f32[2,1024]{1,0:T(2,128)} %param.9) | copy-start | bytes 24580
  161.4 38.2 %copy-start.10 = (s32[2]{0:T(128)S(1)}, s32[2]{0:T(128)}, u32[]{:S(2)}) copy-start(s32[2]{0:T(128)} %param.11) | copy-start | bytes 28
  192.3 31.7 %copy-start.1 = (bf16[2,256,1024]{2,1,0:T(8,128)(2,1)S(1)}, bf16[2,256,1024]{2,1,0:T(8,128)(2,1)}, u32[]{:S(2)}) copy-start(bf16[2,256,1024]{2,1,0:T(8,128)(2,1)} %eta_ref.3) | copy-start | bytes 3145732
  192.3 31.7 %copy-start.3 = (bf16[2,256,1024]{2,1,0:T(8,128)(2,1)S(1)}, bf16[2,256,1024]{2,1,0:T(8,128)(2,1)}, u32[]{:S(2)}) copy-start(bf16[2,256,1024]{2,1,0:T(8,128)(2,1)} %gamma_ref.3) | copy-start | bytes 3145732
  193.7 26.2 %all-to-all-start.4 = ((bf16[64,40,128]{2,1,0:T(8,128)(2,1)}), bf16[64,40,128]{2,1,0:T(8,128)(2,1)S(1)}, u32[]{:S(2)}, u32[]{:S(2)}) async-start(bf16[64,40,128]{2,1,0:T(8,128)(2,1)} %recouple_back.1), calls=%async_computation.4 | async-start | bytes 1310720 | tf_op jit(solution)/shard_map/all_to_all | solution.py:231
  220.1 11.5 %collective-permute-start.5 = (bf16[2,128,128]{2,1,0:T(8,128)(2,1)S(1)}, bf16[2,128,128]{2,1,0:T(8,128)(2,1)S(1)}, u32[]{:S(2)}, u32[]{:S(2)}) collective-permute-start(bf16[2,128,128]{2,1,0:T(8,128)(2,1)S(1)} %get-tuple-element.20), channel_id=1, source_target_pairs={{0,2},{1,3},{2,0},{3,1},{4,6},{5,7},{6,4},{7,5},{8,10},{9,11},{10,... | collective-permute-start | bytes 196616 | tf_op jit(solution)/shard_map/ppermute | solution.py:236
  221.3 10.3 %collective-permute-start.3 = (bf16[4,128,128]{2,1,0:T(8,128)(2,1)S(1)}, bf16[4,128,128]{2,1,0:T(8,128)(2,1)S(1)}, u32[]{:S(2)}, u32[]{:S(2)}) collective-permute-start(bf16[4,128,128]{2,1,0:T(8,128)(2,1)S(1)} %get-tuple-element.18), channel_id=1, source_target_pairs={{0,1},{1,2},{2,3},{3,0},{4,5},{5,6},{6,7},{7,4},{8,9},{9,10},{10,1... | collective-permute-start | bytes 393224 | tf_op jit(solution)/shard_map/ppermute | solution.py:236
  222.2 9.4 %collective-permute-start.4 = (bf16[4,128,128]{2,1,0:T(8,128)(2,1)S(1)}, bf16[4,128,128]{2,1,0:T(8,128)(2,1)S(1)}, u32[]{:S(2)}, u32[]{:S(2)}) collective-permute-start(bf16[4,128,128]{2,1,0:T(8,128)(2,1)S(1)} %get-tuple-element.19), channel_id=1, source_target_pairs={{0,3},{1,0},{2,1},{3,2},{4,7},{5,4},{6,5},{7,6},{8,11},{9,8},{10,9... | collective-permute-start | bytes 393224 | tf_op jit(solution)/shard_map/ppermute | solution.py:236
Sparse Core Ops, SparseCore 0:
  9.2 54.5 all-gather.2
  71.6 60.1 all-gather.4
where the time goes:
time: 241 us; the launch traced here: 240 us
  waiting for transfers between devices  103 us (43%)
  blocking collectives  62.4 us (26%)
  starting transfers between devices  33.9 us (14%)
  Pallas kernels  22 us (9%)
  between operations  13.6 us (6%)
  local copies, waits for them, and re-layouts  5.44 us (2%)
    all_to_all x3, waiting for transfers between devices, exchange(): lax.all_to_all(operand, axis, split_axis=0, concat_axis=0, tiled=True)  84.3 us
    all_to_all x2, blocking collectives, exchange(): lax.all_to_all(operand, axis, split_axis=0, concat_axis=0, tiled=True)  62.4 us
    all_to_all x3, starting transfers between devices, exchange(): lax.all_to_all(operand, axis, split_axis=0, concat_axis=0, tiled=True)  25.6 us
    ppermute x6, waiting for transfers between devices, step(): return lax.ppermute(value, 'panel', [(i, (i + by) % 4) for i in range(4)])  16.9 us
    pallas_call x9, Pallas kernels, call(): pl.pallas_call(kernel, out_shape=shaped[0] if single else shaped, scratch...  14.4 us
    ppermute x6, starting transfers between devices, step(): return lax.ppermute(value, 'panel', [(i, (i + by) % 4) for i in range(4)])  8.21 us
    pallas_call x1, Pallas kernels, pair_part(): pl.pallas_call(pair_kernel, grid=(2, 1024 // step), in_specs=[pl.BlockSpe...  7.57 us
    unnamed x22, local copies, waits for them, and re-layouts  5.43 us
  transfers between devices with their start and end apart: 11, of which 4 were waited for; matrix products, arithmetic and copies ran while one was open for 0% of the time, Pallas kernels for 9%

commit v1 on v0

--- a/solution.py
+++ b/solution.py
@@ -157,65 +157,69 @@
     return jnp.concatenate([low, high], axis=1).reshape(128, LANES)
 
 
-def back_mirror_kernel(in_ref, plus_ref, minus_ref, far_ref):
+def back_mirror_kernel(in_ref, pp_ref, plus_ref, minus_ref, far_ref):
     for ch in range(2):
         for ref, held in ((plus_ref, PLUS), (minus_ref, MINUS), (far_ref, FAR)):
             for u, (l, t) in enumerate(held):
-                ref[ch * len(held) + u] = back_tile(in_ref, l, t, ch).astype(BF16)
+                ref[ch * len(held) + u] = (pp_ref[l, t, ch].T + back_tile(in_ref, l, t, ch)).astype(BF16)
 
 
 def finish_kernel(in_ref, plus_ref, minus_ref, far_ref, pp_ref, out_ref):
     panel = lax.axis_index("panel")
     for ch in range(2):
         for l in range(2):
+
+            def put(offset, value):
+                out_ref[ch, l * 128 : (l + 1) * 128, pl.ds(tile_at(panel, l, offset), LANES)] = value.astype(BF16)
+
+            for t, offset in enumerate(OFFSETS):
+                put(offset, pp_ref[l, t, ch] + back_tile(in_ref, l, t, ch).T)
+            put(2, minus_ref[ch * 2 + l])
+            if l == 0:
+                put(-1, plus_ref[ch * 2])
+                put(-3, far_ref[ch])
+            else:
+                put(-1, pp_ref[0, 1, ch].T + back_tile(in_ref, 0, 1, ch))
+                put(-3, plus_ref[ch * 2 + 1])
+
+
+def contract_first(a, b):
+    return lax.dot_general(a, b, (((0,), (0,)), ((), ())), preferred_element_type=F32)
+
+
+def pair_kernel(eta_ref, gamma_ref, weight_ref, own_ref, plus_ref, far_ref, minus_ref, scaled, plain):
+    panel = lax.axis_index("panel")
+    for ch in range(2):
+        for l in range(2):
+            row = weight_ref[ch : ch + 1, pl.ds(tile_at(panel, l, 0), LANES)]
+            weight = jnp.broadcast_to(row, (128, LANES)).T
             rows = slice(l * 128, (l + 1) * 128)
-
-            def put(offset, value):
-                columns = pl.ds(tile_at(panel, l, offset), LANES)
-                out_ref[ch, rows, columns] = (pp_ref[ch, rows, columns] + value).astype(BF16)
-
-            for t, offset in enumerate(OFFSETS):
-                put(offset, back_tile(in_ref, l, t, ch).T)
-            put(2, minus_ref[ch * 2 + l].astype(F32))
-            if l == 0:
-                put(-1, plus_ref[ch * 2].astype(F32))
-                put(-3, far_ref[ch].astype(F32))
-            else:
-                put(-1, back_tile(in_ref, 0, 1, ch))
-                put(-3, plus_ref[ch * 2 + 1].astype(F32))
-
-
-def pair_kernel(eta_ref, gamma_ref, eta_all_ref, gamma_all_ref, weight_ref, out_ref):
-    weight = weight_ref[0]
-    own = (eta_ref[0].astype(F32) * weight).astype(BF16)
-    other = (eta_all_ref[0].astype(F32) * weight).astype(BF16)
-    out_ref[0] = contract_last(own, gamma_all_ref[0]) + contract_last(gamma_ref[0], other)
-
-
-def pair_part(eta, gamma, eta_all, gamma_all, weight):
-    step = 256
-    return pl.pallas_call(
-        pair_kernel,
-        grid=(2, 1024 // step),
-        in_specs=[
-            pl.BlockSpec((1, 256, 1024), lambda c, q: (c, 0, 0)),
-            pl.BlockSpec((1, 256, 1024), lambda c, q: (c, 0, 0)),
-            pl.BlockSpec((1, step, 1024), lambda c, q: (c, q, 0)),
-            pl.BlockSpec((1, step, 1024), lambda c, q: (c, q, 0)),
-            pl.BlockSpec((1, 1, 1024), lambda c, q: (c, 0, 0)),
-        ],
-        out_specs=pl.BlockSpec((1, 256, step), lambda c, q: (c, 0, q)),
-        out_shape=jax.ShapeDtypeStruct((2, 256, 1024), F32),
-        compiler_params=params(),
-        cost_estimate=cost(2 * 2 * 2 * 256 * 1024 * 1024, 12 * 1024 * 1024),
-        name="pair_part",
-    )(eta, gamma, eta_all, gamma_all, weight.reshape(2, 1, 1024))
-
-
-def call(kernel, shapes, args, flops=0, scratch=(), name=None):
+            for j in range(8):
+                source = pl.ds(tile_at(panel, j, 0), LANES)
+                columns = slice(j * LANES, (j + 1) * LANES)
+                scaled[ch, rows, columns] = (eta_ref[ch, rows, source].astype(F32) * weight).astype(BF16)
+                plain[ch, rows, columns] = gamma_ref[ch, rows, source]
+        for owner, ref in enumerate((own_ref, plus_ref, far_ref, minus_ref)):
+            columns = slice(owner * 256, (owner + 1) * 256)
+            total = contract_first(scaled[ch, :, columns], plain[ch]) + contract_first(plain[ch, :, columns], scaled[ch])
+            for l in range(2):
+                for t, offset in enumerate(OFFSETS):
+                    column = (2 * owner + l + offset) % 8 * LANES
+                    ref[l, t, ch] = -total[l * 128 : (l + 1) * 128, column : column + LANES].astype(BF16)
+
+
+def pair_sum_kernel(own_ref, plus_ref, far_ref, minus_ref, out_ref):
+    for l in range(2):
+        for t in range(5):
+            for ch in range(2):
+                parts = [ref[l, t, ch].astype(F32) for ref in (own_ref, plus_ref, far_ref, minus_ref)]
+                out_ref[l, t, ch] = (parts[0] + parts[1]) + (parts[2] + parts[3])
+
+
+def call(kernel, shapes, args, flops=0, scratch=(), name=None, dtype=BF16):
     single = not isinstance(shapes, list)
     outs = [shapes] if single else shapes
-    shaped = [jax.ShapeDtypeStruct(s, BF16) for s in outs]
+    shaped = [jax.ShapeDtypeStruct(s, dtype) for s in outs]
     size = sum(a.size * a.dtype.itemsize for a in args) + sum(2 * s.size for s in shaped)
     return pl.pallas_call(
         kernel,
@@ -241,14 +245,23 @@
 def shards(eta, gamma, pp_weight, cc_weight, live_pairs, forward_table, back_table):
     positions = lax.broadcasted_iota(jnp.int32, pp_weight.shape, 1)
     weight_pp = jnp.where(positions < live_pairs[:, None], pp_weight, F32(0.0))
-    eta_all = lax.all_gather(eta, "panel", axis=1, tiled=True)
-    gamma_all = lax.all_gather(gamma, "panel", axis=1, tiled=True)
-
     packed = call(pack_kernel, (64, 5, 16, LANES), (eta, gamma), name="pack")
     forward_wide, back_wide = call(spread_kernel, [(1024, 1024), (512, 512)], (forward_table, back_table), flops=600_000_000, name="spread")
     packed = exchange(packed, "chan")
+    pp = call(
+        pair_kernel,
+        [(2, 5, 2, 128, LANES)] * 4,
+        (eta, gamma, weight_pp),
+        flops=2_200_000_000,
+        scratch=[pltpu.VMEM((2, 256, 1024), BF16)] * 2,
+        name="pair",
+    )
+    packed, *pp = lax.optimization_barrier((packed, *pp))
     mixed = call(recouple_kernel, (64, 5, 16, LANES), (forward_wide, packed), flops=1_400_000_000, name="recouple")
     mixed = exchange(mixed, "chan")
+    pp_received = mirror(pp[1], pp[3], pp[2])
+    pp_part = call(pair_sum_kernel, (2, 5, 2, 128, LANES), (pp[0], *pp_received), name="pair_sum", dtype=F32)
+    mixed, pp_part = lax.optimization_barrier((mixed, pp_part))
     sends = call(mirror_kernel, [(8, 128, LANES), (8, 128, LANES), (4, 128, LANES)], (mixed,), name="mirror")
     received = mirror(*sends)
     partial = call(
@@ -264,9 +277,8 @@
     part = exchange(part, "chan")
     part = call(recouple_back_kernel, (64, 40, LANES), (back_wide, part), flops=400_000_000, name="recouple_back")
     part = exchange(part, "chan")
-    back_sends = call(back_mirror_kernel, [(4, 128, LANES), (4, 128, LANES), (2, 128, LANES)], (part,), name="back_mirror")
+    back_sends = call(back_mirror_kernel, [(4, 128, LANES), (4, 128, LANES), (2, 128, LANES)], (part, pp_part), name="back_mirror")
     back_received = mirror(*back_sends)
-    pp_part = pair_part(eta, gamma, eta_all, gamma_all, weight_pp)
     return call(finish_kernel, (2, 256, 1024), (part, *back_received, pp_part), name="finish")
 
 

time: 241 us -> 213 us (0.88)
  waiting for transfers between devices: 103 us -> 65.3 us
  blocking collectives: 62.4 us -> 89.9 us
  between operations: 13.6 us -> 0.18 us
  Pallas kernels: 22 us -> 16.9 us
  local copies, waits for them, and re-layouts: 5.44 us -> 8.76 us
  starting transfers between devices: 33.9 us -> 31.1 us
    all_to_all x3 -> x2, waiting for transfers between devices: 84.3 us -> 25.7 us  [exchange(): lax.all_to_all(operand, axis, split_axis=0, concat_axis=0, tiled=True)]
    all_to_all x2 -> x3, blocking collectives: 62.4 us -> 89.9 us  [exchange(): lax.all_to_all(operand, axis, split_axis=0, concat_axis=0, tiled=True)]
    ppermute x6 -> x9, waiting for transfers between devices: 16.9 us -> 39.6 us  [step(): return lax.ppermute(value, 'panel', [(i, (i + by) % 4) for i in range(4)])]
    pallas_call x1 -> x0, Pallas kernels: 7.57 us -> none  [pair_part(): pl.pallas_call(pair_kernel, grid=(2, 1024 // step), in_specs=[pl.BlockSpe...]
    all_to_all x3 -> x2, starting transfers between devices: 25.6 us -> 19.7 us  [exchange(): lax.all_to_all(operand, axis, split_axis=0, concat_axis=0, tiled=True)]
    unnamed x22 -> x36, local copies, waits for them, and re-layouts: 5.43 us -> 8.76 us
    ppermute x6 -> x9, starting transfers between devices: 8.21 us -> 11.3 us  [step(): return lax.ppermute(value, 'panel', [(i, (i + by) % 4) for i in range(4)])]
    pallas_call x9 -> x11, Pallas kernels: 14.4 us -> 16.9 us  [call(): pl.pallas_call(kernel, out_shape=shaped[0] if single else shaped, scratch...]
  transfers between devices with their start and end apart: 11 -> 11, of which waited for: 4 -> 6; matrix products, arithmetic and copies ran while one was open for 0% -> 0% of each run, Pallas kernels for 9% -> 2%
where the time goes in v1:
time: 213 us; the launch traced here: 212 us
  blocking collectives  89.9 us (42%)
  waiting for transfers between devices  65.3 us (31%)
  starting transfers between devices  31.1 us (15%)
  Pallas kernels  16.9 us (8%)
  local copies, waits for them, and re-layouts  8.76 us (4%)
    all_to_all x3, blocking collectives, exchange(): lax.all_to_all(operand, axis, split_axis=0, concat_axis=0, tiled=True)  89.9 us
    ppermute x9, waiting for transfers between devices, step(): return lax.ppermute(value, 'panel', [(i, (i + by) % 4) for i in range(4)])  39.6 us
    all_to_all x2, waiting for transfers between devices, exchange(): lax.all_to_all(operand, axis, split_axis=0, concat_axis=0, tiled=True)  25.7 us
    all_to_all x2, starting transfers between devices, exchange(): lax.all_to_all(operand, axis, split_axis=0, concat_axis=0, tiled=True)  19.7 us
    pallas_call x11, Pallas kernels, call(): pl.pallas_call(kernel, out_shape=shaped[0] if single else shaped, scratch...  16.9 us
    ppermute x9, starting transfers between devices, step(): return lax.ppermute(value, 'panel', [(i, (i + by) % 4) for i in range(4)])  11.3 us
    unnamed x36, local copies, waits for them, and re-layouts  8.76 us
  transfers between devices with their start and end apart: 11, of which 6 were waited for; matrix products, arithmetic and copies ran while one was open for 0% of the time, Pallas kernels for 2%

profile of v1, /device:TPU:1, one launch (start us, length us, event | category | flops | bytes accessed | tf_op | source)
XLA Modules:
  0.0 212.2 jit_solution(11058639894751462015)
XLA Ops:
  2.5 1.4 pack.1
  3.9 13.3 %all-to-all-start = ((bf16[64,5,16,128]{3,2,1,0:T(8,128)(2,1)}), bf16[64,5,16,128]{3,2,1,0:T(8,128)(2,1)S(1)}, u32[]{:S(2)}, u32[]{:S(2)}) async-start(bf16[64,5,16,128]{3,2,1,0:T(8,128)(2,1)} %pack.1), calls=%async_computation | async-start | bytes 2621440 | tf_op jit(solution)/shard_map/all_to_all | solution.py:235
  19.1 1.3 copy-done.14
  20.5 2.9 %pair.1 = (bf16[2,5,2,128,128]{4,3,2,1,0:T(8,128)(2,1)S(1)}, bf16[2,5,2,128,128]{4,3,2,1,0:T(8,128)(2,1)S(1)}, bf16[2,5,2,128,128]{4,3,2,1,0:T(8,128)(2,1)S(1)}, bf16[2,5,2,128,128]{4,3,2,1,0:T(8,128)(2,1)S(1)}) custom-call(bf16[2,256,1024]{2,1,0:T(8,128)(2,1)S(1)} %copy-done.1, bf16[2,256,1024]{2,1,0:T(8,128)(2,1)S(1)} %copy-done.3, ...), custom_call_target="tpu_custom_call" | custom-call | flops 2200000000 | bytes 4726784 | tf_op jit(solution)/shard_map/pair/pallas_call | solution.py:224
  26.0 24.8 %all-to-all-done.in_ref = bf16[64,5,16,128]{3,2,1,0:T(8,128)(2,1)S(1)} async-done(((bf16[64,5,16,128]{3,2,1,0:T(8,128)(2,1)}), bf16[64,5,16,128]{3,2,1,0:T(8,128)(2,1)S(1)}, u32[]{:S(2)}, u32[]{:S(2)}) %all-to-all-start) | async-done | bytes 1310752 | tf_op jit(solution)/shard_map/all_to_all | solution.py:235
  50.8 1.6 copy-done.15
  52.4 2.9 %recouple.1 = bf16[64,5,16,128]{3,2,1,0:T(8,128)(2,1)} custom-call(bf16[1024,1024]{1,0:T(8,128)(2,1)S(1)} %copy-done.15, bf16[64,5,16,128]{3,2,1,0:T(8,128)(2,1)S(1)} %all-to-all-done.in_ref), custom_call_target="tpu_custom_call" | custom-call | flops 1400000000 | bytes 4718592 | tf_op jit(solution)/shard_map/recouple/pallas_call | solution.py:224
  55.2 6.5 %all-to-all-start.1 = ((bf16[64,5,16,128]{3,2,1,0:T(8,128)(2,1)}), bf16[64,5,16,128]{3,2,1,0:T(8,128)(2,1)S(1)}, u32[]{:S(2)}, u32[]{:S(2)}) async-start(bf16[64,5,16,128]{3,2,1,0:T(8,128)(2,1)} %recouple.1), calls=%async_computation.1 | async-start | bytes 2621440 | tf_op jit(solution)/shard_map/all_to_all | solution.py:235
  61.7 1.3 collective-permute-start
  63.0 1.5 collective-permute-start.1
  64.5 1.5 collective-permute-start.2
  66.0 13.1 %collective-permute-done.plus_ref = bf16[2,5,2,128,128]{4,3,2,1,0:T(8,128)(2,1)S(1)} collective-permute-done((bf16[2,5,2,128,128]{4,3,2,1,0:T(8,128)(2,1)}, bf16[2,5,2,128,128]{4,3,2,1,0:T(8,128)(2,1)S(1)}, u32[]{:S(2)}, u32[]{:S(2)}) %collective-permute-start) | collective-permute-done | bytes 655392 | tf_op jit(solution)/shard_map/ppermute | solution.py:240
  79.0 15.0 %collective-permute-done.2.minus_ref = bf16[2,5,2,128,128]{4,3,2,1,0:T(8,128)(2,1)S(1)} collective-permute-done((bf16[2,5,2,128,128]{4,3,2,1,0:T(8,128)(2,1)S(1)}, bf16[2,5,2,128,128]{4,3,2,1,0:T(8,128)(2,1)S(1)}, u32[]{:S(2)}, u32[]{:S(2)}) %collective-permute-start.2) | collective-permute-done | bytes 655392 | tf_op jit(solution)/shard_map/ppermute | solution.py:240
  97.9 1.5 collective-permute-start.4
  99.4 1.5 collective-permute-start.5
  100.9 6.9 %collective-permute-done.5.far_ref = bf16[4,128,128]{2,1,0:T(8,128)(2,1)S(1)} collective-permute-done((bf16[4,128,128]{2,1,0:T(8,128)(2,1)S(1)}, bf16[4,128,128]{2,1,0:T(8,128)(2,1)S(1)}, u32[]{:S(2)}, u32[]{:S(2)}) %collective-permute-start.5) | collective-permute-done | bytes 131104 | tf_op jit(solution)/shard_map/ppermute | solution.py:240
  107.8 3.3 %product.1 = bf16[4,2,5,2,128,128]{5,4,3,2,1,0:T(8,128)(2,1)S(1)} custom-call(bf16[64,5,16,128]{3,2,1,0:T(8,128)(2,1)S(1)} %all-to-all-done.1.in_ref, bf16[8,128,128]{2,1,0:T(8,128)(2,1)S(1)} %collective-permute-done.3.plus_ref, bf16[8,128,128]{2,1,0:T(8,128)(2,1)S(1)} %collective-permute-done.4.minus_ref, ...), custom_call_target="tpu_custom_call" | custom-call | flops 2200000000 | bytes 4595712 | tf_op jit(solution)/shard_map/product/pallas_call | solution.py:224
  111.2 31.3 %all_to_all.25.in_ref = bf16[4,2,5,2,128,128]{5,4,3,2,1,0:T(8,128)(2,1)S(1)} all-to-all(bf16[4,2,5,2,128,128]{5,4,3,2,1,0:T(8,128)(2,1)S(1)} %product.1), channel_id=1, replica_groups=mesh['chan'=64,'panel'=4] {'panel'}, dimensions={0} | all-to-all | bytes 5242880 | tf_op jit(solution)/shard_map/all_to_all | solution.py:235
  142.4 1.5 sum.1
  143.9 32.6 %all_to_all.26.in_ref = bf16[64,40,128]{2,1,0:T(8,128)(2,1)S(1)} all-to-all(bf16[64,40,128]{2,1,0:T(8,128)(2,1)S(1)} %sum.1), channel_id=1, replica_groups=mesh['chan'=64,'panel'=4] {'chan'}, dimensions={0} | all-to-all | bytes 1310720 | tf_op jit(solution)/shard_map/all_to_all | solution.py:235
  177.1 26.0 %all_to_all.27.in_ref = bf16[64,40,128]{2,1,0:T(8,128)(2,1)S(1)} all-to-all(bf16[64,40,128]{2,1,0:T(8,128)(2,1)S(1)} %recouple_back.1), channel_id=1, replica_groups=mesh['chan'=64,'panel'=4] {'chan'}, dimensions={0} | all-to-all | bytes 1310720 | tf_op jit(solution)/shard_map/all_to_all | solution.py:235
  203.7 2.4 %collective-permute-start.7 = (bf16[4,128,128]{2,1,0:T(8,128)(2,1)S(1)}, bf16[4,128,128]{2,1,0:T(8,128)(2,1)S(1)}, u32[]{:S(2)}, u32[]{:S(2)}) collective-permute-start(bf16[4,128,128]{2,1,0:T(8,128)(2,1)S(1)} %get-tuple-element.41), channel_id=1, source_target_pairs={{0,3},{1,0},{2,1},{3,2},{4,7},{5,4},{6,5},{7,6},{8,11},{9,8},{10,9... | collective-permute-start | bytes 393224 | tf_op jit(solution)/shard_map/ppermute | solution.py:240
  206.1 4.6 %collective-permute-done.8.far_ref = bf16[2,128,128]{2,1,0:T(8,128)(2,1)S(1)} collective-permute-done((bf16[2,128,128]{2,1,0:T(8,128)(2,1)S(1)}, bf16[2,128,128]{2,1,0:T(8,128)(2,1)S(1)}, u32[]{:S(2)}, u32[]{:S(2)}) %collective-permute-start.8) | collective-permute-done | bytes 65568 | tf_op jit(solution)/shard_map/ppermute | solution.py:240
  210.7 1.4 finish.1
  (49 shorter events, 11.9 us)
Async XLA Ops:
  0.0 1.2 copy-start
  3.9 13.3 %copy-start.11 = (bf16[128,128]{1,0:T(8,128)(2,1)S(1)}, bf16[128,128]{1,0:T(8,128)(2,1)}, u32[]{:S(2)}) copy-start(bf16[128,128]{1,0:T(8,128)(2,1)} %forward_ref.1) | copy-start | bytes 98308
  3.9 13.3 %copy-start.12 = (bf16[128,128]{1,0:T(8,128)(2,1)S(1)}, bf16[128,128]{1,0:T(8,128)(2,1)}, u32[]{:S(2)}) copy-start(bf16[128,128]{1,0:T(8,128)(2,1)} %back_ref.1) | copy-start | bytes 98308
  3.9 46.9 %all-to-all-start = ((bf16[64,5,16,128]{3,2,1,0:T(8,128)(2,1)}), bf16[64,5,16,128]{3,2,1,0:T(8,128)(2,1)S(1)}, u32[]{:S(2)}, u32[]{:S(2)}) async-start(bf16[64,5,16,128]{3,2,1,0:T(8,128)(2,1)} %pack.1), calls=%async_computation | async-start | bytes 2621440 | tf_op jit(solution)/shard_map/all_to_all | solution.py:235
  17.2 3.3 %copy-start.16 = (f32[2,1024]{1,0:T(2,128)S(1)}, f32[2,1024]{1,0:T(2,128)}, u32[]{:S(2)}) copy-start(f32[2,1024]{1,0:T(2,128)} %param.9) | copy-start | bytes 24580
  17.2 3.3 %copy-start.17 = (s32[2]{0:T(128)S(1)}, s32[2]{0:T(128)}, u32[]{:S(2)}) copy-start(s32[2]{0:T(128)} %param.11) | copy-start | bytes 28
  17.2 3.3 %copy-start.1 = (bf16[2,256,1024]{2,1,0:T(8,128)(2,1)S(1)}, bf16[2,256,1024]{2,1,0:T(8,128)(2,1)}, u32[]{:S(2)}) copy-start(bf16[2,256,1024]{2,1,0:T(8,128)(2,1)} %eta_ref.3) | copy-start | bytes 3145732
  17.2 3.3 %copy-start.3 = (bf16[2,256,1024]{2,1,0:T(8,128)(2,1)S(1)}, bf16[2,256,1024]{2,1,0:T(8,128)(2,1)}, u32[]{:S(2)}) copy-start(bf16[2,256,1024]{2,1,0:T(8,128)(2,1)} %gamma_ref.3) | copy-start | bytes 3145732
  19.1 1.4 copy-start.14
  50.8 1.6 copy-start.15
  55.2 7.8 %copy-start.9 = (bf16[2,5,2,128,128]{4,3,2,1,0:T(8,128)(2,1)S(1)}, bf16[2,5,2,128,128]{4,3,2,1,0:T(8,128)(2,1)}, u32[]{:S(2)}) copy-start(bf16[2,5,2,128,128]{4,3,2,1,0:T(8,128)(2,1)} %copy-done.8) | copy-start | bytes 1966084
  55.2 9.2 %copy-start.7 = (bf16[2,5,2,128,128]{4,3,2,1,0:T(8,128)(2,1)S(1)}, bf16[2,5,2,128,128]{4,3,2,1,0:T(8,128)(2,1)}, u32[]{:S(2)}) copy-start(bf16[2,5,2,128,128]{4,3,2,1,0:T(8,128)(2,1)} %copy-done.6) | copy-start | bytes 1966084
  55.2 40.1 %all-to-all-start.1 = ((bf16[64,5,16,128]{3,2,1,0:T(8,128)(2,1)}), bf16[64,5,16,128]{3,2,1,0:T(8,128)(2,1)S(1)}, u32[]{:S(2)}, u32[]{:S(2)}) async-start(bf16[64,5,16,128]{3,2,1,0:T(8,128)(2,1)} %recouple.1), calls=%async_computation.1 | async-start | bytes 2621440 | tf_op jit(solution)/shard_map/all_to_all | solution.py:235
  61.7 17.4 %collective-permute-start = (bf16[2,5,2,128,128]{4,3,2,1,0:T(8,128)(2,1)}, bf16[2,5,2,128,128]{4,3,2,1,0:T(8,128)(2,1)S(1)}, u32[]{:S(2)}, u32[]{:S(2)}) collective-permute-start(bf16[2,5,2,128,128]{4,3,2,1,0:T(8,128)(2,1)} %copy-done.10), channel_id=1, source_target_pairs={{0,1},{1,2},{2,3},{3,0},{4,5},{5,6},{6,7},{7,4},{8,9},{9,10},{10,1... | collective-permute-start | bytes 1966088 | tf_op jit(solution)/shard_map/ppermute | solution.py:240
  63.0 16.1 %collective-permute-start.1 = (bf16[2,5,2,128,128]{4,3,2,1,0:T(8,128)(2,1)S(1)}, bf16[2,5,2,128,128]{4,3,2,1,0:T(8,128)(2,1)S(1)}, u32[]{:S(2)}, u32[]{:S(2)}) collective-permute-start(bf16[2,5,2,128,128]{4,3,2,1,0:T(8,128)(2,1)S(1)} %copy-done.9), channel_id=1, source_target_pairs={{0,3},{1,0},{2,1},{3,2},{4,7},{5,4},{6,5},{7,6},{8,11},{9,8},{10,9... | collective-permute-start | bytes 1966088 | tf_op jit(solution)/shard_map/ppermute | solution.py:240
  64.5 29.6 %collective-permute-start.2 = (bf16[2,5,2,128,128]{4,3,2,1,0:T(8,128)(2,1)S(1)}, bf16[2,5,2,128,128]{4,3,2,1,0:T(8,128)(2,1)S(1)}, u32[]{:S(2)}, u32[]{:S(2)}) collective-permute-start(bf16[2,5,2,128,128]{4,3,2,1,0:T(8,128)(2,1)S(1)} %copy-done.7), channel_id=1, source_target_pairs={{0,2},{1,3},{2,0},{3,1},{4,6},{5,7},{6,4},{7,5},{8,10},{9,11},{10,... | collective-permute-start | bytes 1966088 | tf_op jit(solution)/shard_map/ppermute | solution.py:240
  94.4 13.4 %copy-start.13 = (f32[2,1024]{1,0:T(2,128)S(1)}, f32[2,1024]{1,0:T(2,128)}, u32[]{:S(2)}) copy-start(f32[2,1024]{1,0:T(2,128)} %weight_ref.1) | copy-start | bytes 24580
  96.6 11.2 %collective-permute-start.3 = (bf16[8,128,128]{2,1,0:T(8,128)(2,1)S(1)}, bf16[8,128,128]{2,1,0:T(8,128)(2,1)S(1)}, u32[]{:S(2)}, u32[]{:S(2)}) collective-permute-start(bf16[8,128,128]{2,1,0:T(8,128)(2,1)S(1)} %get-tuple-element.36), channel_id=1, source_target_pairs={{0,1},{1,2},{2,3},{3,0},{4,5},{5,6},{6,7},{7,4},{8,9},{9,10},{10,1... | collective-permute-start | bytes 786440 | tf_op jit(solution)/shard_map/ppermute | solution.py:240
  97.9 9.9 %collective-permute-start.4 = (bf16[8,128,128]{2,1,0:T(8,128)(2,1)S(1)}, bf16[8,128,128]{2,1,0:T(8,128)(2,1)S(1)}, u32[]{:S(2)}, u32[]{:S(2)}) collective-permute-start(bf16[8,128,128]{2,1,0:T(8,128)(2,1)S(1)} %get-tuple-element.37), channel_id=1, source_target_pairs={{0,3},{1,0},{2,1},{3,2},{4,7},{5,4},{6,5},{7,6},{8,11},{9,8},{10,9... | collective-permute-start | bytes 786440 | tf_op jit(solution)/shard_map/ppermute | solution.py:240
  99.4 8.4 %collective-permute-start.5 = (bf16[4,128,128]{2,1,0:T(8,128)(2,1)S(1)}, bf16[4,128,128]{2,1,0:T(8,128)(2,1)S(1)}, u32[]{:S(2)}, u32[]{:S(2)}) collective-permute-start(bf16[4,128,128]{2,1,0:T(8,128)(2,1)S(1)} %get-tuple-element.38), channel_id=1, source_target_pairs={{0,2},{1,3},{2,0},{3,1},{4,6},{5,7},{6,4},{7,5},{8,10},{9,11},{10,... | collective-permute-start | bytes 393224 | tf_op jit(solution)/shard_map/ppermute | solution.py:240
  143.9 32.6 %copy-start.5 = (bf16[512,512]{1,0:T(8,128)(2,1)S(1)}, bf16[512,512]{1,0:T(8,128)(2,1)}, u32[]{:S(2)}) copy-start(bf16[512,512]{1,0:T(8,128)(2,1)} %copy-done.4) | copy-start | bytes 1572868
  203.3 7.4 %collective-permute-start.6 = (bf16[4,128,128]{2,1,0:T(8,128)(2,1)S(1)}, bf16[4,128,128]{2,1,0:T(8,128)(2,1)S(1)}, u32[]{:S(2)}, u32[]{:S(2)}) collective-permute-start(bf16[4,128,128]{2,1,0:T(8,128)(2,1)S(1)} %get-tuple-element.40), channel_id=1, source_target_pairs={{0,1},{1,2},{2,3},{3,0},{4,5},{5,6},{6,7},{7,4},{8,9},{9,10},{10,1... | collective-permute-start | bytes 393224 | tf_op jit(solution)/shard_map/ppermute | solution.py:240
  203.7 7.0 %collective-permute-start.7 = (bf16[4,128,128]{2,1,0:T(8,128)(2,1)S(1)}, bf16[4,128,128]{2,1,0:T(8,128)(2,1)S(1)}, u32[]{:S(2)}, u32[]{:S(2)}) collective-permute-start(bf16[4,128,128]{2,1,0:T(8,128)(2,1)S(1)} %get-tuple-element.41), channel_id=1, source_target_pairs={{0,3},{1,0},{2,1},{3,2},{4,7},{5,4},{6,5},{7,6},{8,11},{9,8},{10,9... | collective-permute-start | bytes 393224 | tf_op jit(solution)/shard_map/ppermute | solution.py:240
  206.1 4.6 %collective-permute-start.8 = (bf16[2,128,128]{2,1,0:T(8,128)(2,1)S(1)}, bf16[2,128,128]{2,1,0:T(8,128)(2,1)S(1)}, u32[]{:S(2)}, u32[]{:S(2)}) collective-permute-start(bf16[2,128,128]{2,1,0:T(8,128)(2,1)S(1)} %get-tuple-element.42), channel_id=1, source_target_pairs={{0,2},{1,3},{2,0},{3,1},{4,6},{5,7},{6,4},{7,5},{8,10},{9,11},{10,... | collective-permute-start | bytes 196616 | tf_op jit(solution)/shard_map/ppermute | solution.py:240
  (5 other events, 4.6 us)

commit v2 on v1

--- a/solution.py
+++ b/solution.py
@@ -88,55 +88,111 @@
 def mirror_kernel(in_ref, plus_ref, minus_ref, far_ref):
     for arr in range(2):
         for ch in range(2):
-            for ref, held in ((plus_ref, PLUS), (minus_ref, MINUS), (far_ref, FAR)):
-                for u, (l, t) in enumerate(held):
-                    ref[(arr * 2 + ch) * len(held) + u] = swap_blocks(tile_of(in_ref, arr, l, t, ch).T).astype(BF16)
-
-
-def product_kernel(in_ref, plus_ref, minus_ref, far_ref, weight_ref, out_ref, scaled, plain):
+            base = arr * 2 + ch
+            for u, (l, t) in enumerate(PLUS + ((0, 4), (1, 3))):
+                plus_ref[base * 4 + u] = swap_blocks(tile_of(in_ref, arr, l, t, ch).T).astype(BF16)
+            for u, (l, t) in enumerate(MINUS):
+                minus_ref[base * 4 + u] = swap_blocks(tile_of(in_ref, arr, l, t, ch).T).astype(BF16)
+            for u, (l, t) in enumerate(((1, 3), (1, 4))):
+                tile = swap_blocks(tile_of(in_ref, arr, l, t, ch))
+                minus_ref[base * 4 + 2 + u] = (-tile if arr == 0 else tile).astype(BF16)
+            for u, (l, t) in enumerate(FAR):
+                far_ref[base + u] = swap_blocks(tile_of(in_ref, arr, l, t, ch).T).astype(BF16)
+
+
+def product_kernel(
+    in_ref, plus_ref, minus_ref, far_ref, weight_ref, own_ref, plus_out, far_out, minus_out, by_lane, by_row, plain, edge_lane, edge_row, edge_plain
+):
     panel = lax.axis_index("panel")
     for ch in range(2):
+        lanes = [weight_ref[ch : ch + 1, pl.ds(tile_at(panel, j, 0), LANES)] for j in range(8)]
+        rows = [jnp.broadcast_to(lane, (128, LANES)).T for lane in lanes]
         for l in range(2):
-            weight = weight_ref[ch : ch + 1, pl.ds(tile_at(panel, l, 0), LANES)]
 
             def put(arr, offset, value):
-                rows = pl.ds(tile_at(panel, l, offset), LANES)
-                columns = slice(l * LANES, (l + 1) * LANES)
+                j = (l + offset) % 8
+                place = (slice(j * 128, (j + 1) * 128), slice(l * LANES, (l + 1) * LANES))
                 if arr == 0:
-                    scaled[ch, rows, columns] = (value * weight).astype(BF16)
+                    by_lane.at[ch][place] = (value * lanes[l]).astype(BF16)
+                    by_row.at[ch][place] = (value * rows[j]).astype(BF16)
                 else:
-                    plain[ch, rows, columns] = value.astype(BF16)
+                    plain.at[ch][place] = value.astype(BF16)
 
             for arr in range(2):
                 base = arr * 2 + ch
                 for t, offset in enumerate(OFFSETS):
                     tile = swap_blocks(tile_of(in_ref, arr, l, t, ch))
                     put(arr, offset, -tile if arr == 0 else tile)
-                put(arr, 2, minus_ref[base * 2 + l].astype(F32))
+                put(arr, 2, minus_ref[base * 4 + l].astype(F32))
                 if l == 0:
-                    put(arr, -1, plus_ref[base * 2].astype(F32))
+                    put(arr, -1, plus_ref[base * 4].astype(F32))
                     put(arr, -3, far_ref[base].astype(F32))
                 else:
                     put(arr, -1, swap_blocks(tile_of(in_ref, arr, 0, 1, ch).T))
-                    put(arr, -3, plus_ref[base * 2 + 1].astype(F32))
-        for owner in range(4):
-            rows = slice(owner * 256, (owner + 1) * 256)
-            total = contract_last(scaled[ch, rows], plain[ch]) + contract_last(plain[ch, rows], scaled[ch])
-            for l in range(2):
-                for t, offset in enumerate(OFFSETS):
-                    column = (2 * owner + l + offset) % 8 * LANES
-                    out_ref[owner, l, t, ch] = total[l * 128 : (l + 1) * 128, column : column + LANES].astype(BF16)
-
-
-def sum_kernel(in_ref, out_ref):
+                    put(arr, -3, plus_ref[base * 4 + 1].astype(F32))
+        for arr in range(2):
+            base = arr * 4 * 2 + ch * 4
+            for r in range(2):
+                for c in range(2):
+                    ref = plus_ref if c == 0 else minus_ref
+                    value = ref[base + 2 + r].astype(F32)
+                    place = (slice(r * 128, (r + 1) * 128), slice(c * LANES, (c + 1) * LANES))
+                    if arr == 0:
+                        edge_lane.at[ch][place] = (value * lanes[2 + c]).astype(BF16)
+                        edge_row.at[ch][place] = (value * rows[6 + r]).astype(BF16)
+                    else:
+                        edge_plain.at[ch][place] = value.astype(BF16)
+
+        def block(ref, j):
+            return ref[ch, j * 256 : (j + 1) * 256]
+
+        def inner(i, j):
+            return contract_last(block(by_lane, i), block(plain, j)) + contract_last(block(plain, i), block(by_lane, j))
+
+        def tile(value, i, j):
+            return value[i * 128 : (i + 1) * 128, j * 128 : (j + 1) * 128]
+
+        diagonal = contract_first(by_row[ch], plain[ch]) + contract_first(plain[ch], by_row[ch])
+        for (l, t), (i, j) in (((0, 0), (0, 0)), ((0, 1), (0, 1)), ((1, 0), (1, 1))):
+            own_ref[l, t, ch] = -tile(diagonal, i, j)
+        ahead = inner(0, 1) - contract_first(block(by_row, 3), edge_plain[ch]) - contract_first(block(plain, 3), edge_row[ch])
+        own_ref[0, 3, ch] = tile(ahead, 0, 1)
+        own_ref[1, 1, ch] = tile(ahead, 1, 0)
+        plus_out[ch, 0] = tile(ahead, 0, 0).astype(BF16)
+        plus_out[ch, 1] = tile(ahead, 1, 1).astype(BF16)
+        behind = inner(3, 0) + jnp.dot(edge_lane[ch], block(plain, 1), preferred_element_type=F32) - jnp.dot(edge_plain[ch], block(by_row, 1), preferred_element_type=F32)
+        own_ref[0, 2, ch] = tile(behind, 0, 0)
+        own_ref[1, 2, ch] = tile(behind, 1, 1)
+        minus_out[ch, 0] = tile(behind, 0, 1).astype(BF16)
+        minus_out[ch, 1] = tile(behind, 1, 0).astype(BF16)
+        across = inner(0, 2)
+        for (l, t), (i, j) in ACROSS:
+            own_ref[l, t, ch] = tile(across, i, j)
+        for ref, start, value in ((far_out, 0, inner(2, 0)), (minus_out, 2, inner(3, 1)), (plus_out, 2, inner(1, 3))):
+            for u, (held, (i, j)) in enumerate(ACROSS):
+                ref[ch, start + u] = tile(value, i, j).astype(BF16)
+
+
+ACROSS = (((0, 4), (0, 0)), ((1, 3), (1, 0)), ((1, 4), (1, 1)))
+
+
+def sum_kernel(own_ref, plus_ref, far_ref, minus_ref, out_ref):
+    def total(l, t, ch):
+        value = own_ref[l, t, ch]
+        if t == 2:
+            return (value + plus_ref[ch, l].astype(F32)).T
+        if (l, t) in ((0, 3), (1, 1)):
+            return value + minus_ref[ch, l].astype(F32)
+        for u, (held, _) in enumerate(ACROSS):
+            if held == (l, t):
+                near = plus_ref[ch, 2 + u].astype(F32) + minus_ref[ch, 2 + u].astype(F32)
+                return value + far_ref[ch, u].astype(F32) + near
+        return value
+
     for l in range(2):
         low, high = [], []
         for t in range(5):
-            both = []
-            for ch in range(2):
-                parts = [in_ref[p, l, t, ch].astype(F32) for p in range(4)]
-                total = (parts[0] + parts[1]) + (parts[2] + parts[3])
-                both.append(swap_blocks(total).reshape(16, 8, LANES))
+            both = [swap_blocks(total(l, t, ch)).reshape(16, 8, LANES) for ch in range(2)]
             low += [both[0][:, :4], both[1][:, :4]]
             high += [both[0][:, 4:], both[1][:, 4:]]
         out_ref[l * 32 : l * 32 + 16] = jnp.concatenate(low, axis=1).astype(BF16)
@@ -219,8 +275,9 @@
 def call(kernel, shapes, args, flops=0, scratch=(), name=None, dtype=BF16):
     single = not isinstance(shapes, list)
     outs = [shapes] if single else shapes
-    shaped = [jax.ShapeDtypeStruct(s, dtype) for s in outs]
-    size = sum(a.size * a.dtype.itemsize for a in args) + sum(2 * s.size for s in shaped)
+    types = dtype if isinstance(dtype, list) else [dtype] * len(outs)
+    shaped = [jax.ShapeDtypeStruct(s, d) for s, d in zip(outs, types)]
+    size = sum(a.size * a.dtype.itemsize for a in [*args, *shaped])
     return pl.pallas_call(
         kernel,
         out_shape=shaped[0] if single else shaped,
@@ -262,18 +319,19 @@
     pp_received = mirror(pp[1], pp[3], pp[2])
     pp_part = call(pair_sum_kernel, (2, 5, 2, 128, LANES), (pp[0], *pp_received), name="pair_sum", dtype=F32)
     mixed, pp_part = lax.optimization_barrier((mixed, pp_part))
-    sends = call(mirror_kernel, [(8, 128, LANES), (8, 128, LANES), (4, 128, LANES)], (mixed,), name="mirror")
+    sends = call(mirror_kernel, [(16, 128, LANES), (16, 128, LANES), (4, 128, LANES)], (mixed,), name="mirror")
     received = mirror(*sends)
-    partial = call(
+    own, *partial = call(
         product_kernel,
-        (4, 2, 5, 2, 128, LANES),
+        [(2, 5, 2, 128, LANES), (2, 5, 128, LANES), (2, 3, 128, LANES), (2, 5, 128, LANES)],
         (mixed, *received, cc_weight),
-        flops=2_200_000_000,
-        scratch=[pltpu.VMEM((2, 1024, 256), BF16)] * 2,
+        flops=1_400_000_000,
+        scratch=[pltpu.VMEM((2, 1024, 256), BF16)] * 3 + [pltpu.VMEM((2, 256, 256), BF16)] * 3,
         name="product",
+        dtype=[F32, BF16, BF16, BF16],
     )
-    partial = exchange(partial, "panel")
-    part = call(sum_kernel, (64, 40, LANES), (partial,), name="sum")
+    plus, minus, far = mirror(partial[0], partial[2], partial[1])
+    part = call(sum_kernel, (64, 40, LANES), (own, plus, far, minus), name="sum")
     part = exchange(part, "chan")
     part = call(recouple_back_kernel, (64, 40, LANES), (back_wide, part), flops=400_000_000, name="recouple_back")
     part = exchange(part, "chan")

time: 213 us -> 201 us (0.944)
  blocking collectives: 89.9 us -> 59.1 us
  waiting for transfers between devices: 65.3 us -> 79 us
  starting transfers between devices: 31.1 us -> 34.3 us
    all_to_all x3 -> x2, blocking collectives: 89.9 us -> 59.1 us  [exchange(): lax.all_to_all(operand, axis, split_axis=0, concat_axis=0, tiled=True)]
    ppermute x9 -> x12, waiting for transfers between devices: 39.6 us -> 53.3 us  [step(): return lax.ppermute(value, 'panel', [(i, (i + by) % 4) for i in range(4)])]
    ppermute x9 -> x12, starting transfers between devices: 11.3 us -> 14.6 us  [step(): return lax.ppermute(value, 'panel', [(i, (i + by) % 4) for i in range(4)])]
    pallas_call x11, Pallas kernels: 16.9 us -> 19 us  [call(): pl.pallas_call(kernel, out_shape=shaped[0] if single else shaped, scratch...]
  transfers between devices with their start and end apart: 11 -> 14, of which waited for: 6 -> 7; matrix products, arithmetic and copies ran while one was open for 0% -> 0% of each run, Pallas kernels for 2% -> 2%
where the time goes in v2:
time: 201 us; the launch traced here: 200 us
  waiting for transfers between devices  79 us (39%)
  blocking collectives  59.1 us (29%)
  starting transfers between devices  34.3 us (17%)
  Pallas kernels  19 us (9%)
  local copies, waits for them, and re-layouts  8.77 us (4%)
    all_to_all x2, blocking collectives, exchange(): lax.all_to_all(operand, axis, split_axis=0, concat_axis=0, tiled=True)  59.1 us
    ppermute x12, waiting for transfers between devices, step(): return lax.ppermute(value, 'panel', [(i, (i + by) % 4) for i in range(4)])  53.3 us
    all_to_all x2, waiting for transfers between devices, exchange(): lax.all_to_all(operand, axis, split_axis=0, concat_axis=0, tiled=True)  25.7 us
    all_to_all x2, starting transfers between devices, exchange(): lax.all_to_all(operand, axis, split_axis=0, concat_axis=0, tiled=True)  19.7 us
    pallas_call x11, Pallas kernels, call(): pl.pallas_call(kernel, out_shape=shaped[0] if single else shaped, scratch...  19 us
    ppermute x12, starting transfers between devices, step(): return lax.ppermute(value, 'panel', [(i, (i + by) % 4) for i in range(4)])  14.6 us
    unnamed x36, local copies, waits for them, and re-layouts  8.77 us
  transfers between devices with their start and end apart: 14, of which 7 were waited for; matrix products, arithmetic and copies ran while one was open for 0% of the time, Pallas kernels for 2%

profile of v2, /device:TPU:1, one launch (start us, length us, event | category | flops | bytes accessed | tf_op | source)
XLA Modules:
  0.0 200.5 jit_solution(12552065530435863044)
XLA Ops:
  3.8 13.3 %all-to-all-start = ((bf16[64,5,16,128]{3,2,1,0:T(8,128)(2,1)}), bf16[64,5,16,128]{3,2,1,0:T(8,128)(2,1)S(1)}, u32[]{:S(2)}, u32[]{:S(2)}) async-start(bf16[64,5,16,128]{3,2,1,0:T(8,128)(2,1)} %pack.1), calls=%async_computation | async-start | bytes 2621440 | tf_op jit(solution)/shard_map/all_to_all | solution.py:292
  20.5 2.9 %pair.1 = (bf16[2,5,2,128,128]{4,3,2,1,0:T(8,128)(2,1)S(1)}, bf16[2,5,2,128,128]{4,3,2,1,0:T(8,128)(2,1)S(1)}, bf16[2,5,2,128,128]{4,3,2,1,0:T(8,128)(2,1)S(1)}, bf16[2,5,2,128,128]{4,3,2,1,0:T(8,128)(2,1)S(1)}) custom-call(bf16[2,256,1024]{2,1,0:T(8,128)(2,1)S(1)} %copy-done.1, bf16[2,256,1024]{2,1,0:T(8,128)(2,1)S(1)} %copy-done.3, ...), custom_call_target="tpu_custom_call" | custom-call | flops 2200000000 | bytes 4726784 | tf_op jit(solution)/shard_map/pair/pallas_call | solution.py:281
  26.0 24.8 %all-to-all-done.in_ref = bf16[64,5,16,128]{3,2,1,0:T(8,128)(2,1)S(1)} async-done(((bf16[64,5,16,128]{3,2,1,0:T(8,128)(2,1)}), bf16[64,5,16,128]{3,2,1,0:T(8,128)(2,1)S(1)}, u32[]{:S(2)}, u32[]{:S(2)}) %all-to-all-start) | async-done | bytes 1310752 | tf_op jit(solution)/shard_map/all_to_all | solution.py:292
  50.8 1.6 copy-done.15
  52.3 2.9 %recouple.1 = bf16[64,5,16,128]{3,2,1,0:T(8,128)(2,1)} custom-call(bf16[1024,1024]{1,0:T(8,128)(2,1)S(1)} %copy-done.15, bf16[64,5,16,128]{3,2,1,0:T(8,128)(2,1)S(1)} %all-to-all-done.in_ref), custom_call_target="tpu_custom_call" | custom-call | flops 1400000000 | bytes 4718592 | tf_op jit(solution)/shard_map/recouple/pallas_call | solution.py:281
  55.2 6.5 %all-to-all-start.1 = ((bf16[64,5,16,128]{3,2,1,0:T(8,128)(2,1)}), bf16[64,5,16,128]{3,2,1,0:T(8,128)(2,1)S(1)}, u32[]{:S(2)}, u32[]{:S(2)}) async-start(bf16[64,5,16,128]{3,2,1,0:T(8,128)(2,1)} %recouple.1), calls=%async_computation.1 | async-start | bytes 2621440 | tf_op jit(solution)/shard_map/all_to_all | solution.py:292
  63.0 1.5 collective-permute-start.1
  64.4 1.5 collective-permute-start.2
  66.0 13.1 %collective-permute-done.plus_ref = bf16[2,5,2,128,128]{4,3,2,1,0:T(8,128)(2,1)S(1)} collective-permute-done((bf16[2,5,2,128,128]{4,3,2,1,0:T(8,128)(2,1)}, bf16[2,5,2,128,128]{4,3,2,1,0:T(8,128)(2,1)S(1)}, u32[]{:S(2)}, u32[]{:S(2)}) %collective-permute-start) | collective-permute-done | bytes 655392 | tf_op jit(solution)/shard_map/ppermute | solution.py:297
  79.0 15.0 %collective-permute-done.2.minus_ref = bf16[2,5,2,128,128]{4,3,2,1,0:T(8,128)(2,1)S(1)} collective-permute-done((bf16[2,5,2,128,128]{4,3,2,1,0:T(8,128)(2,1)S(1)}, bf16[2,5,2,128,128]{4,3,2,1,0:T(8,128)(2,1)S(1)}, u32[]{:S(2)}, u32[]{:S(2)}) %collective-permute-start.2) | collective-permute-done | bytes 655392 | tf_op jit(solution)/shard_map/ppermute | solution.py:297
  95.3 2.4 %mirror.1 = (bf16[16,128,128]{2,1,0:T(8,128)(2,1)S(1)}, bf16[16,128,128]{2,1,0:T(8,128)(2,1)S(1)}, bf16[4,128,128]{2,1,0:T(8,128)(2,1)S(1)}) custom-call(bf16[64,5,16,128]{3,2,1,0:T(8,128)(2,1)S(1)} %all-to-all-done.1.in_ref), custom_call_target="tpu_custom_call" | custom-call | bytes 2490368 | tf_op jit(solution)/shard_map/mirror/pallas_call | solution.py:281
  97.6 1.5 collective-permute-start.3
  99.1 1.5 collective-permute-start.4
  100.6 1.5 collective-permute-start.5
  102.1 12.6 %collective-permute-done.5.far_ref = bf16[4,128,128]{2,1,0:T(8,128)(2,1)S(1)} collective-permute-done((bf16[4,128,128]{2,1,0:T(8,128)(2,1)S(1)}, bf16[4,128,128]{2,1,0:T(8,128)(2,1)S(1)}, u32[]{:S(2)}, u32[]{:S(2)}) %collective-permute-start.5) | collective-permute-done | bytes 131104 | tf_op jit(solution)/shard_map/ppermute | solution.py:297
  114.7 4.4 %product.1 = (f32[2,5,2,128,128]{4,3,2,1,0:T(8,128)S(1)}, bf16[2,5,128,128]{3,2,1,0:T(8,128)(2,1)S(1)}, bf16[2,3,128,128]{3,2,1,0:T(8,128)(2,1)S(1)}, bf16[2,5,128,128]{3,2,1,0:T(8,128)(2,1)S(1)}) custom-call(bf16[64,5,16,128]{3,2,1,0:T(8,128)(2,1)S(1)} %all-to-all-done.1.in_ref, bf16[16,128,128]{2,1,0:T(8,128)(2,1)S(1)} %collective-permute-done.3.plus_ref, ...), custom_call_target="tpu_custom_call" | custom-call | flops 1400000000 | bytes 4661248 | tf_op jit(solution)/shard_map/product/pallas_call | solution.py:281
  119.8 2.1 %collective-permute-start.8 = (bf16[2,5,128,128]{3,2,1,0:T(8,128)(2,1)S(1)}, bf16[2,5,128,128]{3,2,1,0:T(8,128)(2,1)S(1)}, u32[]{:S(2)}, u32[]{:S(2)}) collective-permute-start(bf16[2,5,128,128]{3,2,1,0:T(8,128)(2,1)S(1)} %get-tuple-element.46), channel_id=1, source_target_pairs={{0,3},{1,0},{2,1},{3,2},{4,7},{5,4},{6,5},{7,6},{8,11},{9,8},{10,9... | collective-permute-start | bytes 983048 | tf_op jit(solution)/shard_map/ppermute | solution.py:297
  121.9 8.2 %collective-permute-done.7.far_ref = bf16[2,3,128,128]{3,2,1,0:T(8,128)(2,1)S(1)} collective-permute-done((bf16[2,3,128,128]{3,2,1,0:T(8,128)(2,1)S(1)}, bf16[2,3,128,128]{3,2,1,0:T(8,128)(2,1)S(1)}, u32[]{:S(2)}, u32[]{:S(2)}) %collective-permute-start.7) | collective-permute-done | bytes 196640 | tf_op jit(solution)/shard_map/ppermute | solution.py:297
  130.0 1.5 sum.1
  131.5 33.1 %all_to_all.20.in_ref = bf16[64,40,128]{2,1,0:T(8,128)(2,1)S(1)} all-to-all(bf16[64,40,128]{2,1,0:T(8,128)(2,1)S(1)} %sum.1), channel_id=1, replica_groups=mesh['chan'=64,'panel'=4] {'chan'}, dimensions={0} | all-to-all | bytes 1310720 | tf_op jit(solution)/shard_map/all_to_all | solution.py:292
  165.2 26.0 %all_to_all.21.in_ref = bf16[64,40,128]{2,1,0:T(8,128)(2,1)S(1)} all-to-all(bf16[64,40,128]{2,1,0:T(8,128)(2,1)S(1)} %recouple_back.1), channel_id=1, replica_groups=mesh['chan'=64,'panel'=4] {'chan'}, dimensions={0} | all-to-all | bytes 1310720 | tf_op jit(solution)/shard_map/all_to_all | solution.py:292
  192.5 1.8 collective-permute-start.10
  194.6 4.5 %collective-permute-done.11.far_ref = bf16[2,128,128]{2,1,0:T(8,128)(2,1)S(1)} collective-permute-done((bf16[2,128,128]{2,1,0:T(8,128)(2,1)S(1)}, bf16[2,128,128]{2,1,0:T(8,128)(2,1)S(1)}, u32[]{:S(2)}, u32[]{:S(2)}) %collective-permute-start.11) | collective-permute-done | bytes 65568 | tf_op jit(solution)/shard_map/ppermute | solution.py:297
  199.0 1.4 finish.1
  (54 shorter events, 15.0 us)
Async XLA Ops:
  3.8 13.3 %copy-start.11 = (bf16[128,128]{1,0:T(8,128)(2,1)S(1)}, bf16[128,128]{1,0:T(8,128)(2,1)}, u32[]{:S(2)}) copy-start(bf16[128,128]{1,0:T(8,128)(2,1)} %forward_ref.1) | copy-start | bytes 98308
  3.8 13.3 %copy-start.12 = (bf16[128,128]{1,0:T(8,128)(2,1)S(1)}, bf16[128,128]{1,0:T(8,128)(2,1)}, u32[]{:S(2)}) copy-start(bf16[128,128]{1,0:T(8,128)(2,1)} %back_ref.1) | copy-start | bytes 98308
  3.8 46.9 %all-to-all-start = ((bf16[64,5,16,128]{3,2,1,0:T(8,128)(2,1)}), bf16[64,5,16,128]{3,2,1,0:T(8,128)(2,1)S(1)}, u32[]{:S(2)}, u32[]{:S(2)}) async-start(bf16[64,5,16,128]{3,2,1,0:T(8,128)(2,1)} %pack.1), calls=%async_computation | async-start | bytes 2621440 | tf_op jit(solution)/shard_map/all_to_all | solution.py:292
  17.2 3.3 %copy-start.16 = (f32[2,1024]{1,0:T(2,128)S(1)}, f32[2,1024]{1,0:T(2,128)}, u32[]{:S(2)}) copy-start(f32[2,1024]{1,0:T(2,128)} %param.9) | copy-start | bytes 24580
  17.2 3.3 %copy-start.17 = (s32[2]{0:T(128)S(1)}, s32[2]{0:T(128)}, u32[]{:S(2)}) copy-start(s32[2]{0:T(128)} %param.11) | copy-start | bytes 28
  17.2 3.3 %copy-start.1 = (bf16[2,256,1024]{2,1,0:T(8,128)(2,1)S(1)}, bf16[2,256,1024]{2,1,0:T(8,128)(2,1)}, u32[]{:S(2)}) copy-start(bf16[2,256,1024]{2,1,0:T(8,128)(2,1)} %eta_ref.3) | copy-start | bytes 3145732
  17.2 3.3 %copy-start.3 = (bf16[2,256,1024]{2,1,0:T(8,128)(2,1)S(1)}, bf16[2,256,1024]{2,1,0:T(8,128)(2,1)}, u32[]{:S(2)}) copy-start(bf16[2,256,1024]{2,1,0:T(8,128)(2,1)} %gamma_ref.3) | copy-start | bytes 3145732
  55.2 7.8 %copy-start.9 = (bf16[2,5,2,128,128]{4,3,2,1,0:T(8,128)(2,1)S(1)}, bf16[2,5,2,128,128]{4,3,2,1,0:T(8,128)(2,1)}, u32[]{:S(2)}) copy-start(bf16[2,5,2,128,128]{4,3,2,1,0:T(8,128)(2,1)} %copy-done.8) | copy-start | bytes 1966084
  55.2 9.2 %copy-start.7 = (bf16[2,5,2,128,128]{4,3,2,1,0:T(8,128)(2,1)S(1)}, bf16[2,5,2,128,128]{4,3,2,1,0:T(8,128)(2,1)}, u32[]{:S(2)}) copy-start(bf16[2,5,2,128,128]{4,3,2,1,0:T(8,128)(2,1)} %copy-done.6) | copy-start | bytes 1966084
  55.2 40.1 %all-to-all-start.1 = ((bf16[64,5,16,128]{3,2,1,0:T(8,128)(2,1)}), bf16[64,5,16,128]{3,2,1,0:T(8,128)(2,1)S(1)}, u32[]{:S(2)}, u32[]{:S(2)}) async-start(bf16[64,5,16,128]{3,2,1,0:T(8,128)(2,1)} %recouple.1), calls=%async_computation.1 | async-start | bytes 2621440 | tf_op jit(solution)/shard_map/all_to_all | solution.py:292
  61.7 17.4 %collective-permute-start = (bf16[2,5,2,128,128]{4,3,2,1,0:T(8,128)(2,1)}, bf16[2,5,2,128,128]{4,3,2,1,0:T(8,128)(2,1)S(1)}, u32[]{:S(2)}, u32[]{:S(2)}) collective-permute-start(bf16[2,5,2,128,128]{4,3,2,1,0:T(8,128)(2,1)} %copy-done.10), channel_id=1, source_target_pairs={{0,1},{1,2},{2,3},{3,0},{4,5},{5,6},{6,7},{7,4},{8,9},{9,10},{10,1... | collective-permute-start | bytes 1966088 | tf_op jit(solution)/shard_map/ppermute | solution.py:297
  63.0 16.1 %collective-permute-start.1 = (bf16[2,5,2,128,128]{4,3,2,1,0:T(8,128)(2,1)S(1)}, bf16[2,5,2,128,128]{4,3,2,1,0:T(8,128)(2,1)S(1)}, u32[]{:S(2)}, u32[]{:S(2)}) collective-permute-start(bf16[2,5,2,128,128]{4,3,2,1,0:T(8,128)(2,1)S(1)} %copy-done.9), channel_id=1, source_target_pairs={{0,3},{1,0},{2,1},{3,2},{4,7},{5,4},{6,5},{7,6},{8,11},{9,8},{10,9... | collective-permute-start | bytes 1966088 | tf_op jit(solution)/shard_map/ppermute | solution.py:297
  64.4 29.6 %collective-permute-start.2 = (bf16[2,5,2,128,128]{4,3,2,1,0:T(8,128)(2,1)S(1)}, bf16[2,5,2,128,128]{4,3,2,1,0:T(8,128)(2,1)S(1)}, u32[]{:S(2)}, u32[]{:S(2)}) collective-permute-start(bf16[2,5,2,128,128]{4,3,2,1,0:T(8,128)(2,1)S(1)} %copy-done.7), channel_id=1, source_target_pairs={{0,2},{1,3},{2,0},{3,1},{4,6},{5,7},{6,4},{7,5},{8,10},{9,11},{10,... | collective-permute-start | bytes 1966088 | tf_op jit(solution)/shard_map/ppermute | solution.py:297
  94.3 20.3 %copy-start.13 = (f32[2,1024]{1,0:T(2,128)S(1)}, f32[2,1024]{1,0:T(2,128)}, u32[]{:S(2)}) copy-start(f32[2,1024]{1,0:T(2,128)} %weight_ref.1) | copy-start | bytes 24580
  97.6 17.0 %collective-permute-start.3 = (bf16[16,128,128]{2,1,0:T(8,128)(2,1)S(1)}, bf16[16,128,128]{2,1,0:T(8,128)(2,1)S(1)}, u32[]{:S(2)}, u32[]{:S(2)}) collective-permute-start(bf16[16,128,128]{2,1,0:T(8,128)(2,1)S(1)} %get-tuple-element.40), channel_id=1, source_target_pairs={{0,1},{1,2},{2,3},{3,0},{4,5},{5,6},{6,7},{7,4},{8,9},{9,10},{10,1... | collective-permute-start | bytes 1572872 | tf_op jit(solution)/shard_map/ppermute | solution.py:297
  99.1 15.6 %collective-permute-start.4 = (bf16[16,128,128]{2,1,0:T(8,128)(2,1)S(1)}, bf16[16,128,128]{2,1,0:T(8,128)(2,1)S(1)}, u32[]{:S(2)}, u32[]{:S(2)}) collective-permute-start(bf16[16,128,128]{2,1,0:T(8,128)(2,1)S(1)} %get-tuple-element.41), channel_id=1, source_target_pairs={{0,3},{1,0},{2,1},{3,2},{4,7},{5,4},{6,5},{7,6},{8,11},{9,8},{10,9... | collective-permute-start | bytes 1572872 | tf_op jit(solution)/shard_map/ppermute | solution.py:297
  100.6 14.1 %collective-permute-start.5 = (bf16[4,128,128]{2,1,0:T(8,128)(2,1)S(1)}, bf16[4,128,128]{2,1,0:T(8,128)(2,1)S(1)}, u32[]{:S(2)}, u32[]{:S(2)}) collective-permute-start(bf16[4,128,128]{2,1,0:T(8,128)(2,1)S(1)} %get-tuple-element.42), channel_id=1, source_target_pairs={{0,2},{1,3},{2,0},{3,1},{4,6},{5,7},{6,4},{7,5},{8,10},{9,11},{10,... | collective-permute-start | bytes 393224 | tf_op jit(solution)/shard_map/ppermute | solution.py:297
  119.1 10.9 %collective-permute-start.6 = (bf16[2,5,128,128]{3,2,1,0:T(8,128)(2,1)S(1)}, bf16[2,5,128,128]{3,2,1,0:T(8,128)(2,1)S(1)}, u32[]{:S(2)}, u32[]{:S(2)}) collective-permute-start(bf16[2,5,128,128]{3,2,1,0:T(8,128)(2,1)S(1)} %get-tuple-element.44), channel_id=1, source_target_pairs={{0,1},{1,2},{2,3},{3,0},{4,5},{5,6},{6,7},{7,4},{8,9},{9,10},{10,1... | collective-permute-start | bytes 983048 | tf_op jit(solution)/shard_map/ppermute | solution.py:297
  119.8 10.3 %collective-permute-start.8 = (bf16[2,5,128,128]{3,2,1,0:T(8,128)(2,1)S(1)}, bf16[2,5,128,128]{3,2,1,0:T(8,128)(2,1)S(1)}, u32[]{:S(2)}, u32[]{:S(2)}) collective-permute-start(bf16[2,5,128,128]{3,2,1,0:T(8,128)(2,1)S(1)} %get-tuple-element.46), channel_id=1, source_target_pairs={{0,3},{1,0},{2,1},{3,2},{4,7},{5,4},{6,5},{7,6},{8,11},{9,8},{10,9... | collective-permute-start | bytes 983048 | tf_op jit(solution)/shard_map/ppermute | solution.py:297
  121.8 8.2 %collective-permute-start.7 = (bf16[2,3,128,128]{3,2,1,0:T(8,128)(2,1)S(1)}, bf16[2,3,128,128]{3,2,1,0:T(8,128)(2,1)S(1)}, u32[]{:S(2)}, u32[]{:S(2)}) collective-permute-start(bf16[2,3,128,128]{3,2,1,0:T(8,128)(2,1)S(1)} %get-tuple-element.45), channel_id=1, source_target_pairs={{0,2},{1,3},{2,0},{3,1},{4,6},{5,7},{6,4},{7,5},{8,10},{9,11},{10,... | collective-permute-start | bytes 589832 | tf_op jit(solution)/shard_map/ppermute | solution.py:297
  131.5 33.1 %copy-start.5 = (bf16[512,512]{1,0:T(8,128)(2,1)S(1)}, bf16[512,512]{1,0:T(8,128)(2,1)}, u32[]{:S(2)}) copy-start(bf16[512,512]{1,0:T(8,128)(2,1)} %copy-done.4) | copy-start | bytes 1572868
  191.5 7.6 %collective-permute-start.9 = (bf16[4,128,128]{2,1,0:T(8,128)(2,1)S(1)}, bf16[4,128,128]{2,1,0:T(8,128)(2,1)S(1)}, u32[]{:S(2)}, u32[]{:S(2)}) collective-permute-start(bf16[4,128,128]{2,1,0:T(8,128)(2,1)S(1)} %get-tuple-element.48), channel_id=1, source_target_pairs={{0,1},{1,2},{2,3},{3,0},{4,5},{5,6},{6,7},{7,4},{8,9},{9,10},{10,1... | collective-permute-start | bytes 393224 | tf_op jit(solution)/shard_map/ppermute | solution.py:297
  192.5 6.6 %collective-permute-start.10 = (bf16[4,128,128]{2,1,0:T(8,128)(2,1)S(1)}, bf16[4,128,128]{2,1,0:T(8,128)(2,1)S(1)}, u32[]{:S(2)}, u32[]{:S(2)}) collective-permute-start(bf16[4,128,128]{2,1,0:T(8,128)(2,1)S(1)} %get-tuple-element.49), channel_id=1, source_target_pairs={{0,3},{1,0},{2,1},{3,2},{4,7},{5,4},{6,5},{7,6},{8,11},{9,8},{10,9... | collective-permute-start | bytes 393224 | tf_op jit(solution)/shard_map/ppermute | solution.py:297
  194.2 4.8 %collective-permute-start.11 = (bf16[2,128,128]{2,1,0:T(8,128)(2,1)S(1)}, bf16[2,128,128]{2,1,0:T(8,128)(2,1)S(1)}, u32[]{:S(2)}, u32[]{:S(2)}) collective-permute-start(bf16[2,128,128]{2,1,0:T(8,128)(2,1)S(1)} %get-tuple-element.50), channel_id=1, source_target_pairs={{0,2},{1,3},{2,0},{3,1},{4,6},{5,7},{6,4},{7,5},{8,10},{9,11},{10,... | collective-permute-start | bytes 196616 | tf_op jit(solution)/shard_map/ppermute | solution.py:297
  (8 other events, 8.7 us)

commit v3 on v1

v3 whole, which is shorter than its diff:
```python
import jax
import jax.numpy as jnp
from jax import lax
from jax.experimental import pallas as pl
from jax.experimental.pallas import tpu as pltpu
from jax.sharding import PartitionSpec as P

BF16 = jnp.bfloat16
F32 = jnp.float32
OFFSETS = (0, 1, -2, 3, 4)
LANES = 128


def params():
    return pltpu.CompilerParams(vmem_limit_bytes=24 * 1024 * 1024)


def cost(flops, size):
    return pl.CostEstimate(flops=flops, bytes_accessed=size, transcendentals=0)


def tile_at(panel, l, offset):
    return pl.multiple_of(lax.rem(2 * panel + l + offset + 8, 8) * LANES, LANES)


def swap_blocks(x):
    lane = lax.broadcasted_iota(jnp.int32, (64, LANES), 1)
    top, bottom = x[:64], x[64:]
    low = lane < 64
    upper = jnp.where(low, top, pltpu.roll(bottom, 64, 1))
    lower = jnp.where(low, pltpu.roll(top, 64, 1), bottom)
    even = (lane[:32] & 32) == 0
    parts = []
    for half in (upper, lower):
        first, second = half[:32], half[32:]
        parts.append(jnp.where(even, first, pltpu.roll(second, 32, 1)))
        parts.append(jnp.where(even, pltpu.roll(first, 96, 1), second))
    return jnp.concatenate(parts, axis=0)


def contract_last(a, b):
    return lax.dot_general(a, b, (((1,), (1,)), ((), ())), preferred_element_type=F32)


def interleave(both):
    return [jnp.concatenate([both[0][:, r : r + 4], both[1][:, r : r + 4]], axis=1) for r in (0, 4)]


def pack_kernel(eta_ref, gamma_ref, out_ref, held, sems):
    panel = lax.axis_index("panel")
    copies = {}
    for arr, ref in enumerate((eta_ref, gamma_ref)):
        for l in range(2):
            for ch in range(2):
                rows = slice(l * 128, (l + 1) * 128)
                copy = pltpu.make_async_copy(ref.at[ch, rows], held.at[arr, ch, rows], sems.at[arr, l, ch])
                copy.start()
                copies[arr, l, ch] = copy
    for arr in range(2):
        for l in range(2):
            for ch in range(2):
                copies[arr, l, ch].wait()
            pieces = []
            for offset in OFFSETS:
                column = tile_at(panel, l, offset)
                pieces += interleave([swap_blocks(held[arr, ch, l * 128 : (l + 1) * 128, pl.ds(column, LANES)].astype(F32)).reshape(16, 8, LANES) for ch in range(2)])
            start = arr * 32 + l * 16
            out_ref[start : start + 16] = jnp.concatenate(pieces, axis=1).astype(BF16)


def spread_kernel(forward_ref, back_ref, weight_ref, forward_out, back_out, rows_out):
    panel = lax.axis_index("panel")
    for ch in range(2):
        for j in range(8):
            lane = weight_ref[ch : ch + 1, pl.ds(tile_at(panel, j, 0), LANES)]
            rows_out[ch, j] = jnp.broadcast_to(lane, (128, LANES)).T
    for ref, out in ((forward_ref, forward_out), (back_ref, back_out)):
        shift = 2
        size = 128 << shift
        row = lax.broadcasted_iota(jnp.int32, (size, 128), 0) >> shift
        column = lax.broadcasted_iota(jnp.int32, (size, 128), 1)
        copies = jnp.where(row == column, F32(1.0), F32(0.0)).astype(BF16)
        tall = jnp.dot(copies, ref[...], preferred_element_type=F32).astype(BF16)
        mask = (1 << shift) - 1
        for start in range(0, size, 256):
            wide = contract_last(tall[start : start + 256], copies)
            row = lax.broadcasted_iota(jnp.int32, wide.shape, 0) & mask
            column = lax.broadcasted_iota(jnp.int32, wide.shape, 1) & mask
            out[start : start + 256, :] = jnp.where(row == column, wide, F32(0.0)).astype(BF16)


def recouple_rows(table_ref, in_ref, count):
    value = in_ref[...].astype(F32)
    rhs = jnp.concatenate([value[:, q * 8 : q * 8 + 8].reshape(512, LANES) for q in range(count)], axis=1).astype(BF16)
    mixed = jnp.dot(table_ref[...], rhs, preferred_element_type=F32)
    return [mixed[:, q * LANES : (q + 1) * LANES].reshape(64, 8, LANES) for q in range(count)]


def recouple_kernel(table_ref, in_ref, out_ref):
    pieces = recouple_rows(table_ref, in_ref, 10)
    for ch in range(2):
        rows = [piece[:, ch * 4 : ch * 4 + 4] for piece in pieces]
        out_ref[:, ch * 40 : ch * 40 + 40] = jnp.concatenate(rows, axis=1).astype(BF16)


def tile_of(ref, ch, arr, l, t):
    start = arr * 32 + l * 16
    return ref[start : start + 16].astype(F32)[:, ch * 40 + t * 8 : ch * 40 + t * 8 + 8].reshape(128, LANES)


PLUS = ((1, 1), (0, 3))
MINUS = ((0, 2), (1, 2))
FAR = ((1, 3),)


def mirror_kernel(in_ref, plus_ref, minus_ref, far_ref):
    for ch in range(2):
        for arr in range(2):
            base = (ch * 2 + arr) * 4
            for u, (l, t) in enumerate(PLUS + ((0, 4), (1, 3))):
                plus_ref[base + u] = tile_of(in_ref, ch, arr, l, t).T.astype(BF16)
            for u, (l, t) in enumerate(MINUS):
                minus_ref[base + u] = tile_of(in_ref, ch, arr, l, t).T.astype(BF16)
            for u, (l, t) in enumerate(((1, 3), (1, 4))):
                tile = tile_of(in_ref, ch, arr, l, t)
                minus_ref[base + 2 + u] = (-tile if arr == 0 else tile).astype(BF16)
            far_ref[ch * 2 + arr] = tile_of(in_ref, ch, arr, *FAR[0]).T.astype(BF16)


def product_kernel(in_ref, plus_ref, minus_ref, far_ref, weight_ref, rows_ref, *refs):
    for ch in range(2):
        product_channel(ch, in_ref, plus_ref, minus_ref, far_ref, weight_ref, rows_ref, *refs)


def product_channel(
    ch, in_ref, plus_ref, minus_ref, far_ref, weight_ref, rows_ref, own_ref, plus_out, far_out, minus_out, by_lane, by_row, plain, edge_lane, edge_row, edge_plain
):
    own_ref, plus_out, far_out, minus_out, by_lane, by_row, plain, edge_lane, edge_row, edge_plain = (
        ref.at[ch] for ref in (own_ref, plus_out, far_out, minus_out, by_lane, by_row, plain, edge_lane, edge_row, edge_plain)
    )
    panel = lax.axis_index("panel")
    lanes = [weight_ref[ch : ch + 1, pl.ds(tile_at(panel, j, 0), LANES)] for j in range(4)]
    rows = [rows_ref[ch, j] for j in range(8)]
    for l in range(2):

        def put(arr, offset, value):
            j = (l + offset) % 8
            place = (slice(j * 128, (j + 1) * 128), slice(l * LANES, (l + 1) * LANES))
            if arr == 0:
                by_lane[place] = (value * lanes[l]).astype(BF16)
                by_row[place] = (value * rows[j]).astype(BF16)
            else:
                plain[place] = value.astype(BF16)

        for arr in range(2):
            for t, offset in enumerate(OFFSETS):
                tile = tile_of(in_ref, ch, arr, l, t)
                put(arr, offset, -tile if arr == 0 else tile)
            put(arr, 2, minus_ref[(ch * 2 + arr) * 4 + l].astype(F32))
            if l == 0:
                put(arr, -1, plus_ref[(ch * 2 + arr) * 4].astype(F32))
                put(arr, -3, far_ref[ch * 2 + arr].astype(F32))
            else:
                put(arr, -1, tile_of(in_ref, ch, arr, 0, 1).T)
                put(arr, -3, plus_ref[(ch * 2 + arr) * 4 + 1].astype(F32))
    for arr in range(2):
        for r in range(2):
            for c in range(2):
                ref = plus_ref if c == 0 else minus_ref
                value = ref[(ch * 2 + arr) * 4 + 2 + r].astype(F32)
                place = (slice(r * 128, (r + 1) * 128), slice(c * LANES, (c + 1) * LANES))
                if arr == 0:
                    edge_lane[place] = (value * lanes[2 + c]).astype(BF16)
                    edge_row[place] = (value * rows[6 + r]).astype(BF16)
                else:
                    edge_plain[place] = value.astype(BF16)

    def block(ref, j):
        return ref[j * 256 : (j + 1) * 256]

    def inner(i, j):
        return contract_last(block(by_lane, i), block(plain, j)) + contract_last(block(plain, i), block(by_lane, j))

    def tile(value, i, j):
        return value[i * 128 : (i + 1) * 128, j * 128 : (j + 1) * 128]

    diagonal = contract_first(by_row[...], plain[...]) + contract_first(plain[...], by_row[...])
    for (l, t), (i, j) in (((0, 0), (0, 0)), ((0, 1), (0, 1)), ((1, 0), (1, 1))):
        own_ref[l, t] = -tile(diagonal, i, j)
    ahead = inner(0, 1) - contract_first(block(by_row, 3), edge_plain[...]) - contract_first(block(plain, 3), edge_row[...])
    own_ref[0, 3] = tile(ahead, 0, 1)
    own_ref[1, 1] = tile(ahead, 1, 0)
    plus_out[0] = tile(ahead, 0, 0).astype(BF16)
    plus_out[1] = tile(ahead, 1, 1).astype(BF16)
    behind = inner(3, 0)
    behind += jnp.dot(edge_lane[...], block(plain, 1), preferred_element_type=F32)
    behind -= jnp.dot(edge_plain[...], block(by_row, 1), preferred_element_type=F32)
    own_ref[0, 2] = tile(behind, 0, 0)
    own_ref[1, 2] = tile(behind, 1, 1)
    minus_out[0] = tile(behind, 0, 1).astype(BF16)
    minus_out[1] = tile(behind, 1, 0).astype(BF16)
    across = inner(0, 2)
    for (l, t), (i, j) in ACROSS:
        own_ref[l, t] = tile(across, i, j)
    for ref, start, value in ((far_out, 0, inner(2, 0)), (minus_out, 2, inner(3, 1)), (plus_out, 2, inner(1, 3))):
        for u, (held, (i, j)) in enumerate(ACROSS):
            ref[start + u] = tile(value, i, j).astype(BF16)


ACROSS = (((0, 4), (0, 0)), ((1, 3), (1, 0)), ((1, 4), (1, 1)))


def total(own_ref, plus_ref, far_ref, minus_ref, l, t):
    value = own_ref[l, t]
    if t == 2:
        return (value + plus_ref[l].astype(F32)).T
    if (l, t) in ((0, 3), (1, 1)):
        return value + minus_ref[l].astype(F32)
    for u, (held, _) in enumerate(ACROSS):
        if held == (l, t):
            near = plus_ref[2 + u].astype(F32) + minus_ref[2 + u].astype(F32)
            return value + far_ref[u].astype(F32) + near
    return value


def sum_kernel(own_ref, plus_ref, far_ref, minus_ref, out_ref):
    refs = (own_ref, plus_ref, far_ref, minus_ref)
    for l in range(2):
        low, high = [], []
        for t in range(5):
            pieces = interleave([swap_blocks(total(*(ref.at[ch] for ref in refs), l, t)).reshape(16, 8, LANES) for ch in range(2)])
            low.append(pieces[0])
            high.append(pieces[1])
        out_ref[l * 32 : l * 32 + 16] = jnp.concatenate(low, axis=1).astype(BF16)
        out_ref[l * 32 + 16 : l * 32 + 32] = jnp.concatenate(high, axis=1).astype(BF16)


def recouple_back_kernel(table_ref, in_ref, out_ref):
    out_ref[...] = jnp.concatenate(recouple_rows(table_ref, in_ref, 5), axis=1).astype(BF16)


def back_tile(ref, l, t, ch):
    low = ref[l * 32 : l * 32 + 16].astype(F32)[:, t * 8 + ch * 4 : t * 8 + ch * 4 + 4]
    high = ref[l * 32 + 16 : l * 32 + 32].astype(F32)[:, t * 8 + ch * 4 : t * 8 + ch * 4 + 4]
    return jnp.concatenate([low, high], axis=1).reshape(128, LANES)


def back_mirror_kernel(in_ref, pp_ref, plus_ref, minus_ref, far_ref):
    for ch in range(2):
        for ref, held in ((plus_ref, PLUS), (minus_ref, MINUS), (far_ref, FAR)):
            for u, (l, t) in enumerate(held):
                ref[ch * len(held) + u] = (pp_ref[l, t, ch].T + back_tile(in_ref, l, t, ch)).astype(BF16)


def finish_kernel(in_ref, plus_ref, minus_ref, far_ref, pp_ref, out_ref):
    panel = lax.axis_index("panel")
    for ch in range(2):
        for l in range(2):

            def put(offset, value):
                out_ref[ch, l * 128 : (l + 1) * 128, pl.ds(tile_at(panel, l, offset), LANES)] = value.astype(BF16)

            for t, offset in enumerate(OFFSETS):
                put(offset, pp_ref[l, t, ch] + back_tile(in_ref, l, t, ch).T)
            put(2, minus_ref[ch * 2 + l])
            if l == 0:
                put(-1, plus_ref[ch * 2])
                put(-3, far_ref[ch])
            else:
                put(-1, pp_ref[0, 1, ch].T + back_tile(in_ref, 0, 1, ch))
                put(-3, plus_ref[ch * 2 + 1])


def contract_first(a, b):
    return lax.dot_general(a, b, (((0,), (0,)), ((), ())), preferred_element_type=F32)


def pair_kernel(eta_ref, gamma_ref, weight_ref, own_ref, plus_ref, far_ref, minus_ref, scaled, plain):
    panel = lax.axis_index("panel")
    for ch in range(2):
        for l in range(2):
            row = weight_ref[ch : ch + 1, pl.ds(tile_at(panel, l, 0), LANES)]
            weight = jnp.broadcast_to(row, (128, LANES)).T
            rows = slice(l * 128, (l + 1) * 128)
            for j in range(8):
                source = pl.ds(tile_at(panel, j, 0), LANES)
                columns = slice(j * LANES, (j + 1) * LANES)
                scaled[ch, rows, columns] = (eta_ref[ch, rows, source].astype(F32) * weight).astype(BF16)
                plain[ch, rows, columns] = gamma_ref[ch, rows, source]
        for owner, ref in enumerate((own_ref, plus_ref, far_ref, minus_ref)):
            columns = slice(owner * 256, (owner + 1) * 256)
            total = contract_first(scaled[ch, :, columns], plain[ch]) + contract_first(plain[ch, :, columns], scaled[ch])
            for l in range(2):
                for t, offset in enumerate(OFFSETS):
                    column = (2 * owner + l + offset) % 8 * LANES
                    ref[l, t, ch] = -total[l * 128 : (l + 1) * 128, column : column + LANES].astype(BF16)


def pair_sum_kernel(own_ref, plus_ref, far_ref, minus_ref, out_ref):
    for l in range(2):
        for t in range(5):
            for ch in range(2):
                parts = [ref[l, t, ch].astype(F32) for ref in (own_ref, plus_ref, far_ref, minus_ref)]
                out_ref[l, t, ch] = (parts[0] + parts[1]) + (parts[2] + parts[3])


def call(kernel, shapes, args, flops=0, scratch=(), name=None, dtype=BF16, space=None):
    single = not isinstance(shapes, list)
    outs = [shapes] if single else shapes
    types = dtype if isinstance(dtype, list) else [dtype] * len(outs)
    shaped = [jax.ShapeDtypeStruct(s, d) for s, d in zip(outs, types)]
    size = sum(a.size * a.dtype.itemsize for a in [*args, *shaped])
    return pl.pallas_call(
        kernel,
        out_shape=shaped[0] if single else shaped,
        in_specs=[pl.BlockSpec(memory_space=space or pltpu.VMEM)] * len(args),
        scratch_shapes=list(scratch),
        compiler_params=params(),
        cost_estimate=cost(flops, size),
        name=name,
    )(*args)


def exchange(operand, axis):
    return lax.all_to_all(operand, axis, split_axis=0, concat_axis=0, tiled=True)


def step(value, by):
    return lax.ppermute(value, "panel", [(i, (i + by) % 4) for i in range(4)])


def mirror(plus, minus, far):
    return step(plus, 1), step(minus, 3), step(far, 2)


def shards(eta, gamma, pp_weight, cc_weight, live_pairs, forward_table, back_table):
    positions = lax.broadcasted_iota(jnp.int32, pp_weight.shape, 1)
    weight_pp = jnp.where(positions < live_pairs[:, None], pp_weight, F32(0.0))
    packed = call(
        pack_kernel,
        (64, 80, LANES),
        (eta, gamma),
        scratch=[pltpu.VMEM((2, 2, 256, 1024), BF16), pltpu.SemaphoreType.DMA((2, 2, 2))],
        name="pack",
        space=pltpu.HBM,
    )
    forward_wide, back_wide, weight_rows = call(
        spread_kernel,
        [(512, 512), (512, 512), (2, 8, 128, LANES)],
        (forward_table, back_table, cc_weight),
        flops=300_000_000,
        name="spread",
        dtype=[BF16, BF16, F32],
    )
    packed = exchange(packed, "chan")
    pp_own, *pp = call(
        pair_kernel,
        [(2, 5, 2, 128, LANES)] * 4,
        (eta, gamma, weight_pp),
        flops=2_200_000_000,
        scratch=[pltpu.VMEM((2, 256, 1024), BF16)] * 2,
        name="pair",
    )
    pp_plus, pp_minus = step(pp[0], 1), step(pp[2], 3)
    packed, pp_own, pp_far, pp_plus, pp_minus = lax.optimization_barrier((packed, pp_own, pp[1], pp_plus, pp_minus))
    mixed = call(recouple_kernel, (64, 80, LANES), (forward_wide, packed), flops=700_000_000, name="recouple")
    mixed = exchange(mixed, "chan")
    pp_far = step(pp_far, 2)
    pp_part = call(pair_sum_kernel, (2, 5, 2, 128, LANES), (pp_own, pp_plus, pp_far, pp_minus), name="pair_sum", dtype=F32)
    mixed, pp_part = lax.optimization_barrier((mixed, pp_part))
    sends = call(mirror_kernel, [(16, 128, LANES), (16, 128, LANES), (4, 128, LANES)], (mixed,), name="mirror")
    received = mirror(*sends)
    own, *partial = call(
        product_kernel,
        [(2, 2, 5, 128, LANES), (2, 5, 128, LANES), (2, 3, 128, LANES), (2, 5, 128, LANES)],
        (mixed, *received, cc_weight, weight_rows),
        flops=1_400_000_000,
        scratch=[pltpu.VMEM((2, 1024, 256), BF16)] * 3 + [pltpu.VMEM((2, 256, 256), BF16)] * 3,
        name="product",
        dtype=[F32, BF16, BF16, BF16],
    )
    plus, minus, far = mirror(partial[0], partial[2], partial[1])
    part = call(sum_kernel, (64, 40, LANES), (own, plus, far, minus), name="sum")
    part = exchange(part, "chan")
    part = call(recouple_back_kernel, (64, 40, LANES), (back_wide, part), flops=400_000_000, name="recouple_back")
    part = exchange(part, "chan")
    back_sends = call(back_mirror_kernel, [(4, 128, LANES), (4, 128, LANES), (2, 128, LANES)], (part, pp_part), name="back_mirror")
    back_received = mirror(*back_sends)
    return call(finish_kernel, (2, 256, 1024), (part, *back_received, pp_part), name="finish")


def solution(mesh):
    in_specs = (
        P("chan", "panel", None),
        P("chan", "panel", None),
        P("chan", None),
        P("chan", None),
        P("chan"),
        P(),
        P(),
    )
    out_specs = P("chan", "panel", None)
    return jax.shard_map(shards, mesh=mesh, in_specs=in_specs, out_specs=out_specs, check_vma=False)
```

time: 213 us -> 196 us (0.920)
  blocking collectives: 89.9 us -> 58 us
  waiting for transfers between devices: 65.3 us -> 75.2 us
  starting transfers between devices: 31.1 us -> 36.2 us
  Pallas kernels: 16.9 us -> 14.7 us
  local copies, waits for them, and re-layouts: 8.76 us -> 10.9 us
    all_to_all x3 -> x2, blocking collectives: 89.9 us -> 58 us  [exchange(): lax.all_to_all(operand, axis, split_axis=0, concat_axis=0, tiled=True)]
    ppermute x9 -> x12, waiting for transfers between devices: 39.6 us -> 51.4 us  [step(): return lax.ppermute(value, 'panel', [(i, (i + by) % 4) for i in range(4)])]
    ppermute x9 -> x12, starting transfers between devices: 11.3 us -> 16.5 us  [step(): return lax.ppermute(value, 'panel', [(i, (i + by) % 4) for i in range(4)])]
    pallas_call x11, Pallas kernels: 16.9 us -> 14.7 us  [call(): pl.pallas_call(kernel, out_shape=shaped[0] if single else shaped, in_spec...]
    unnamed x36 -> x44, local copies, waits for them, and re-layouts: 8.76 us -> 10.9 us
  transfers between devices with their start and end apart: 11 -> 14, of which waited for: 6 -> 7; matrix products, arithmetic and copies ran while one was open for 0% -> 0% of each run, Pallas kernels for 2% -> 2%
where the time goes in v3:
time: 196 us; the launch traced here: 195 us
  waiting for transfers between devices  75.2 us (38%)
  blocking collectives  58 us (30%)
  starting transfers between devices  36.2 us (18%)
  Pallas kernels  14.7 us (8%)
  local copies, waits for them, and re-layouts  10.9 us (6%)
    all_to_all x2, blocking collectives, exchange(): lax.all_to_all(operand, axis, split_axis=0, concat_axis=0, tiled=True)  58 us
    ppermute x12, waiting for transfers between devices, step(): return lax.ppermute(value, 'panel', [(i, (i + by) % 4) for i in range(4)])  51.4 us
    all_to_all x2, waiting for transfers between devices, exchange(): lax.all_to_all(operand, axis, split_axis=0, concat_axis=0, tiled=True)  23.8 us
    all_to_all x2, starting transfers between devices, exchange(): lax.all_to_all(operand, axis, split_axis=0, concat_axis=0, tiled=True)  19.8 us
    ppermute x12, starting transfers between devices, step(): return lax.ppermute(value, 'panel', [(i, (i + by) % 4) for i in range(4)])  16.5 us
    pallas_call x11, Pallas kernels, call(): pl.pallas_call(kernel, out_shape=shaped[0] if single else shaped, in_spec...  14.7 us
    unnamed x44, local copies, waits for them, and re-layouts  10.9 us
  transfers between devices with their start and end apart: 14, of which 7 were waited for; matrix products, arithmetic and copies ran while one was open for 0% of the time, Pallas kernels for 2%

profile of v3, /device:TPU:1, one launch (start us, length us, event | category | flops | bytes accessed | tf_op | source)
XLA Modules:
  0.0 195.3 jit_solution(11250752525294791251)
XLA Ops:
  0.0 1.2 copy-done.1
  2.5 3.6 %pack.1 = bf16[64,80,128]{2,1,0:T(8,128)(2,1)} custom-call(bf16[2,256,1024]{2,1,0:T(8,128)(2,1)S(1)} %copy-done.1, bf16[2,256,1024]{2,1,0:T(8,128)(2,1)S(1)} %copy-done.3), custom_call_target="tpu_custom_call" | custom-call | bytes 3407872 | tf_op jit(solution)/shard_map/pack/pallas_call | solution.py:313
  6.1 13.3 %all-to-all-start = ((bf16[64,80,128]{2,1,0:T(8,128)(2,1)}), bf16[64,80,128]{2,1,0:T(8,128)(2,1)S(1)}, u32[]{:S(2)}, u32[]{:S(2)}) async-start(bf16[64,80,128]{2,1,0:T(8,128)(2,1)} %pack.1), calls=%async_computation | async-start | bytes 2621440 | tf_op jit(solution)/shard_map/all_to_all | solution.py:325
  19.5 2.9 %pair.1 = (bf16[2,5,2,128,128]{4,3,2,1,0:T(8,128)(2,1)S(1)}, bf16[2,5,2,128,128]{4,3,2,1,0:T(8,128)(2,1)S(1)}, bf16[2,5,2,128,128]{4,3,2,1,0:T(8,128)(2,1)S(1)}, bf16[2,5,2,128,128]{4,3,2,1,0:T(8,128)(2,1)S(1)}) custom-call(bf16[2,256,1024]{2,1,0:T(8,128)(2,1)S(1)} %copy-done.2, bf16[2,256,1024]{2,1,0:T(8,128)(2,1)S(1)} %copy-done.4, ...), custom_call_target="tpu_custom_call" | custom-call | flops 2200000000 | bytes 4726784 | tf_op jit(solution)/shard_map/pair/pallas_call | solution.py:313
  25.4 1.5 collective-permute-start.1
  29.3 11.9 %collective-permute-done.plus_ref = bf16[2,5,2,128,128]{4,3,2,1,0:T(8,128)(2,1)S(1)} collective-permute-done((bf16[2,5,2,128,128]{4,3,2,1,0:T(8,128)(2,1)S(1)}, bf16[2,5,2,128,128]{4,3,2,1,0:T(8,128)(2,1)S(1)}, u32[]{:S(2)}, u32[]{:S(2)}) %collective-permute-start) | collective-permute-done | bytes 655392 | tf_op jit(solution)/shard_map/ppermute | solution.py:329
  42.9 10.1 %all-to-all-done.in_ref = bf16[64,80,128]{2,1,0:T(8,128)(2,1)S(1)} async-done(((bf16[64,80,128]{2,1,0:T(8,128)(2,1)}), bf16[64,80,128]{2,1,0:T(8,128)(2,1)S(1)}, u32[]{:S(2)}, u32[]{:S(2)}) %all-to-all-start) | async-done | bytes 1310752 | tf_op jit(solution)/shard_map/all_to_all | solution.py:325
  55.0 6.5 %all-to-all-start.1 = ((bf16[64,80,128]{2,1,0:T(8,128)(2,1)}), bf16[64,80,128]{2,1,0:T(8,128)(2,1)S(1)}, u32[]{:S(2)}, u32[]{:S(2)}) async-start(bf16[64,80,128]{2,1,0:T(8,128)(2,1)} %copy-done), calls=%async_computation.1 | async-start | bytes 2621440 | tf_op jit(solution)/shard_map/all_to_all | solution.py:325
  61.5 2.8 %collective-permute-start.2 = (bf16[2,5,2,128,128]{4,3,2,1,0:T(8,128)(2,1)S(1)}, bf16[2,5,2,128,128]{4,3,2,1,0:T(8,128)(2,1)S(1)}, u32[]{:S(2)}, u32[]{:S(2)}) collective-permute-start(bf16[2,5,2,128,128]{4,3,2,1,0:T(8,128)(2,1)S(1)} %copy-done.14), channel_id=1, source_target_pairs={{0,2},{1,3},{2,0},{3,1},{4,6},{5,7},{6,4},{7,5},{8,10},{9,11},{10,... | collective-permute-start | bytes 1966088 | tf_op jit(solution)/shard_map/ppermute | solution.py:329
  64.3 14.6 %collective-permute-done.2.far_ref = bf16[2,5,2,128,128]{4,3,2,1,0:T(8,128)(2,1)S(1)} collective-permute-done((bf16[2,5,2,128,128]{4,3,2,1,0:T(8,128)(2,1)S(1)}, bf16[2,5,2,128,128]{4,3,2,1,0:T(8,128)(2,1)S(1)}, u32[]{:S(2)}, u32[]{:S(2)}) %collective-permute-start.2) | collective-permute-done | bytes 655392 | tf_op jit(solution)/shard_map/ppermute | solution.py:329
  81.4 13.7 %all-to-all-done.1.in_ref = bf16[64,80,128]{2,1,0:T(8,128)(2,1)S(1)} async-done(((bf16[64,80,128]{2,1,0:T(8,128)(2,1)}), bf16[64,80,128]{2,1,0:T(8,128)(2,1)S(1)}, u32[]{:S(2)}, u32[]{:S(2)}) %all-to-all-start.1) | async-done | bytes 1310752 | tf_op jit(solution)/shard_map/all_to_all | solution.py:325
  95.4 1.3 collective-permute-start.3
  96.6 1.5 collective-permute-start.4
  98.1 1.5 collective-permute-start.5
  99.6 12.6 %collective-permute-done.5.far_ref = bf16[4,128,128]{2,1,0:T(8,128)(2,1)S(1)} collective-permute-done((bf16[4,128,128]{2,1,0:T(8,128)(2,1)S(1)}, bf16[4,128,128]{2,1,0:T(8,128)(2,1)S(1)}, u32[]{:S(2)}, u32[]{:S(2)}) %collective-permute-start.5) | collective-permute-done | bytes 131104 | tf_op jit(solution)/shard_map/ppermute | solution.py:329
  112.2 2.2 %product.1 = (f32[2,2,5,128,128]{4,3,2,1,0:T(8,128)S(1)}, bf16[2,5,128,128]{3,2,1,0:T(8,128)(2,1)S(1)}, bf16[2,3,128,128]{3,2,1,0:T(8,128)(2,1)S(1)}, bf16[2,5,128,128]{3,2,1,0:T(8,128)(2,1)S(1)}) custom-call(bf16[64,80,128]{2,1,0:T(8,128)(2,1)S(1)} %all-to-all-done.1.in_ref, bf16[16,128,128]{2,1,0:T(8,128)(2,1)S(1)} %collective-permute-done.3.plus_ref, ...), custom_call_target="tpu_custom_call" | custom-call | flops 1400000000 | bytes 5709824 | tf_op jit(solution)/shard_map/product/pallas_call | solution.py:313
  115.1 2.1 %collective-permute-start.8 = (bf16[2,5,128,128]{3,2,1,0:T(8,128)(2,1)S(1)}, bf16[2,5,128,128]{3,2,1,0:T(8,128)(2,1)S(1)}, u32[]{:S(2)}, u32[]{:S(2)}) collective-permute-start(bf16[2,5,128,128]{3,2,1,0:T(8,128)(2,1)S(1)} %get-tuple-element.48), channel_id=1, source_target_pairs={{0,3},{1,0},{2,1},{3,2},{4,7},{5,4},{6,5},{7,6},{8,11},{9,8},{10,9... | collective-permute-start | bytes 983048 | tf_op jit(solution)/shard_map/ppermute | solution.py:329
  117.2 8.2 %collective-permute-done.7.far_ref = bf16[2,3,128,128]{3,2,1,0:T(8,128)(2,1)S(1)} collective-permute-done((bf16[2,3,128,128]{3,2,1,0:T(8,128)(2,1)S(1)}, bf16[2,3,128,128]{3,2,1,0:T(8,128)(2,1)S(1)}, u32[]{:S(2)}, u32[]{:S(2)}) %collective-permute-start.7) | collective-permute-done | bytes 196640 | tf_op jit(solution)/shard_map/ppermute | solution.py:329
  125.4 1.5 sum.1
  126.9 32.0 %all_to_all.20.in_ref = bf16[64,40,128]{2,1,0:T(8,128)(2,1)S(1)} all-to-all(bf16[64,40,128]{2,1,0:T(8,128)(2,1)S(1)} %sum.1), channel_id=1, replica_groups=mesh['chan'=64,'panel'=4] {'chan'}, dimensions={0} | all-to-all | bytes 1310720 | tf_op jit(solution)/shard_map/all_to_all | solution.py:325
  159.4 26.0 %all_to_all.21.in_ref = bf16[64,40,128]{2,1,0:T(8,128)(2,1)S(1)} all-to-all(bf16[64,40,128]{2,1,0:T(8,128)(2,1)S(1)} %recouple_back.1), channel_id=1, replica_groups=mesh['chan'=64,'panel'=4] {'chan'}, dimensions={0} | all-to-all | bytes 1310720 | tf_op jit(solution)/shard_map/all_to_all | solution.py:325
  186.4 2.2 %collective-permute-start.10 = (bf16[4,128,128]{2,1,0:T(8,128)(2,1)S(1)}, bf16[4,128,128]{2,1,0:T(8,128)(2,1)S(1)}, u32[]{:S(2)}, u32[]{:S(2)}) collective-permute-start(bf16[4,128,128]{2,1,0:T(8,128)(2,1)S(1)} %get-tuple-element.51), channel_id=1, source_target_pairs={{0,3},{1,0},{2,1},{3,2},{4,7},{5,4},{6,5},{7,6},{8,11},{9,8},{10,9... | collective-permute-start | bytes 393224 | tf_op jit(solution)/shard_map/ppermute | solution.py:329
  189.6 4.2 %collective-permute-done.11.far_ref = bf16[2,128,128]{2,1,0:T(8,128)(2,1)S(1)} collective-permute-done((bf16[2,128,128]{2,1,0:T(8,128)(2,1)S(1)}, bf16[2,128,128]{2,1,0:T(8,128)(2,1)S(1)}, u32[]{:S(2)}, u32[]{:S(2)}) %collective-permute-start.11) | collective-permute-done | bytes 65568 | tf_op jit(solution)/shard_map/ppermute | solution.py:329
  193.8 1.4 finish.1
  (62 shorter events, 16.3 us)
Async XLA Ops:
  6.1 13.4 %copy-start.20 = (f32[2,1024]{1,0:T(2,128)S(1)}, f32[2,1024]{1,0:T(2,128)}, u32[]{:S(2)}) copy-start(f32[2,1024]{1,0:T(2,128)} %param.9) | copy-start | bytes 24580
  6.1 13.4 %copy-start.21 = (s32[2]{0:T(128)S(1)}, s32[2]{0:T(128)}, u32[]{:S(2)}) copy-start(s32[2]{0:T(128)} %param.11) | copy-start | bytes 28
  6.1 13.4 %copy-start.2 = (bf16[2,256,1024]{2,1,0:T(8,128)(2,1)S(1)}, bf16[2,256,1024]{2,1,0:T(8,128)(2,1)}, u32[]{:S(2)}) copy-start(bf16[2,256,1024]{2,1,0:T(8,128)(2,1)} %eta_ref.3) | copy-start | bytes 3145732
  6.1 13.4 %copy-start.4 = (bf16[2,256,1024]{2,1,0:T(8,128)(2,1)S(1)}, bf16[2,256,1024]{2,1,0:T(8,128)(2,1)}, u32[]{:S(2)}) copy-start(bf16[2,256,1024]{2,1,0:T(8,128)(2,1)} %gamma_ref.3) | copy-start | bytes 3145732
  6.1 46.9 %all-to-all-start = ((bf16[64,80,128]{2,1,0:T(8,128)(2,1)}), bf16[64,80,128]{2,1,0:T(8,128)(2,1)S(1)}, u32[]{:S(2)}, u32[]{:S(2)}) async-start(bf16[64,80,128]{2,1,0:T(8,128)(2,1)} %pack.1), calls=%async_computation | async-start | bytes 2621440 | tf_op jit(solution)/shard_map/all_to_all | solution.py:325
  19.5 7.3 %copy-start.15 = (bf16[128,128]{1,0:T(8,128)(2,1)S(1)}, bf16[128,128]{1,0:T(8,128)(2,1)}, u32[]{:S(2)}) copy-start(bf16[128,128]{1,0:T(8,128)(2,1)} %forward_ref.1) | copy-start | bytes 98308
  19.5 7.3 %copy-start.16 = (bf16[128,128]{1,0:T(8,128)(2,1)S(1)}, bf16[128,128]{1,0:T(8,128)(2,1)}, u32[]{:S(2)}) copy-start(bf16[128,128]{1,0:T(8,128)(2,1)} %back_ref.1) | copy-start | bytes 98308
  19.5 7.3 %copy-start.17 = (f32[2,1024]{1,0:T(2,128)S(1)}, f32[2,1024]{1,0:T(2,128)}, u32[]{:S(2)}) copy-start(f32[2,1024]{1,0:T(2,128)} %weight_ref.3) | copy-start | bytes 24580
  24.2 17.1 %collective-permute-start = (bf16[2,5,2,128,128]{4,3,2,1,0:T(8,128)(2,1)S(1)}, bf16[2,5,2,128,128]{4,3,2,1,0:T(8,128)(2,1)S(1)}, u32[]{:S(2)}, u32[]{:S(2)}) collective-permute-start(bf16[2,5,2,128,128]{4,3,2,1,0:T(8,128)(2,1)S(1)} %get-tuple-element.33), channel_id=1, source_target_pairs={{0,1},{1,2},{2,3},{3,0},{4,5},{5,6},{6,7},{7,4},{8,9},{9,10},{10,1... | collective-permute-start | bytes 1966088 | tf_op jit(solution)/shard_map/ppermute | solution.py:329
  25.4 16.7 %collective-permute-start.1 = (bf16[2,5,2,128,128]{4,3,2,1,0:T(8,128)(2,1)S(1)}, bf16[2,5,2,128,128]{4,3,2,1,0:T(8,128)(2,1)S(1)}, u32[]{:S(2)}, u32[]{:S(2)}) collective-permute-start(bf16[2,5,2,128,128]{4,3,2,1,0:T(8,128)(2,1)S(1)} %get-tuple-element.34), channel_id=1, source_target_pairs={{0,3},{1,0},{2,1},{3,2},{4,7},{5,4},{6,5},{7,6},{8,11},{9,8},{10,9... | collective-permute-start | bytes 1966088 | tf_op jit(solution)/shard_map/ppermute | solution.py:329
  55.0 23.9 %copy-start.6 = (bf16[2,5,2,128,128]{4,3,2,1,0:T(8,128)(2,1)S(1)}, bf16[2,5,2,128,128]{4,3,2,1,0:T(8,128)(2,1)}, u32[]{:S(2)}) copy-start(bf16[2,5,2,128,128]{4,3,2,1,0:T(8,128)(2,1)} %copy-done.5) | copy-start | bytes 1966084
  55.0 40.1 %all-to-all-start.1 = ((bf16[64,80,128]{2,1,0:T(8,128)(2,1)}), bf16[64,80,128]{2,1,0:T(8,128)(2,1)S(1)}, u32[]{:S(2)}, u32[]{:S(2)}) async-start(bf16[64,80,128]{2,1,0:T(8,128)(2,1)} %copy-done), calls=%async_computation.1 | async-start | bytes 2621440 | tf_op jit(solution)/shard_map/all_to_all | solution.py:325
  61.5 17.4 %collective-permute-start.2 = (bf16[2,5,2,128,128]{4,3,2,1,0:T(8,128)(2,1)S(1)}, bf16[2,5,2,128,128]{4,3,2,1,0:T(8,128)(2,1)S(1)}, u32[]{:S(2)}, u32[]{:S(2)}) collective-permute-start(bf16[2,5,2,128,128]{4,3,2,1,0:T(8,128)(2,1)S(1)} %copy-done.14), channel_id=1, source_target_pairs={{0,2},{1,3},{2,0},{3,1},{4,6},{5,7},{6,4},{7,5},{8,10},{9,11},{10,... | collective-permute-start | bytes 1966088 | tf_op jit(solution)/shard_map/ppermute | solution.py:329
  95.0 17.2 %copy-start.19 = (f32[2,8,128,128]{3,2,1,0:T(8,128)S(1)}, f32[2,8,128,128]{3,2,1,0:T(8,128)}, u32[]{:S(2)}) copy-start(f32[2,8,128,128]{3,2,1,0:T(8,128)} %copy-done.18) | copy-start | bytes 3145732
  95.4 16.8 %collective-permute-start.3 = (bf16[16,128,128]{2,1,0:T(8,128)(2,1)S(1)}, bf16[16,128,128]{2,1,0:T(8,128)(2,1)S(1)}, u32[]{:S(2)}, u32[]{:S(2)}) collective-permute-start(bf16[16,128,128]{2,1,0:T(8,128)(2,1)S(1)} %get-tuple-element.41), channel_id=1, source_target_pairs={{0,1},{1,2},{2,3},{3,0},{4,5},{5,6},{6,7},{7,4},{8,9},{9,10},{10,1... | collective-permute-start | bytes 1572872 | tf_op jit(solution)/shard_map/ppermute | solution.py:329
  96.6 15.6 %collective-permute-start.4 = (bf16[16,128,128]{2,1,0:T(8,128)(2,1)S(1)}, bf16[16,128,128]{2,1,0:T(8,128)(2,1)S(1)}, u32[]{:S(2)}, u32[]{:S(2)}) collective-permute-start(bf16[16,128,128]{2,1,0:T(8,128)(2,1)S(1)} %get-tuple-element.42), channel_id=1, source_target_pairs={{0,3},{1,0},{2,1},{3,2},{4,7},{5,4},{6,5},{7,6},{8,11},{9,8},{10,9... | collective-permute-start | bytes 1572872 | tf_op jit(solution)/shard_map/ppermute | solution.py:329
  98.1 14.1 %collective-permute-start.5 = (bf16[4,128,128]{2,1,0:T(8,128)(2,1)S(1)}, bf16[4,128,128]{2,1,0:T(8,128)(2,1)S(1)}, u32[]{:S(2)}, u32[]{:S(2)}) collective-permute-start(bf16[4,128,128]{2,1,0:T(8,128)(2,1)S(1)} %get-tuple-element.43), channel_id=1, source_target_pairs={{0,2},{1,3},{2,0},{3,1},{4,6},{5,7},{6,4},{7,5},{8,10},{9,11},{10,... | collective-permute-start | bytes 393224 | tf_op jit(solution)/shard_map/ppermute | solution.py:329
  114.4 10.9 %collective-permute-start.6 = (bf16[2,5,128,128]{3,2,1,0:T(8,128)(2,1)S(1)}, bf16[2,5,128,128]{3,2,1,0:T(8,128)(2,1)S(1)}, u32[]{:S(2)}, u32[]{:S(2)}) collective-permute-start(bf16[2,5,128,128]{3,2,1,0:T(8,128)(2,1)S(1)} %get-tuple-element.46), channel_id=1, source_target_pairs={{0,1},{1,2},{2,3},{3,0},{4,5},{5,6},{6,7},{7,4},{8,9},{9,10},{10,1... | collective-permute-start | bytes 983048 | tf_op jit(solution)/shard_map/ppermute | solution.py:329
  115.1 10.3 %collective-permute-start.8 = (bf16[2,5,128,128]{3,2,1,0:T(8,128)(2,1)S(1)}, bf16[2,5,128,128]{3,2,1,0:T(8,128)(2,1)S(1)}, u32[]{:S(2)}, u32[]{:S(2)}) collective-permute-start(bf16[2,5,128,128]{3,2,1,0:T(8,128)(2,1)S(1)} %get-tuple-element.48), channel_id=1, source_target_pairs={{0,3},{1,0},{2,1},{3,2},{4,7},{5,4},{6,5},{7,6},{8,11},{9,8},{10,9... | collective-permute-start | bytes 983048 | tf_op jit(solution)/shard_map/ppermute | solution.py:329
  117.2 8.2 %collective-permute-start.7 = (bf16[2,3,128,128]{3,2,1,0:T(8,128)(2,1)S(1)}, bf16[2,3,128,128]{3,2,1,0:T(8,128)(2,1)S(1)}, u32[]{:S(2)}, u32[]{:S(2)}) collective-permute-start(bf16[2,3,128,128]{3,2,1,0:T(8,128)(2,1)S(1)} %get-tuple-element.47), channel_id=1, source_target_pairs={{0,2},{1,3},{2,0},{3,1},{4,6},{5,7},{6,4},{7,5},{8,10},{9,11},{10,... | collective-permute-start | bytes 589832 | tf_op jit(solution)/shard_map/ppermute | solution.py:329
  126.9 32.0 %copy-start.12 = (bf16[512,512]{1,0:T(8,128)(2,1)S(1)}, bf16[512,512]{1,0:T(8,128)(2,1)}, u32[]{:S(2)}) copy-start(bf16[512,512]{1,0:T(8,128)(2,1)} %copy-done.11) | copy-start | bytes 1572868
  185.7 8.1 %collective-permute-start.9 = (bf16[4,128,128]{2,1,0:T(8,128)(2,1)S(1)}, bf16[4,128,128]{2,1,0:T(8,128)(2,1)S(1)}, u32[]{:S(2)}, u32[]{:S(2)}) collective-permute-start(bf16[4,128,128]{2,1,0:T(8,128)(2,1)S(1)} %get-tuple-element.50), channel_id=1, source_target_pairs={{0,1},{1,2},{2,3},{3,0},{4,5},{5,6},{6,7},{7,4},{8,9},{9,10},{10,1... | collective-permute-start | bytes 393224 | tf_op jit(solution)/shard_map/ppermute | solution.py:329
  186.4 7.5 %collective-permute-start.10 = (bf16[4,128,128]{2,1,0:T(8,128)(2,1)S(1)}, bf16[4,128,128]{2,1,0:T(8,128)(2,1)S(1)}, u32[]{:S(2)}, u32[]{:S(2)}) collective-permute-start(bf16[4,128,128]{2,1,0:T(8,128)(2,1)S(1)} %get-tuple-element.51), channel_id=1, source_target_pairs={{0,3},{1,0},{2,1},{3,2},{4,7},{5,4},{6,5},{7,6},{8,11},{9,8},{10,9... | collective-permute-start | bytes 393224 | tf_op jit(solution)/shard_map/ppermute | solution.py:329
  188.5 5.3 %collective-permute-start.11 = (bf16[2,128,128]{2,1,0:T(8,128)(2,1)S(1)}, bf16[2,128,128]{2,1,0:T(8,128)(2,1)S(1)}, u32[]{:S(2)}, u32[]{:S(2)}) collective-permute-start(bf16[2,128,128]{2,1,0:T(8,128)(2,1)S(1)} %get-tuple-element.52), channel_id=1, source_target_pairs={{0,2},{1,3},{2,0},{3,1},{4,6},{5,7},{6,4},{7,5},{8,10},{9,11},{10,... | collective-permute-start | bytes 196616 | tf_op jit(solution)/shard_map/ppermute | solution.py:329
  (12 other events, 17.3 us)

commit v4 on v3

--- a/solution.py
+++ b/solution.py
@@ -11,8 +11,8 @@
 LANES = 128
 
 
-def params():
-    return pltpu.CompilerParams(vmem_limit_bytes=24 * 1024 * 1024)
+def params(mib=24):
+    return pltpu.CompilerParams(vmem_limit_bytes=mib * 1024 * 1024)
 
 
 def cost(flops, size):
@@ -48,23 +48,36 @@
 
 def pack_kernel(eta_ref, gamma_ref, out_ref, held, sems):
     panel = lax.axis_index("panel")
+    either = jnp.where(panel < 2, 0, 1)
+    row = lax.broadcasted_iota(jnp.int32, (128, LANES), 0)
+    column = lax.broadcasted_iota(jnp.int32, (128, LANES), 1)
+    source = (("both", 0, 0, 0, either, 0, 1, 1), (1, "both", 0, 0, 1, either, 1, 1))
     copies = {}
-    for arr, ref in enumerate((eta_ref, gamma_ref)):
-        for l in range(2):
-            for ch in range(2):
+    for l in range(2):
+        for ch in range(2):
+            for arr, ref in enumerate((eta_ref, gamma_ref)):
                 rows = slice(l * 128, (l + 1) * 128)
-                copy = pltpu.make_async_copy(ref.at[ch, rows], held.at[arr, ch, rows], sems.at[arr, l, ch])
+                copy = pltpu.make_async_copy(ref.at[ch, rows], held.at[arr, ch, rows], sems.at[l, ch, arr])
                 copy.start()
-                copies[arr, l, ch] = copy
-    for arr in range(2):
-        for l in range(2):
-            for ch in range(2):
-                copies[arr, l, ch].wait()
+                copies[l, ch, arr] = copy
+
+    def tile(ch, l, j):
+        def read(arr):
+            return held[arr, ch, l * 128 : (l + 1) * 128, pl.ds(tile_at(panel, j, 0), LANES)]
+
+        kind = source[l][j]
+        value = jnp.where(row < column, read(0), read(1)) if kind == "both" else read(kind)
+        return swap_blocks(value).astype(F32).reshape(16, 8, LANES)
+
+    for l in range(2):
+        for ch in range(2):
+            for arr in range(2):
+                copies[l, ch, arr].wait()
+        for part in range(2):
             pieces = []
-            for offset in OFFSETS:
-                column = tile_at(panel, l, offset)
-                pieces += interleave([swap_blocks(held[arr, ch, l * 128 : (l + 1) * 128, pl.ds(column, LANES)].astype(F32)).reshape(16, 8, LANES) for ch in range(2)])
-            start = arr * 32 + l * 16
+            for j in range(part * 4, part * 4 + 4):
+                pieces += interleave([tile(ch, l, j) for ch in range(2)])
+            start = part * 32 + l * 16
             out_ref[start : start + 16] = jnp.concatenate(pieces, axis=1).astype(BF16)
 
 
@@ -97,15 +110,15 @@
 
 
 def recouple_kernel(table_ref, in_ref, out_ref):
-    pieces = recouple_rows(table_ref, in_ref, 10)
+    pieces = recouple_rows(table_ref, in_ref, 8)
     for ch in range(2):
         rows = [piece[:, ch * 4 : ch * 4 + 4] for piece in pieces]
-        out_ref[:, ch * 40 : ch * 40 + 40] = jnp.concatenate(rows, axis=1).astype(BF16)
-
-
-def tile_of(ref, ch, arr, l, t):
-    start = arr * 32 + l * 16
-    return ref[start : start + 16].astype(F32)[:, ch * 40 + t * 8 : ch * 40 + t * 8 + 8].reshape(128, LANES)
+        out_ref[:, ch * 32 : ch * 32 + 32] = jnp.concatenate(rows, axis=1).astype(BF16)
+
+
+def tile_of(ref, ch, l, j):
+    start = j // 4 * 32 + l * 16
+    return ref[start : start + 16].astype(F32)[:, ch * 32 + j % 4 * 8 : ch * 32 + j % 4 * 8 + 8].reshape(128, LANES)
 
 
 PLUS = ((1, 1), (0, 3))
@@ -115,16 +128,14 @@
 
 def mirror_kernel(in_ref, plus_ref, minus_ref, far_ref):
     for ch in range(2):
-        for arr in range(2):
-            base = (ch * 2 + arr) * 4
-            for u, (l, t) in enumerate(PLUS + ((0, 4), (1, 3))):
-                plus_ref[base + u] = tile_of(in_ref, ch, arr, l, t).T.astype(BF16)
-            for u, (l, t) in enumerate(MINUS):
-                minus_ref[base + u] = tile_of(in_ref, ch, arr, l, t).T.astype(BF16)
-            for u, (l, t) in enumerate(((1, 3), (1, 4))):
-                tile = tile_of(in_ref, ch, arr, l, t)
-                minus_ref[base + 2 + u] = (-tile if arr == 0 else tile).astype(BF16)
-            far_ref[ch * 2 + arr] = tile_of(in_ref, ch, arr, *FAR[0]).T.astype(BF16)
+        for l in range(2):
+            for k in range(2):
+                plus_ref[ch, 0, l, k] = tile_of(in_ref, ch, l, 2 + k).astype(BF16)
+                minus_ref[ch, 0, l, k] = tile_of(in_ref, ch, l, 6 + k).astype(BF16)
+                across = tile_of(in_ref, ch, l, 4 + k).astype(BF16)
+                plus_ref[ch, 1, l, k] = across
+                minus_ref[ch, 1, l, k] = across
+                far_ref[ch, l, k] = across
 
 
 def product_kernel(in_ref, plus_ref, minus_ref, far_ref, weight_ref, rows_ref, *refs):
@@ -141,39 +152,53 @@
     panel = lax.axis_index("panel")
     lanes = [weight_ref[ch : ch + 1, pl.ds(tile_at(panel, j, 0), LANES)] for j in range(4)]
     rows = [rows_ref[ch, j] for j in range(8)]
+
+    def held(l, j):
+        return tile_of(in_ref, ch, l, j)
+
+    def plus(part, i, k):
+        return plus_ref[ch, part, i, k].astype(F32)
+
+    def minus(part, i, k):
+        return minus_ref[ch, part, i, k].astype(F32)
+
+    def far(i, k):
+        return far_ref[ch, i, k].astype(F32)
+
+    def put(j, l, eta, gamma):
+        place = (slice(j * 128, (j + 1) * 128), slice(l * LANES, (l + 1) * LANES))
+        by_lane[place] = (eta * lanes[l]).astype(BF16)
+        by_row[place] = (eta * rows[j]).astype(BF16)
+        plain[place] = gamma.astype(BF16)
+
+    def put_edge(i, k, eta, gamma):
+        place = (slice(i * 128, (i + 1) * 128), slice(k * LANES, (k + 1) * LANES))
+        edge_lane[place] = (eta * lanes[2 + k]).astype(BF16)
+        edge_row[place] = (eta * rows[6 + i]).astype(BF16)
+        edge_plain[place] = gamma.astype(BF16)
+
+    row = lax.broadcasted_iota(jnp.int32, (128, LANES), 0)
+    column = lax.broadcasted_iota(jnp.int32, (128, LANES), 1)
+    row_block, column_block = row >> 5, column >> 5
+    first = (row_block > column_block) | ((row_block == column_block) & (row < column))
     for l in range(2):
-
-        def put(arr, offset, value):
-            j = (l + offset) % 8
-            place = (slice(j * 128, (j + 1) * 128), slice(l * LANES, (l + 1) * LANES))
-            if arr == 0:
-                by_lane[place] = (value * lanes[l]).astype(BF16)
-                by_row[place] = (value * rows[j]).astype(BF16)
-            else:
-                plain[place] = value.astype(BF16)
-
-        for arr in range(2):
-            for t, offset in enumerate(OFFSETS):
-                tile = tile_of(in_ref, ch, arr, l, t)
-                put(arr, offset, -tile if arr == 0 else tile)
-            put(arr, 2, minus_ref[(ch * 2 + arr) * 4 + l].astype(F32))
-            if l == 0:
-                put(arr, -1, plus_ref[(ch * 2 + arr) * 4].astype(F32))
-                put(arr, -3, far_ref[ch * 2 + arr].astype(F32))
-            else:
-                put(arr, -1, tile_of(in_ref, ch, arr, 0, 1).T)
-                put(arr, -3, plus_ref[(ch * 2 + arr) * 4 + 1].astype(F32))
-    for arr in range(2):
-        for r in range(2):
-            for c in range(2):
-                ref = plus_ref if c == 0 else minus_ref
-                value = ref[(ch * 2 + arr) * 4 + 2 + r].astype(F32)
-                place = (slice(r * 128, (r + 1) * 128), slice(c * LANES, (c + 1) * LANES))
-                if arr == 0:
-                    edge_lane[place] = (value * lanes[2 + c]).astype(BF16)
-                    edge_row[place] = (value * rows[6 + r]).astype(BF16)
-                else:
-                    edge_plain[place] = value.astype(BF16)
+        value = held(l, l)
+        mirrored = value.T
+        put(l, l, jnp.where(row == column, F32(0.0), jnp.where(first, -value, mirrored)), jnp.where(first, mirrored, value))
+        for k in range(2):
+            put(2 + k, l, -held(l, 2 + k), minus(0, k, l).T)
+            put(6 + k, l, plus(0, k, l).T, held(l, 6 + k))
+        value, mirrored = held(l, 4 + l), far(l, l).T
+        put(4 + l, l, jnp.where(panel < 2, -value, mirrored), jnp.where(panel < 2, mirrored, value))
+        straight, mirrored = minus(1, l, l), plus(1, l, l).T
+        before = lax.rem(panel + 3, 4) < 2
+        put_edge(l, l, jnp.where(before, mirrored, -straight), jnp.where(before, straight, mirrored))
+    put(1, 0, -held(0, 1), held(1, 0).T)
+    put(0, 1, held(0, 1).T, held(1, 0))
+    put(5, 0, -held(0, 5), far(1, 0).T)
+    put(4, 1, far(0, 1).T, held(1, 4))
+    put_edge(0, 1, plus(1, 0, 1).T, minus(1, 1, 0))
+    put_edge(1, 0, -minus(1, 0, 1), plus(1, 1, 0).T)
 
     def block(ref, j):
         return ref[j * 256 : (j + 1) * 256]
@@ -315,7 +340,7 @@
         out_shape=shaped[0] if single else shaped,
         in_specs=[pl.BlockSpec(memory_space=space or pltpu.VMEM)] * len(args),
         scratch_shapes=list(scratch),
-        compiler_params=params(),
+        compiler_params=params(60 if space else 24),
         cost_estimate=cost(flops, size),
         name=name,
     )(*args)
@@ -338,7 +363,7 @@
     weight_pp = jnp.where(positions < live_pairs[:, None], pp_weight, F32(0.0))
     packed = call(
         pack_kernel,
-        (64, 80, LANES),
+        (64, 64, LANES),
         (eta, gamma),
         scratch=[pltpu.VMEM((2, 2, 256, 1024), BF16), pltpu.SemaphoreType.DMA((2, 2, 2))],
         name="pack",
@@ -363,12 +388,12 @@
     )
     pp_plus, pp_minus = step(pp[0], 1), step(pp[2], 3)
     packed, pp_own, pp_far, pp_plus, pp_minus = lax.optimization_barrier((packed, pp_own, pp[1], pp_plus, pp_minus))
-    mixed = call(recouple_kernel, (64, 80, LANES), (forward_wide, packed), flops=700_000_000, name="recouple")
+    mixed = call(recouple_kernel, (64, 64, LANES), (forward_wide, packed), flops=700_000_000, name="recouple")
     mixed = exchange(mixed, "chan")
     pp_far = step(pp_far, 2)
     pp_part = call(pair_sum_kernel, (2, 5, 2, 128, LANES), (pp_own, pp_plus, pp_far, pp_minus), name="pair_sum", dtype=F32)
     mixed, pp_part = lax.optimization_barrier((mixed, pp_part))
-    sends = call(mirror_kernel, [(16, 128, LANES), (16, 128, LANES), (4, 128, LANES)], (mixed,), name="mirror")
+    sends = call(mirror_kernel, [(2, 2, 2, 2, 128, LANES), (2, 2, 2, 2, 128, LANES), (2, 2, 2, 128, LANES)], (mixed,), name="mirror")
     received = mirror(*sends)
     own, *partial = call(
         product_kernel,

time: 196 us -> 186 us (0.949)
  waiting for transfers between devices: 75.2 us -> 68.3 us
  local copies, waits for them, and re-layouts: 10.9 us -> 7.76 us
    all_to_all x2, waiting for transfers between devices: 23.8 us -> 12.5 us  [exchange(): lax.all_to_all(operand, axis, split_axis=0, concat_axis=0, tiled=True)]
    ppermute x12, waiting for transfers between devices: 51.4 us -> 55.7 us  [step(): return lax.ppermute(value, 'panel', [(i, (i + by) % 4) for i in range(4)])]
    unnamed x44 -> x34, local copies, waits for them, and re-layouts: 10.9 us -> 7.76 us
where the time goes in v4:
time: 186 us
  waiting for transfers between devices  68.3 us (37%)
  blocking collectives  57.5 us (31%)
  starting transfers between devices  36.1 us (19%)
  Pallas kernels  16 us (9%)
  local copies, waits for them, and re-layouts  7.76 us (4%)
    all_to_all x2, blocking collectives, exchange(): lax.all_to_all(operand, axis, split_axis=0, concat_axis=0, tiled=True)  57.5 us
    ppermute x12, waiting for transfers between devices, step(): return lax.ppermute(value, 'panel', [(i, (i + by) % 4) for i in range(4)])  55.7 us
    all_to_all x2, starting transfers between devices, exchange(): lax.all_to_all(operand, axis, split_axis=0, concat_axis=0, tiled=True)  20.2 us
    pallas_call x11, Pallas kernels, call(): pl.pallas_call(kernel, out_shape=shaped[0] if single else shaped, in_spec...  16 us
    ppermute x12, starting transfers between devices, step(): return lax.ppermute(value, 'panel', [(i, (i + by) % 4) for i in range(4)])  15.9 us
    all_to_all x2, waiting for transfers between devices, exchange(): lax.all_to_all(operand, axis, split_axis=0, concat_axis=0, tiled=True)  12.5 us
    unnamed x34, local copies, waits for them, and re-layouts  7.76 us
  transfers between devices with their start and end apart: 14, of which 7 were waited for; matrix products, arithmetic and copies ran while one was open for 0% of the time, Pallas kernels for 2%

profile of v4, /device:TPU:1, one launch (start us, length us, event | category | flops | bytes accessed | tf_op | source)
XLA Modules:
  0.0 185.9 jit_solution(17307622612857339363)
XLA Ops:
  0.0 4.0 %pack.1 = bf16[64,64,128]{2,1,0:T(8,128)(2,1)} custom-call(bf16[2,256,1024]{2,1,0:T(8,128)(2,1)} %eta_ref.3, bf16[2,256,1024]{2,1,0:T(8,128)(2,1)} %gamma_ref.3), custom_call_target="tpu_custom_call" | custom-call | bytes 3145728 | tf_op jit(solution)/shard_map/pack/pallas_call | solution.py:338
  4.0 13.3 %all-to-all-start = ((bf16[64,64,128]{2,1,0:T(8,128)(2,1)}), bf16[64,64,128]{2,1,0:T(8,128)(2,1)S(1)}, u32[]{:S(2)}, u32[]{:S(2)}) async-start(bf16[64,64,128]{2,1,0:T(8,128)(2,1)} %pack.1), calls=%async_computation | async-start | bytes 2097152 | tf_op jit(solution)/shard_map/all_to_all | solution.py:350
  17.4 2.9 %pair.1 = (bf16[2,5,2,128,128]{4,3,2,1,0:T(8,128)(2,1)S(1)}, bf16[2,5,2,128,128]{4,3,2,1,0:T(8,128)(2,1)S(1)}, bf16[2,5,2,128,128]{4,3,2,1,0:T(8,128)(2,1)S(1)}, bf16[2,5,2,128,128]{4,3,2,1,0:T(8,128)(2,1)S(1)}) custom-call(bf16[2,256,1024]{2,1,0:T(8,128)(2,1)S(1)} %copy-done, bf16[2,256,1024]{2,1,0:T(8,128)(2,1)S(1)} %copy-done.1, ...), custom_call_target="tpu_custom_call" | custom-call | flops 2200000000 | bytes 4726784 | tf_op jit(solution)/shard_map/pair/pallas_call | solution.py:338
  23.3 1.5 collective-permute-start.1
  26.4 12.7 %collective-permute-done.plus_ref = bf16[2,5,2,128,128]{4,3,2,1,0:T(8,128)(2,1)S(1)} collective-permute-done((bf16[2,5,2,128,128]{4,3,2,1,0:T(8,128)(2,1)S(1)}, bf16[2,5,2,128,128]{4,3,2,1,0:T(8,128)(2,1)S(1)}, u32[]{:S(2)}, u32[]{:S(2)}) %collective-permute-start) | collective-permute-done | bytes 655392 | tf_op jit(solution)/shard_map/ppermute | solution.py:354
  40.8 4.5 %all-to-all-done.in_ref = bf16[64,64,128]{2,1,0:T(8,128)(2,1)S(1)} async-done(((bf16[64,64,128]{2,1,0:T(8,128)(2,1)}), bf16[64,64,128]{2,1,0:T(8,128)(2,1)S(1)}, u32[]{:S(2)}, u32[]{:S(2)}) %all-to-all-start) | async-done | bytes 1048608 | tf_op jit(solution)/shard_map/all_to_all | solution.py:350
  45.3 1.7 recouple.1
  47.0 6.9 %all-to-all-start.1 = ((bf16[64,64,128]{2,1,0:T(8,128)(2,1)}), bf16[64,64,128]{2,1,0:T(8,128)(2,1)S(1)}, u32[]{:S(2)}, u32[]{:S(2)}) async-start(bf16[64,64,128]{2,1,0:T(8,128)(2,1)} %recouple.1), calls=%async_computation.1 | async-start | bytes 2097152 | tf_op jit(solution)/shard_map/all_to_all | solution.py:350
  53.9 2.5 %collective-permute-start.2 = (bf16[2,5,2,128,128]{4,3,2,1,0:T(8,128)(2,1)S(1)}, bf16[2,5,2,128,128]{4,3,2,1,0:T(8,128)(2,1)S(1)}, u32[]{:S(2)}, u32[]{:S(2)}) collective-permute-start(bf16[2,5,2,128,128]{4,3,2,1,0:T(8,128)(2,1)S(1)} %copy-done.9), channel_id=1, source_target_pairs={{0,2},{1,3},{2,0},{3,1},{4,6},{5,7},{6,4},{7,5},{8,10},{9,11},{10,... | collective-permute-start | bytes 1966088 | tf_op jit(solution)/shard_map/ppermute | solution.py:354
  56.4 14.9 %collective-permute-done.2.far_ref = bf16[2,5,2,128,128]{4,3,2,1,0:T(8,128)(2,1)S(1)} collective-permute-done((bf16[2,5,2,128,128]{4,3,2,1,0:T(8,128)(2,1)S(1)}, bf16[2,5,2,128,128]{4,3,2,1,0:T(8,128)(2,1)S(1)}, u32[]{:S(2)}, u32[]{:S(2)}) %collective-permute-start.2) | collective-permute-done | bytes 655392 | tf_op jit(solution)/shard_map/ppermute | solution.py:354
  73.8 8.1 %all-to-all-done.1.in_ref = bf16[64,64,128]{2,1,0:T(8,128)(2,1)S(1)} async-done(((bf16[64,64,128]{2,1,0:T(8,128)(2,1)}), bf16[64,64,128]{2,1,0:T(8,128)(2,1)S(1)}, u32[]{:S(2)}, u32[]{:S(2)}) %all-to-all-start.1) | async-done | bytes 1048608 | tf_op jit(solution)/shard_map/all_to_all | solution.py:350
  83.0 1.8 collective-permute-start.4
  84.8 1.2 collective-permute-start.5
  86.0 15.7 %collective-permute-done.5.far_ref = bf16[2,2,2,128,128]{4,3,2,1,0:T(8,128)(2,1)S(1)} collective-permute-done((bf16[2,2,2,128,128]{4,3,2,1,0:T(8,128)(2,1)S(1)}, bf16[2,2,2,128,128]{4,3,2,1,0:T(8,128)(2,1)S(1)}, u32[]{:S(2)}, u32[]{:S(2)}) %collective-permute-start.5) | collective-permute-done | bytes 262176 | tf_op jit(solution)/shard_map/ppermute | solution.py:354
  101.7 1.2 copy-done.14
  102.9 2.5 %product.1 = (f32[2,2,5,128,128]{4,3,2,1,0:T(8,128)S(1)}, bf16[2,5,128,128]{3,2,1,0:T(8,128)(2,1)S(1)}, bf16[2,3,128,128]{3,2,1,0:T(8,128)(2,1)S(1)}, bf16[2,5,128,128]{3,2,1,0:T(8,128)(2,1)S(1)}) custom-call(bf16[64,64,128]{2,1,0:T(8,128)(2,1)S(1)} %all-to-all-done.1.in_ref, bf16[2,2,2,2,128,128]{5,4,3,2,1,0:T(8,128)(2,1)S(1)} %collective-permute-done.3.plus_ref, ...), custom_call_target="tpu_custom_call" | custom-call | flops 1400000000 | bytes 5578752 | tf_op jit(solution)/shard_map/product/pallas_call | solution.py:338
  106.1 2.1 %collective-permute-start.8 = (bf16[2,5,128,128]{3,2,1,0:T(8,128)(2,1)S(1)}, bf16[2,5,128,128]{3,2,1,0:T(8,128)(2,1)S(1)}, u32[]{:S(2)}, u32[]{:S(2)}) collective-permute-start(bf16[2,5,128,128]{3,2,1,0:T(8,128)(2,1)S(1)} %get-tuple-element.48), channel_id=1, source_target_pairs={{0,3},{1,0},{2,1},{3,2},{4,7},{5,4},{6,5},{7,6},{8,11},{9,8},{10,9... | collective-permute-start | bytes 983048 | tf_op jit(solution)/shard_map/ppermute | solution.py:354
  108.2 8.3 %collective-permute-done.7.far_ref = bf16[2,3,128,128]{3,2,1,0:T(8,128)(2,1)S(1)} collective-permute-done((bf16[2,3,128,128]{3,2,1,0:T(8,128)(2,1)S(1)}, bf16[2,3,128,128]{3,2,1,0:T(8,128)(2,1)S(1)}, u32[]{:S(2)}, u32[]{:S(2)}) %collective-permute-start.7) | collective-permute-done | bytes 196640 | tf_op jit(solution)/shard_map/ppermute | solution.py:354
  116.5 1.5 sum.1
  118.0 31.5 %all_to_all.20.in_ref = bf16[64,40,128]{2,1,0:T(8,128)(2,1)S(1)} all-to-all(bf16[64,40,128]{2,1,0:T(8,128)(2,1)S(1)} %sum.1), channel_id=1, replica_groups=mesh['chan'=64,'panel'=4] {'chan'}, dimensions={0} | all-to-all | bytes 1310720 | tf_op jit(solution)/shard_map/all_to_all | solution.py:350
  150.0 26.0 %all_to_all.21.in_ref = bf16[64,40,128]{2,1,0:T(8,128)(2,1)S(1)} all-to-all(bf16[64,40,128]{2,1,0:T(8,128)(2,1)S(1)} %recouple_back.1), channel_id=1, replica_groups=mesh['chan'=64,'panel'=4] {'chan'}, dimensions={0} | all-to-all | bytes 1310720 | tf_op jit(solution)/shard_map/all_to_all | solution.py:350
  177.0 2.2 %collective-permute-start.10 = (bf16[4,128,128]{2,1,0:T(8,128)(2,1)S(1)}, bf16[4,128,128]{2,1,0:T(8,128)(2,1)S(1)}, u32[]{:S(2)}, u32[]{:S(2)}) collective-permute-start(bf16[4,128,128]{2,1,0:T(8,128)(2,1)S(1)} %get-tuple-element.51), channel_id=1, source_target_pairs={{0,3},{1,0},{2,1},{3,2},{4,7},{5,4},{6,5},{7,6},{8,11},{9,8},{10,9... | collective-permute-start | bytes 393224 | tf_op jit(solution)/shard_map/ppermute | solution.py:354
  180.2 4.2 %collective-permute-done.11.far_ref = bf16[2,128,128]{2,1,0:T(8,128)(2,1)S(1)} collective-permute-done((bf16[2,128,128]{2,1,0:T(8,128)(2,1)S(1)}, bf16[2,128,128]{2,1,0:T(8,128)(2,1)S(1)}, u32[]{:S(2)}, u32[]{:S(2)}) %collective-permute-start.11) | collective-permute-done | bytes 65568 | tf_op jit(solution)/shard_map/ppermute | solution.py:354
  184.5 1.4 finish.1
  (52 shorter events, 13.2 us)
Async XLA Ops:
  0.0 17.3 %copy-start.15 = (f32[2,1024]{1,0:T(2,128)S(1)}, f32[2,1024]{1,0:T(2,128)}, u32[]{:S(2)}) copy-start(f32[2,1024]{1,0:T(2,128)} %param.9) | copy-start | bytes 24580
  0.0 17.3 %copy-start.16 = (s32[2]{0:T(128)S(1)}, s32[2]{0:T(128)}, u32[]{:S(2)}) copy-start(s32[2]{0:T(128)} %param.11) | copy-start | bytes 28
  4.0 13.4 %copy-start = (bf16[2,256,1024]{2,1,0:T(8,128)(2,1)S(1)}, bf16[2,256,1024]{2,1,0:T(8,128)(2,1)}, u32[]{:S(2)}) copy-start(bf16[2,256,1024]{2,1,0:T(8,128)(2,1)} %eta_ref.3) | copy-start | bytes 3145732
  4.0 13.4 %copy-start.1 = (bf16[2,256,1024]{2,1,0:T(8,128)(2,1)S(1)}, bf16[2,256,1024]{2,1,0:T(8,128)(2,1)}, u32[]{:S(2)}) copy-start(bf16[2,256,1024]{2,1,0:T(8,128)(2,1)} %gamma_ref.3) | copy-start | bytes 3145732
  4.0 41.3 %all-to-all-start = ((bf16[64,64,128]{2,1,0:T(8,128)(2,1)}), bf16[64,64,128]{2,1,0:T(8,128)(2,1)S(1)}, u32[]{:S(2)}, u32[]{:S(2)}) async-start(bf16[64,64,128]{2,1,0:T(8,128)(2,1)} %pack.1), calls=%async_computation | async-start | bytes 2097152 | tf_op jit(solution)/shard_map/all_to_all | solution.py:350
  17.4 7.3 %copy-start.10 = (bf16[128,128]{1,0:T(8,128)(2,1)S(1)}, bf16[128,128]{1,0:T(8,128)(2,1)}, u32[]{:S(2)}) copy-start(bf16[128,128]{1,0:T(8,128)(2,1)} %forward_ref.1) | copy-start | bytes 98308
  17.4 7.3 %copy-start.11 = (bf16[128,128]{1,0:T(8,128)(2,1)S(1)}, bf16[128,128]{1,0:T(8,128)(2,1)}, u32[]{:S(2)}) copy-start(bf16[128,128]{1,0:T(8,128)(2,1)} %back_ref.1) | copy-start | bytes 98308
  17.4 7.3 %copy-start.12 = (f32[2,1024]{1,0:T(2,128)S(1)}, f32[2,1024]{1,0:T(2,128)}, u32[]{:S(2)}) copy-start(f32[2,1024]{1,0:T(2,128)} %weight_ref.3) | copy-start | bytes 24580
  22.1 17.1 %collective-permute-start = (bf16[2,5,2,128,128]{4,3,2,1,0:T(8,128)(2,1)S(1)}, bf16[2,5,2,128,128]{4,3,2,1,0:T(8,128)(2,1)S(1)}, u32[]{:S(2)}, u32[]{:S(2)}) collective-permute-start(bf16[2,5,2,128,128]{4,3,2,1,0:T(8,128)(2,1)S(1)} %get-tuple-element.33), channel_id=1, source_target_pairs={{0,1},{1,2},{2,3},{3,0},{4,5},{5,6},{6,7},{7,4},{8,9},{9,10},{10,1... | collective-permute-start | bytes 1966088 | tf_op jit(solution)/shard_map/ppermute | solution.py:354
  23.3 16.7 %collective-permute-start.1 = (bf16[2,5,2,128,128]{4,3,2,1,0:T(8,128)(2,1)S(1)}, bf16[2,5,2,128,128]{4,3,2,1,0:T(8,128)(2,1)S(1)}, u32[]{:S(2)}, u32[]{:S(2)}) collective-permute-start(bf16[2,5,2,128,128]{4,3,2,1,0:T(8,128)(2,1)S(1)} %get-tuple-element.34), channel_id=1, source_target_pairs={{0,3},{1,0},{2,1},{3,2},{4,7},{5,4},{6,5},{7,6},{8,11},{9,8},{10,9... | collective-permute-start | bytes 1966088 | tf_op jit(solution)/shard_map/ppermute | solution.py:354
  47.0 6.9 %copy-start.9 = (bf16[2,5,2,128,128]{4,3,2,1,0:T(8,128)(2,1)S(1)}, bf16[2,5,2,128,128]{4,3,2,1,0:T(8,128)(2,1)}, u32[]{:S(2)}) copy-start(bf16[2,5,2,128,128]{4,3,2,1,0:T(8,128)(2,1)} %copy-done.8) | copy-start | bytes 1966084
  47.0 24.4 %copy-start.3 = (bf16[2,5,2,128,128]{4,3,2,1,0:T(8,128)(2,1)S(1)}, bf16[2,5,2,128,128]{4,3,2,1,0:T(8,128)(2,1)}, u32[]{:S(2)}) copy-start(bf16[2,5,2,128,128]{4,3,2,1,0:T(8,128)(2,1)} %copy-done.2) | copy-start | bytes 1966084
  47.0 34.9 %all-to-all-start.1 = ((bf16[64,64,128]{2,1,0:T(8,128)(2,1)}), bf16[64,64,128]{2,1,0:T(8,128)(2,1)S(1)}, u32[]{:S(2)}, u32[]{:S(2)}) async-start(bf16[64,64,128]{2,1,0:T(8,128)(2,1)} %recouple.1), calls=%async_computation.1 | async-start | bytes 2097152 | tf_op jit(solution)/shard_map/all_to_all | solution.py:350
  53.9 17.4 %collective-permute-start.2 = (bf16[2,5,2,128,128]{4,3,2,1,0:T(8,128)(2,1)S(1)}, bf16[2,5,2,128,128]{4,3,2,1,0:T(8,128)(2,1)S(1)}, u32[]{:S(2)}, u32[]{:S(2)}) collective-permute-start(bf16[2,5,2,128,128]{4,3,2,1,0:T(8,128)(2,1)S(1)} %copy-done.9), channel_id=1, source_target_pairs={{0,2},{1,3},{2,0},{3,1},{4,6},{5,7},{6,4},{7,5},{8,10},{9,11},{10,... | collective-permute-start | bytes 1966088 | tf_op jit(solution)/shard_map/ppermute | solution.py:354
  82.0 19.7 %collective-permute-start.3 = (bf16[2,2,2,2,128,128]{5,4,3,2,1,0:T(8,128)(2,1)S(1)}, bf16[2,2,2,2,128,128]{5,4,3,2,1,0:T(8,128)(2,1)S(1)}, u32[]{:S(2)}, u32[]{:S(2)}) collective-permute-start(bf16[2,2,2,2,128,128]{5,4,3,2,1,0:T(8,128)(2,1)S(1)} %get-tuple-element.41), channel_id=1, source_target_pairs={{0,1},{1,2},{2,3},{3,0},{4,5},{5,6},{6,7},{7,4},{8,9},{9,10},{10,1... | collective-permute-start | bytes 1572872 | tf_op jit(solution)/shard_map/ppermute | solution.py:354
  83.0 18.7 %collective-permute-start.4 = (bf16[2,2,2,2,128,128]{5,4,3,2,1,0:T(8,128)(2,1)S(1)}, bf16[2,2,2,2,128,128]{5,4,3,2,1,0:T(8,128)(2,1)S(1)}, u32[]{:S(2)}, u32[]{:S(2)}) collective-permute-start(bf16[2,2,2,2,128,128]{5,4,3,2,1,0:T(8,128)(2,1)S(1)} %get-tuple-element.42), channel_id=1, source_target_pairs={{0,3},{1,0},{2,1},{3,2},{4,7},{5,4},{6,5},{7,6},{8,11},{9,8},{10,9... | collective-permute-start | bytes 1572872 | tf_op jit(solution)/shard_map/ppermute | solution.py:354
  84.8 16.9 %collective-permute-start.5 = (bf16[2,2,2,128,128]{4,3,2,1,0:T(8,128)(2,1)S(1)}, bf16[2,2,2,128,128]{4,3,2,1,0:T(8,128)(2,1)S(1)}, u32[]{:S(2)}, u32[]{:S(2)}) collective-permute-start(bf16[2,2,2,128,128]{4,3,2,1,0:T(8,128)(2,1)S(1)} %get-tuple-element.43), channel_id=1, source_target_pairs={{0,2},{1,3},{2,0},{3,1},{4,6},{5,7},{6,4},{7,5},{8,10},{9,11},{10,... | collective-permute-start | bytes 786440 | tf_op jit(solution)/shard_map/ppermute | solution.py:354
  101.7 1.2 copy-start.14
  105.5 11.0 %collective-permute-start.6 = (bf16[2,5,128,128]{3,2,1,0:T(8,128)(2,1)S(1)}, bf16[2,5,128,128]{3,2,1,0:T(8,128)(2,1)S(1)}, u32[]{:S(2)}, u32[]{:S(2)}) collective-permute-start(bf16[2,5,128,128]{3,2,1,0:T(8,128)(2,1)S(1)} %get-tuple-element.46), channel_id=1, source_target_pairs={{0,1},{1,2},{2,3},{3,0},{4,5},{5,6},{6,7},{7,4},{8,9},{9,10},{10,1... | collective-permute-start | bytes 983048 | tf_op jit(solution)/shard_map/ppermute | solution.py:354
  106.1 10.4 %collective-permute-start.8 = (bf16[2,5,128,128]{3,2,1,0:T(8,128)(2,1)S(1)}, bf16[2,5,128,128]{3,2,1,0:T(8,128)(2,1)S(1)}, u32[]{:S(2)}, u32[]{:S(2)}) collective-permute-start(bf16[2,5,128,128]{3,2,1,0:T(8,128)(2,1)S(1)} %get-tuple-element.48), channel_id=1, source_target_pairs={{0,3},{1,0},{2,1},{3,2},{4,7},{5,4},{6,5},{7,6},{8,11},{9,8},{10,9... | collective-permute-start | bytes 983048 | tf_op jit(solution)/shard_map/ppermute | solution.py:354
  108.2 8.3 %collective-permute-start.7 = (bf16[2,3,128,128]{3,2,1,0:T(8,128)(2,1)S(1)}, bf16[2,3,128,128]{3,2,1,0:T(8,128)(2,1)S(1)}, u32[]{:S(2)}, u32[]{:S(2)}) collective-permute-start(bf16[2,3,128,128]{3,2,1,0:T(8,128)(2,1)S(1)} %get-tuple-element.47), channel_id=1, source_target_pairs={{0,2},{1,3},{2,0},{3,1},{4,6},{5,7},{6,4},{7,5},{8,10},{9,11},{10,... | collective-permute-start | bytes 589832 | tf_op jit(solution)/shard_map/ppermute | solution.py:354
  176.3 8.1 %collective-permute-start.9 = (bf16[4,128,128]{2,1,0:T(8,128)(2,1)S(1)}, bf16[4,128,128]{2,1,0:T(8,128)(2,1)S(1)}, u32[]{:S(2)}, u32[]{:S(2)}) collective-permute-start(bf16[4,128,128]{2,1,0:T(8,128)(2,1)S(1)} %get-tuple-element.50), channel_id=1, source_target_pairs={{0,1},{1,2},{2,3},{3,0},{4,5},{5,6},{6,7},{7,4},{8,9},{9,10},{10,1... | collective-permute-start | bytes 393224 | tf_op jit(solution)/shard_map/ppermute | solution.py:354
  177.0 7.5 %collective-permute-start.10 = (bf16[4,128,128]{2,1,0:T(8,128)(2,1)S(1)}, bf16[4,128,128]{2,1,0:T(8,128)(2,1)S(1)}, u32[]{:S(2)}, u32[]{:S(2)}) collective-permute-start(bf16[4,128,128]{2,1,0:T(8,128)(2,1)S(1)} %get-tuple-element.51), channel_id=1, source_target_pairs={{0,3},{1,0},{2,1},{3,2},{4,7},{5,4},{6,5},{7,6},{8,11},{9,8},{10,9... | collective-permute-start | bytes 393224 | tf_op jit(solution)/shard_map/ppermute | solution.py:354
  179.1 5.3 %collective-permute-start.11 = (bf16[2,128,128]{2,1,0:T(8,128)(2,1)S(1)}, bf16[2,128,128]{2,1,0:T(8,128)(2,1)S(1)}, u32[]{:S(2)}, u32[]{:S(2)}) collective-permute-start(bf16[2,128,128]{2,1,0:T(8,128)(2,1)S(1)} %get-tuple-element.52), channel_id=1, source_target_pairs={{0,2},{1,3},{2,0},{3,1},{4,6},{5,7},{6,4},{7,5},{8,10},{9,11},{10,... | collective-permute-start | bytes 196616 | tf_op jit(solution)/shard_map/ppermute | solution.py:354
  (7 other events, 6.5 us)

commit v5 on v4

--- a/solution.py
+++ b/solution.py
@@ -46,12 +46,14 @@
     return [jnp.concatenate([both[0][:, r : r + 4], both[1][:, r : r + 4]], axis=1) for r in (0, 4)]
 
 
+SOURCE = ((2, 0, 0, 0, 3, 0, 1, 1), (1, 2, 0, 0, 1, 3, 1, 1))
+
+
 def pack_kernel(eta_ref, gamma_ref, out_ref, held, sems):
     panel = lax.axis_index("panel")
     either = jnp.where(panel < 2, 0, 1)
     row = lax.broadcasted_iota(jnp.int32, (128, LANES), 0)
     column = lax.broadcasted_iota(jnp.int32, (128, LANES), 1)
-    source = (("both", 0, 0, 0, either, 0, 1, 1), (1, "both", 0, 0, 1, either, 1, 1))
     copies = {}
     for l in range(2):
         for ch in range(2):
@@ -65,8 +67,8 @@
         def read(arr):
             return held[arr, ch, l * 128 : (l + 1) * 128, pl.ds(tile_at(panel, j, 0), LANES)]
 
-        kind = source[l][j]
-        value = jnp.where(row < column, read(0), read(1)) if kind == "both" else read(kind)
+        kind = SOURCE[l][j]
+        value = jnp.where(row < column, read(0), read(1)) if kind == 2 else read(either if kind == 3 else kind)
         return swap_blocks(value).astype(F32).reshape(16, 8, LANES)
 
     for l in range(2):
@@ -81,12 +83,7 @@
             out_ref[start : start + 16] = jnp.concatenate(pieces, axis=1).astype(BF16)
 
 
-def spread_kernel(forward_ref, back_ref, weight_ref, forward_out, back_out, rows_out):
-    panel = lax.axis_index("panel")
-    for ch in range(2):
-        for j in range(8):
-            lane = weight_ref[ch : ch + 1, pl.ds(tile_at(panel, j, 0), LANES)]
-            rows_out[ch, j] = jnp.broadcast_to(lane, (128, LANES)).T
+def spread_kernel(forward_ref, back_ref, forward_out, back_out):
     for ref, out in ((forward_ref, forward_out), (back_ref, back_out)):
         shift = 2
         size = 128 << shift
@@ -116,144 +113,106 @@
         out_ref[:, ch * 32 : ch * 32 + 32] = jnp.concatenate(rows, axis=1).astype(BF16)
 
 
-def tile_of(ref, ch, l, j):
-    start = j // 4 * 32 + l * 16
-    return ref[start : start + 16].astype(F32)[:, ch * 32 + j % 4 * 8 : ch * 32 + j % 4 * 8 + 8].reshape(128, LANES)
-
-
 PLUS = ((1, 1), (0, 3))
 MINUS = ((0, 2), (1, 2))
 FAR = ((1, 3),)
 
 
-def mirror_kernel(in_ref, plus_ref, minus_ref, far_ref):
-    for ch in range(2):
-        for l in range(2):
-            for k in range(2):
-                plus_ref[ch, 0, l, k] = tile_of(in_ref, ch, l, 2 + k).astype(BF16)
-                minus_ref[ch, 0, l, k] = tile_of(in_ref, ch, l, 6 + k).astype(BF16)
-                across = tile_of(in_ref, ch, l, 4 + k).astype(BF16)
-                plus_ref[ch, 1, l, k] = across
-                minus_ref[ch, 1, l, k] = across
-                far_ref[ch, l, k] = across
-
-
-def product_kernel(in_ref, plus_ref, minus_ref, far_ref, weight_ref, rows_ref, *refs):
-    for ch in range(2):
-        product_channel(ch, in_ref, plus_ref, minus_ref, far_ref, weight_ref, rows_ref, *refs)
-
-
-def product_channel(
-    ch, in_ref, plus_ref, minus_ref, far_ref, weight_ref, rows_ref, own_ref, plus_out, far_out, minus_out, by_lane, by_row, plain, edge_lane, edge_row, edge_plain
-):
-    own_ref, plus_out, far_out, minus_out, by_lane, by_row, plain, edge_lane, edge_row, edge_plain = (
-        ref.at[ch] for ref in (own_ref, plus_out, far_out, minus_out, by_lane, by_row, plain, edge_lane, edge_row, edge_plain)
-    )
+def place():
+    return lax.rem(lax.axis_index("panel") + 4 - lax.rem(lax.axis_index("chan"), 2), 4)
+
+
+def send_kernel(in_ref, plus_ref, minus_ref, far_ref):
+    here = place()
+
+    def rows(ch):
+        return in_ref[:, pl.ds(pl.multiple_of(ch * 32, 32), 32), :]
+
+    plus_ref[...] = rows(jnp.where(here == 1, 1, 0))
+    minus_ref[...] = rows(jnp.where(here == 1, 0, 1))
+    far_ref[...] = rows(jnp.where(here == 0, 1, 0))
+
+
+def tile_of(ref, l, j, first=0):
+    start = j // 4 * 32 + l * 16
+    return ref[start : start + 16, pl.ds(first, 32), :].astype(F32)[:, j % 4 * 8 : j % 4 * 8 + 8].reshape(128, LANES)
+
+
+def product_kernel(in_ref, plus_ref, minus_ref, far_ref, weight_ref, own_out, plus_out, far_out, minus_out, scaled, plain, forward):
     panel = lax.axis_index("panel")
-    lanes = [weight_ref[ch : ch + 1, pl.ds(tile_at(panel, j, 0), LANES)] for j in range(4)]
-    rows = [rows_ref[ch, j] for j in range(8)]
-
-    def held(l, j):
-        return tile_of(in_ref, ch, l, j)
-
-    def plus(part, i, k):
-        return plus_ref[ch, part, i, k].astype(F32)
-
-    def minus(part, i, k):
-        return minus_ref[ch, part, i, k].astype(F32)
-
-    def far(i, k):
-        return far_ref[ch, i, k].astype(F32)
-
-    def put(j, l, eta, gamma):
-        place = (slice(j * 128, (j + 1) * 128), slice(l * LANES, (l + 1) * LANES))
-        by_lane[place] = (eta * lanes[l]).astype(BF16)
-        by_row[place] = (eta * rows[j]).astype(BF16)
-        plain[place] = gamma.astype(BF16)
-
-    def put_edge(i, k, eta, gamma):
-        place = (slice(i * 128, (i + 1) * 128), slice(k * LANES, (k + 1) * LANES))
-        edge_lane[place] = (eta * lanes[2 + k]).astype(BF16)
-        edge_row[place] = (eta * rows[6 + i]).astype(BF16)
-        edge_plain[place] = gamma.astype(BF16)
+    own = jnp.where(place() == 2, 1, 0)
+
+    def tile(r, c):
+        b, l = divmod(r, 2)
+        j = (c - 2 * b) % 8
+        if b == 0:
+            return tile_of(in_ref, l, j, pl.multiple_of(own * 32, 32))
+        return tile_of((minus_ref, far_ref, plus_ref)[b - 1], l, j)
+
+    lanes = []
+    for j in range(8):
+        columns = pl.ds(tile_at(panel, j, 0), LANES)
+        lanes.append(jnp.where(own == 0, weight_ref[0:1, columns], weight_ref[1:2, columns]))
+
+    def put(ref, r, c, value):
+        if ref is scaled:
+            value = value * lanes[c]
+        ref[r * 128 : (r + 1) * 128, c * LANES : (c + 1) * LANES] = value.astype(BF16)
 
     row = lax.broadcasted_iota(jnp.int32, (128, LANES), 0)
     column = lax.broadcasted_iota(jnp.int32, (128, LANES), 1)
     row_block, column_block = row >> 5, column >> 5
     first = (row_block > column_block) | ((row_block == column_block) & (row < column))
-    for l in range(2):
-        value = held(l, l)
+    for r in range(8):
+        value = tile(r, r)
         mirrored = value.T
-        put(l, l, jnp.where(row == column, F32(0.0), jnp.where(first, -value, mirrored)), jnp.where(first, mirrored, value))
-        for k in range(2):
-            put(2 + k, l, -held(l, 2 + k), minus(0, k, l).T)
-            put(6 + k, l, plus(0, k, l).T, held(l, 6 + k))
-        value, mirrored = held(l, 4 + l), far(l, l).T
-        put(4 + l, l, jnp.where(panel < 2, -value, mirrored), jnp.where(panel < 2, mirrored, value))
-        straight, mirrored = minus(1, l, l), plus(1, l, l).T
-        before = lax.rem(panel + 3, 4) < 2
-        put_edge(l, l, jnp.where(before, mirrored, -straight), jnp.where(before, straight, mirrored))
-    put(1, 0, -held(0, 1), held(1, 0).T)
-    put(0, 1, held(0, 1).T, held(1, 0))
-    put(5, 0, -held(0, 5), far(1, 0).T)
-    put(4, 1, far(0, 1).T, held(1, 4))
-    put_edge(0, 1, plus(1, 0, 1).T, minus(1, 1, 0))
-    put_edge(1, 0, -minus(1, 0, 1), plus(1, 1, 0).T)
-
-    def block(ref, j):
-        return ref[j * 256 : (j + 1) * 256]
-
-    def inner(i, j):
-        return contract_last(block(by_lane, i), block(plain, j)) + contract_last(block(plain, i), block(by_lane, j))
-
-    def tile(value, i, j):
-        return value[i * 128 : (i + 1) * 128, j * 128 : (j + 1) * 128]
-
-    diagonal = contract_first(by_row[...], plain[...]) + contract_first(plain[...], by_row[...])
-    for (l, t), (i, j) in (((0, 0), (0, 0)), ((0, 1), (0, 1)), ((1, 0), (1, 1))):
-        own_ref[l, t] = -tile(diagonal, i, j)
-    ahead = inner(0, 1) - contract_first(block(by_row, 3), edge_plain[...]) - contract_first(block(plain, 3), edge_row[...])
-    own_ref[0, 3] = tile(ahead, 0, 1)
-    own_ref[1, 1] = tile(ahead, 1, 0)
-    plus_out[0] = tile(ahead, 0, 0).astype(BF16)
-    plus_out[1] = tile(ahead, 1, 1).astype(BF16)
-    behind = inner(3, 0)
-    behind += jnp.dot(edge_lane[...], block(plain, 1), preferred_element_type=F32)
-    behind -= jnp.dot(edge_plain[...], block(by_row, 1), preferred_element_type=F32)
-    own_ref[0, 2] = tile(behind, 0, 0)
-    own_ref[1, 2] = tile(behind, 1, 1)
-    minus_out[0] = tile(behind, 0, 1).astype(BF16)
-    minus_out[1] = tile(behind, 1, 0).astype(BF16)
-    across = inner(0, 2)
-    for (l, t), (i, j) in ACROSS:
-        own_ref[l, t] = tile(across, i, j)
-    for ref, start, value in ((far_out, 0, inner(2, 0)), (minus_out, 2, inner(3, 1)), (plus_out, 2, inner(1, 3))):
-        for u, (held, (i, j)) in enumerate(ACROSS):
-            ref[start + u] = tile(value, i, j).astype(BF16)
-
-
-ACROSS = (((0, 4), (0, 0)), ((1, 3), (1, 0)), ((1, 4), (1, 1)))
-
-
-def total(own_ref, plus_ref, far_ref, minus_ref, l, t):
-    value = own_ref[l, t]
-    if t == 2:
-        return (value + plus_ref[l].astype(F32)).T
-    if (l, t) in ((0, 3), (1, 1)):
-        return value + minus_ref[l].astype(F32)
-    for u, (held, _) in enumerate(ACROSS):
-        if held == (l, t):
-            near = plus_ref[2 + u].astype(F32) + minus_ref[2 + u].astype(F32)
-            return value + far_ref[u].astype(F32) + near
-    return value
-
-
-def sum_kernel(own_ref, plus_ref, far_ref, minus_ref, out_ref):
-    refs = (own_ref, plus_ref, far_ref, minus_ref)
+        put(scaled, r, r, jnp.where(row == column, F32(0.0), jnp.where(first, -value, mirrored)))
+        put(plain, r, r, jnp.where(first, mirrored, value))
+    for r in range(8):
+        for step in (1, 2, 3, 4):
+            c = (r + step) % 8
+            if step == 4:
+                if r >= 4:
+                    continue
+                one, other = tile(r, c), tile(c, r)
+                is_eta = lax.rem(panel + r // 2, 4) < 2
+                one_t, other_t = one.T, other.T
+                put(scaled, r, c, jnp.where(is_eta, one_t, -other))
+                put(scaled, c, r, jnp.where(is_eta, -one, other_t))
+                put(plain, r, c, jnp.where(is_eta, other, one_t))
+                put(plain, c, r, jnp.where(is_eta, other_t, one))
+                continue
+            p, q = (r, c) if SOURCE[r % 2][(c - r // 2 * 2) % 8] == 0 else (c, r)
+            value = tile(p, q)
+            put(scaled, q, p, -value)
+            put(scaled, p, q, value.T)
+            value = tile(q, p)
+            put(plain, p, q, value)
+            put(plain, q, p, value.T)
+    for b in range(4):
+        forward[b * 256 : (b + 1) * 256, :] = contract_last(scaled[b * 256 : (b + 1) * 256], plain[...])
+    for b, ref in enumerate((own_out, plus_out, far_out, minus_out)):
+        for l in range(2):
+            for t, offset in enumerate(OFFSETS):
+                r, c = 2 * b + l, (2 * b + l + offset) % 8
+                value = forward[r * 128 : (r + 1) * 128, c * LANES : (c + 1) * LANES]
+                other = forward[c * 128 : (c + 1) * 128, r * LANES : (r + 1) * LANES]
+                ref[l, t] = (value + other.T).astype(BF16)
+
+
+def part_kernel(own_ref, plus_ref, far_ref, minus_ref, out_ref):
+    here = place()
+
+    def pick(l, t, refs):
+        value = refs[0][l, t]
+        for k in range(1, 4):
+            value = jnp.where(here == k, refs[k][l, t], value)
+        return swap_blocks(value).astype(F32).reshape(16, 8, LANES)
+
     for l in range(2):
         low, high = [], []
         for t in range(5):
-            pieces = interleave([swap_blocks(total(*(ref.at[ch] for ref in refs), l, t)).reshape(16, 8, LANES) for ch in range(2)])
+            pieces = interleave([pick(l, t, (own_ref, plus_ref, far_ref, minus_ref)), pick(l, t, (far_ref, minus_ref, own_ref, plus_ref))])
             low.append(pieces[0])
             high.append(pieces[1])
         out_ref[l * 32 : l * 32 + 16] = jnp.concatenate(low, axis=1).astype(BF16)
@@ -358,6 +317,23 @@
     return step(plus, 1), step(minus, 3), step(far, 2)
 
 
+def route(value, by, places):
+    pairs = []
+    for chan in range(64):
+        for here in places:
+            panel = (here + chan % 2) % 4
+            pairs.append((chan * 4 + panel, chan * 4 + (panel + by) % 4))
+    return lax.ppermute(value, ("chan", "panel"), pairs)
+
+
+def to_owner(plus, minus, far):
+    return route(plus, 1, (1, 3)), route(minus, 3, (1, 3)), route(far, 2, (0, 2))
+
+
+def from_owner(plus, far, minus):
+    return route(plus, 1, (0, 2)), route(far, 2, (0, 2)), route(minus, 3, (0, 2))
+
+
 def shards(eta, gamma, pp_weight, cc_weight, live_pairs, forward_table, back_table):
     positions = lax.broadcasted_iota(jnp.int32, pp_weight.shape, 1)
     weight_pp = jnp.where(positions < live_pairs[:, None], pp_weight, F32(0.0))
@@ -369,14 +345,7 @@
         name="pack",
         space=pltpu.HBM,
     )
-    forward_wide, back_wide, weight_rows = call(
-        spread_kernel,
-        [(512, 512), (512, 512), (2, 8, 128, LANES)],
-        (forward_table, back_table, cc_weight),
-        flops=300_000_000,
-        name="spread",
-        dtype=[BF16, BF16, F32],
-    )
+    forward_wide, back_wide = call(spread_kernel, [(512, 512)] * 2, (forward_table, back_table), flops=300_000_000, name="spread")
     packed = exchange(packed, "chan")
     pp_own, *pp = call(
         pair_kernel,
@@ -393,19 +362,18 @@
     pp_far = step(pp_far, 2)
     pp_part = call(pair_sum_kernel, (2, 5, 2, 128, LANES), (pp_own, pp_plus, pp_far, pp_minus), name="pair_sum", dtype=F32)
     mixed, pp_part = lax.optimization_barrier((mixed, pp_part))
-    sends = call(mirror_kernel, [(2, 2, 2, 2, 128, LANES), (2, 2, 2, 2, 128, LANES), (2, 2, 2, 128, LANES)], (mixed,), name="mirror")
-    received = mirror(*sends)
-    own, *partial = call(
+    sends = call(send_kernel, [(64, 32, LANES)] * 3, (mixed,), name="send")
+    received = to_owner(*sends)
+    own, *outs = call(
         product_kernel,
-        [(2, 2, 5, 128, LANES), (2, 5, 128, LANES), (2, 3, 128, LANES), (2, 5, 128, LANES)],
-        (mixed, *received, cc_weight, weight_rows),
-        flops=1_400_000_000,
-        scratch=[pltpu.VMEM((2, 1024, 256), BF16)] * 3 + [pltpu.VMEM((2, 256, 256), BF16)] * 3,
+        [(2, 5, 128, LANES)] * 4,
+        (mixed, *received, cc_weight),
+        flops=2_200_000_000,
+        scratch=[pltpu.VMEM((1024, 1024), BF16)] * 2 + [pltpu.VMEM((1024, 1024), F32)],
         name="product",
-        dtype=[F32, BF16, BF16, BF16],
     )
-    plus, minus, far = mirror(partial[0], partial[2], partial[1])
-    part = call(sum_kernel, (64, 40, LANES), (own, plus, far, minus), name="sum")
+    outs = from_owner(*outs)
+    part = call(part_kernel, (64, 40, LANES), (own, *outs), name="part")
     part = exchange(part, "chan")
     part = call(recouple_back_kernel, (64, 40, LANES), (back_wide, part), flops=400_000_000, name="recouple_back")
     part = exchange(part, "chan")

time: 186 us -> 182 us (0.978)
  blocking collectives: 57.5 us -> 51.2 us
  starting transfers between devices: 36.1 us -> 39.4 us
  local copies, waits for them, and re-layouts: 7.76 us -> 4.76 us
    ppermute x0 -> x6, waiting for transfers between devices: none -> 23.9 us  [route(): return lax.ppermute(value, ('chan', 'panel'), pairs)]
    ppermute x12 -> x6, waiting for transfers between devices: 55.7 us -> 32.5 us  [step(): return lax.ppermute(value, 'panel', [(i, (i + by) % 4) for i in range(4)])]
    ppermute x0 -> x6, starting transfers between devices: none -> 9.84 us  [route(): return lax.ppermute(value, ('chan', 'panel'), pairs)]
    all_to_all x2, blocking collectives: 57.5 us -> 51.2 us  [exchange(): lax.all_to_all(operand, axis, split_axis=0, concat_axis=0, tiled=True)]
    ppermute x12 -> x6, starting transfers between devices: 15.9 us -> 9.69 us  [step(): return lax.ppermute(value, 'panel', [(i, (i + by) % 4) for i in range(4)])]
    unnamed x34 -> x30, local copies, waits for them, and re-layouts: 7.76 us -> 4.76 us
  transfers between devices with their start and end apart: 14 -> 14, of which waited for: 7 -> 9; matrix products, arithmetic and copies ran while one was open for 0% -> 0% of each run, Pallas kernels for 2% -> 2%
where the time goes in v5:
time: 182 us
  waiting for transfers between devices  69.8 us (38%)
  blocking collectives  51.2 us (28%)
  starting transfers between devices  39.4 us (22%)
  Pallas kernels  16.2 us (9%)
  local copies, waits for them, and re-layouts  4.76 us (3%)
    all_to_all x2, blocking collectives, exchange(): lax.all_to_all(operand, axis, split_axis=0, concat_axis=0, tiled=True)  51.2 us
    ppermute x6, waiting for transfers between devices, step(): return lax.ppermute(value, 'panel', [(i, (i + by) % 4) for i in range(4)])  32.5 us
    ppermute x6, waiting for transfers between devices, route(): return lax.ppermute(value, ('chan', 'panel'), pairs)  23.9 us
    all_to_all x2, starting transfers between devices, exchange(): lax.all_to_all(operand, axis, split_axis=0, concat_axis=0, tiled=True)  19.9 us
    pallas_call x11, Pallas kernels, call(): pl.pallas_call(kernel, out_shape=shaped[0] if single else shaped, in_spec...  16.2 us
    all_to_all x2, waiting for transfers between devices, exchange(): lax.all_to_all(operand, axis, split_axis=0, concat_axis=0, tiled=True)  13.4 us
    ppermute x6, starting transfers between devices, route(): return lax.ppermute(value, ('chan', 'panel'), pairs)  9.84 us
    ppermute x6, starting transfers between devices, step(): return lax.ppermute(value, 'panel', [(i, (i + by) % 4) for i in range(4)])  9.69 us
  transfers between devices with their start and end apart: 14, of which 9 were waited for; matrix products, arithmetic and copies ran while one was open for 0% of the time, Pallas kernels for 2%

profile of v5, /device:TPU:1, one launch (start us, length us, event | category | flops | bytes accessed | tf_op | source)
XLA Modules:
  0.0 181.7 jit_solution(6892294690916386136)
XLA Ops:
  0.0 4.0 %pack.1 = bf16[64,64,128]{2,1,0:T(8,128)(2,1)} custom-call(bf16[2,256,1024]{2,1,0:T(8,128)(2,1)} %eta_ref.3, bf16[2,256,1024]{2,1,0:T(8,128)(2,1)} %gamma_ref.3), custom_call_target="tpu_custom_call" | custom-call | bytes 3145728 | tf_op jit(solution)/shard_map/pack/pallas_call | solution.py:297
  4.0 13.3 %all-to-all-start = ((bf16[64,64,128]{2,1,0:T(8,128)(2,1)}), bf16[64,64,128]{2,1,0:T(8,128)(2,1)S(1)}, u32[]{:S(2)}, u32[]{:S(2)}) async-start(bf16[64,64,128]{2,1,0:T(8,128)(2,1)} %pack.1), calls=%async_computation | async-start | bytes 2097152 | tf_op jit(solution)/shard_map/all_to_all | solution.py:309
  17.4 2.9 %pair.1 = (bf16[2,5,2,128,128]{4,3,2,1,0:T(8,128)(2,1)S(1)}, bf16[2,5,2,128,128]{4,3,2,1,0:T(8,128)(2,1)S(1)}, bf16[2,5,2,128,128]{4,3,2,1,0:T(8,128)(2,1)S(1)}, bf16[2,5,2,128,128]{4,3,2,1,0:T(8,128)(2,1)S(1)}) custom-call(bf16[2,256,1024]{2,1,0:T(8,128)(2,1)S(1)} %copy-done, bf16[2,256,1024]{2,1,0:T(8,128)(2,1)S(1)} %copy-done.1, ...), custom_call_target="tpu_custom_call" | custom-call | flops 2200000000 | bytes 4726784 | tf_op jit(solution)/shard_map/pair/pallas_call | solution.py:297
  22.4 1.5 collective-permute-start.1
  24.6 13.7 %collective-permute-done.plus_ref = bf16[2,5,2,128,128]{4,3,2,1,0:T(8,128)(2,1)S(1)} collective-permute-done((bf16[2,5,2,128,128]{4,3,2,1,0:T(8,128)(2,1)S(1)}, bf16[2,5,2,128,128]{4,3,2,1,0:T(8,128)(2,1)S(1)}, u32[]{:S(2)}, u32[]{:S(2)}) %collective-permute-start) | collective-permute-done | bytes 655392 | tf_op jit(solution)/shard_map/ppermute | solution.py:313
  40.0 5.3 %all-to-all-done.in_ref = bf16[64,64,128]{2,1,0:T(8,128)(2,1)S(1)} async-done(((bf16[64,64,128]{2,1,0:T(8,128)(2,1)}), bf16[64,64,128]{2,1,0:T(8,128)(2,1)S(1)}, u32[]{:S(2)}, u32[]{:S(2)}) %all-to-all-start) | async-done | bytes 1048608 | tf_op jit(solution)/shard_map/all_to_all | solution.py:309
  45.3 1.7 recouple.1
  47.0 6.6 %all-to-all-start.1 = ((bf16[64,64,128]{2,1,0:T(8,128)(2,1)}), bf16[64,64,128]{2,1,0:T(8,128)(2,1)S(1)}, u32[]{:S(2)}, u32[]{:S(2)}) async-start(bf16[64,64,128]{2,1,0:T(8,128)(2,1)} %recouple.1), calls=%async_computation.1 | async-start | bytes 2097152 | tf_op jit(solution)/shard_map/all_to_all | solution.py:309
  53.6 2.8 %collective-permute-start.2 = (bf16[2,5,2,128,128]{4,3,2,1,0:T(8,128)(2,1)S(1)}, bf16[2,5,2,128,128]{4,3,2,1,0:T(8,128)(2,1)S(1)}, u32[]{:S(2)}, u32[]{:S(2)}) collective-permute-start(bf16[2,5,2,128,128]{4,3,2,1,0:T(8,128)(2,1)S(1)} %copy-done.9), channel_id=1, source_target_pairs={{0,2},{1,3},{2,0},{3,1},{4,6},{5,7},{6,4},{7,5},{8,10},{9,11},{10,... | collective-permute-start | bytes 1966088 | tf_op jit(solution)/shard_map/ppermute | solution.py:313
  56.4 14.6 %collective-permute-done.2.far_ref = bf16[2,5,2,128,128]{4,3,2,1,0:T(8,128)(2,1)S(1)} collective-permute-done((bf16[2,5,2,128,128]{4,3,2,1,0:T(8,128)(2,1)S(1)}, bf16[2,5,2,128,128]{4,3,2,1,0:T(8,128)(2,1)S(1)}, u32[]{:S(2)}, u32[]{:S(2)}) %collective-permute-start.2) | collective-permute-done | bytes 655392 | tf_op jit(solution)/shard_map/ppermute | solution.py:313
  73.5 8.1 %all-to-all-done.1.in_ref = bf16[64,64,128]{2,1,0:T(8,128)(2,1)S(1)} async-done(((bf16[64,64,128]{2,1,0:T(8,128)(2,1)}), bf16[64,64,128]{2,1,0:T(8,128)(2,1)S(1)}, u32[]{:S(2)}, u32[]{:S(2)}) %all-to-all-start.1) | async-done | bytes 1048608 | tf_op jit(solution)/shard_map/all_to_all | solution.py:309
  81.7 3.1 %collective-permute-start.3 = (bf16[64,32,128]{2,1,0:T(8,128)(2,1)S(1)}, bf16[64,32,128]{2,1,0:T(8,128)(2,1)S(1)}, u32[]{:S(2)}, u32[]{:S(2)}) collective-permute-start(bf16[64,32,128]{2,1,0:T(8,128)(2,1)S(1)} %get-tuple-element.40), channel_id=1, source_target_pairs={{1,2},{3,0},{6,7},{4,5},{9,10},{11,8},{14,15},{12,13},{17,18},{19,... | collective-permute-start | bytes 1572872 | tf_op jit(solution)/shard_map/ppermute | solution.py:326
  84.8 2.6 %collective-permute-start.4 = (bf16[64,32,128]{2,1,0:T(8,128)(2,1)S(1)}, bf16[64,32,128]{2,1,0:T(8,128)(2,1)S(1)}, u32[]{:S(2)}, u32[]{:S(2)}) collective-permute-start(bf16[64,32,128]{2,1,0:T(8,128)(2,1)S(1)} %get-tuple-element.41), channel_id=1, source_target_pairs={{1,0},{3,2},{6,5},{4,7},{9,8},{11,10},{14,13},{12,15},{17,16},{19,... | collective-permute-start | bytes 1572872 | tf_op jit(solution)/shard_map/ppermute | solution.py:326
  88.3 2.6 %collective-permute-done.3.plus_ref = bf16[64,32,128]{2,1,0:T(8,128)(2,1)S(1)} collective-permute-done((bf16[64,32,128]{2,1,0:T(8,128)(2,1)S(1)}, bf16[64,32,128]{2,1,0:T(8,128)(2,1)S(1)}, u32[]{:S(2)}, u32[]{:S(2)}) %collective-permute-start.3) | collective-permute-done | bytes 524320 | tf_op jit(solution)/shard_map/ppermute | solution.py:326
  90.9 6.4 %collective-permute-done.4.minus_ref = bf16[64,32,128]{2,1,0:T(8,128)(2,1)S(1)} collective-permute-done((bf16[64,32,128]{2,1,0:T(8,128)(2,1)S(1)}, bf16[64,32,128]{2,1,0:T(8,128)(2,1)S(1)}, u32[]{:S(2)}, u32[]{:S(2)}) %collective-permute-start.4) | collective-permute-done | bytes 524320 | tf_op jit(solution)/shard_map/ppermute | solution.py:326
  97.4 3.2 %product.1 = (bf16[2,5,128,128]{3,2,1,0:T(8,128)(2,1)S(1)}, bf16[2,5,128,128]{3,2,1,0:T(8,128)(2,1)S(1)}, bf16[2,5,128,128]{3,2,1,0:T(8,128)(2,1)S(1)}, bf16[2,5,128,128]{3,2,1,0:T(8,128)(2,1)S(1)}) custom-call(bf16[64,64,128]{2,1,0:T(8,128)(2,1)S(1)} %all-to-all-done.1.in_ref, bf16[64,32,128]{2,1,0:T(8,128)(2,1)S(1)} %collective-permute-done.3.plus_ref, ...), custom_call_target="tpu_custom_call" | custom-call | flops 2200000000 | bytes 3940352 | tf_op jit(solution)/shard_map/product/pallas_call | solution.py:297
  103.8 8.8 %collective-permute-done.6.plus_ref = bf16[2,5,128,128]{3,2,1,0:T(8,128)(2,1)S(1)} collective-permute-done((bf16[2,5,128,128]{3,2,1,0:T(8,128)(2,1)S(1)}, bf16[2,5,128,128]{3,2,1,0:T(8,128)(2,1)S(1)}, u32[]{:S(2)}, u32[]{:S(2)}) %collective-permute-start.6) | collective-permute-done | bytes 327712 | tf_op jit(solution)/shard_map/ppermute | solution.py:326
  112.7 6.1 %collective-permute-done.8.minus_ref = bf16[2,5,128,128]{3,2,1,0:T(8,128)(2,1)S(1)} collective-permute-done((bf16[2,5,128,128]{3,2,1,0:T(8,128)(2,1)S(1)}, bf16[2,5,128,128]{3,2,1,0:T(8,128)(2,1)S(1)}, u32[]{:S(2)}, u32[]{:S(2)}) %collective-permute-start.8) | collective-permute-done | bytes 327712 | tf_op jit(solution)/shard_map/ppermute | solution.py:326
  119.8 25.2 %all_to_all.20.in_ref = bf16[64,40,128]{2,1,0:T(8,128)(2,1)S(1)} all-to-all(bf16[64,40,128]{2,1,0:T(8,128)(2,1)S(1)} %part.1), channel_id=1, replica_groups=mesh['chan'=64,'panel'=4] {'chan'}, dimensions={0} | all-to-all | bytes 1310720 | tf_op jit(solution)/shard_map/all_to_all | solution.py:309
  145.6 26.0 %all_to_all.21.in_ref = bf16[64,40,128]{2,1,0:T(8,128)(2,1)S(1)} all-to-all(bf16[64,40,128]{2,1,0:T(8,128)(2,1)S(1)} %recouple_back.1), channel_id=1, replica_groups=mesh['chan'=64,'panel'=4] {'chan'}, dimensions={0} | all-to-all | bytes 1310720 | tf_op jit(solution)/shard_map/all_to_all | solution.py:309
  171.9 1.8 collective-permute-start.9
  173.7 1.3 collective-permute-start.10
  176.1 4.2 %collective-permute-done.11.far_ref = bf16[2,128,128]{2,1,0:T(8,128)(2,1)S(1)} collective-permute-done((bf16[2,128,128]{2,1,0:T(8,128)(2,1)S(1)}, bf16[2,128,128]{2,1,0:T(8,128)(2,1)S(1)}, u32[]{:S(2)}, u32[]{:S(2)}) %collective-permute-start.11) | collective-permute-done | bytes 65568 | tf_op jit(solution)/shard_map/ppermute | solution.py:313
  180.3 1.4 finish.1
  (48 shorter events, 14.3 us)
Async XLA Ops:
  0.0 17.3 %copy-start.13 = (f32[2,1024]{1,0:T(2,128)S(1)}, f32[2,1024]{1,0:T(2,128)}, u32[]{:S(2)}) copy-start(f32[2,1024]{1,0:T(2,128)} %param.9) | copy-start | bytes 24580
  0.0 17.3 %copy-start.14 = (s32[2]{0:T(128)S(1)}, s32[2]{0:T(128)}, u32[]{:S(2)}) copy-start(s32[2]{0:T(128)} %param.11) | copy-start | bytes 28
  4.0 13.4 %copy-start = (bf16[2,256,1024]{2,1,0:T(8,128)(2,1)S(1)}, bf16[2,256,1024]{2,1,0:T(8,128)(2,1)}, u32[]{:S(2)}) copy-start(bf16[2,256,1024]{2,1,0:T(8,128)(2,1)} %eta_ref.3) | copy-start | bytes 3145732
  4.0 13.4 %copy-start.1 = (bf16[2,256,1024]{2,1,0:T(8,128)(2,1)S(1)}, bf16[2,256,1024]{2,1,0:T(8,128)(2,1)}, u32[]{:S(2)}) copy-start(bf16[2,256,1024]{2,1,0:T(8,128)(2,1)} %gamma_ref.3) | copy-start | bytes 3145732
  4.0 41.3 %all-to-all-start = ((bf16[64,64,128]{2,1,0:T(8,128)(2,1)}), bf16[64,64,128]{2,1,0:T(8,128)(2,1)S(1)}, u32[]{:S(2)}, u32[]{:S(2)}) async-start(bf16[64,64,128]{2,1,0:T(8,128)(2,1)} %pack.1), calls=%async_computation | async-start | bytes 2097152 | tf_op jit(solution)/shard_map/all_to_all | solution.py:309
  17.4 6.5 %copy-start.10 = (bf16[128,128]{1,0:T(8,128)(2,1)S(1)}, bf16[128,128]{1,0:T(8,128)(2,1)}, u32[]{:S(2)}) copy-start(bf16[128,128]{1,0:T(8,128)(2,1)} %forward_ref.1) | copy-start | bytes 98308
  17.4 6.5 %copy-start.11 = (bf16[128,128]{1,0:T(8,128)(2,1)S(1)}, bf16[128,128]{1,0:T(8,128)(2,1)}, u32[]{:S(2)}) copy-start(bf16[128,128]{1,0:T(8,128)(2,1)} %back_ref.1) | copy-start | bytes 98308
  21.2 17.1 %copy-start.2 = (bf16[2,5,2,128,128]{4,3,2,1,0:T(8,128)(2,1)}, bf16[2,5,2,128,128]{4,3,2,1,0:T(8,128)(2,1)S(1)}, u32[]{:S(2)}) copy-start(bf16[2,5,2,128,128]{4,3,2,1,0:T(8,128)(2,1)S(1)} %get-tuple-element.35.own_ref) | copy-start | bytes 1966084
  21.2 17.1 %collective-permute-start = (bf16[2,5,2,128,128]{4,3,2,1,0:T(8,128)(2,1)S(1)}, bf16[2,5,2,128,128]{4,3,2,1,0:T(8,128)(2,1)S(1)}, u32[]{:S(2)}, u32[]{:S(2)}) collective-permute-start(bf16[2,5,2,128,128]{4,3,2,1,0:T(8,128)(2,1)S(1)} %get-tuple-element.32), channel_id=1, source_target_pairs={{0,1},{1,2},{2,3},{3,0},{4,5},{5,6},{6,7},{7,4},{8,9},{9,10},{10,1... | collective-permute-start | bytes 1966088 | tf_op jit(solution)/shard_map/ppermute | solution.py:313
  22.4 16.7 %collective-permute-start.1 = (bf16[2,5,2,128,128]{4,3,2,1,0:T(8,128)(2,1)S(1)}, bf16[2,5,2,128,128]{4,3,2,1,0:T(8,128)(2,1)S(1)}, u32[]{:S(2)}, u32[]{:S(2)}) collective-permute-start(bf16[2,5,2,128,128]{4,3,2,1,0:T(8,128)(2,1)S(1)} %get-tuple-element.33), channel_id=1, source_target_pairs={{0,3},{1,0},{2,1},{3,2},{4,7},{5,4},{6,5},{7,6},{8,11},{9,8},{10,9... | collective-permute-start | bytes 1966088 | tf_op jit(solution)/shard_map/ppermute | solution.py:313
  47.0 6.6 %copy-start.9 = (bf16[2,5,2,128,128]{4,3,2,1,0:T(8,128)(2,1)S(1)}, bf16[2,5,2,128,128]{4,3,2,1,0:T(8,128)(2,1)}, u32[]{:S(2)}) copy-start(bf16[2,5,2,128,128]{4,3,2,1,0:T(8,128)(2,1)} %copy-done.8) | copy-start | bytes 1966084
  47.0 24.1 %copy-start.3 = (bf16[2,5,2,128,128]{4,3,2,1,0:T(8,128)(2,1)S(1)}, bf16[2,5,2,128,128]{4,3,2,1,0:T(8,128)(2,1)}, u32[]{:S(2)}) copy-start(bf16[2,5,2,128,128]{4,3,2,1,0:T(8,128)(2,1)} %copy-done.2) | copy-start | bytes 1966084
  47.0 50.4 %copy-start.12 = (f32[2,1024]{1,0:T(2,128)S(1)}, f32[2,1024]{1,0:T(2,128)}, u32[]{:S(2)}) copy-start(f32[2,1024]{1,0:T(2,128)} %weight_ref.1) | copy-start | bytes 24580
  47.0 34.6 %all-to-all-start.1 = ((bf16[64,64,128]{2,1,0:T(8,128)(2,1)}), bf16[64,64,128]{2,1,0:T(8,128)(2,1)S(1)}, u32[]{:S(2)}, u32[]{:S(2)}) async-start(bf16[64,64,128]{2,1,0:T(8,128)(2,1)} %recouple.1), calls=%async_computation.1 | async-start | bytes 2097152 | tf_op jit(solution)/shard_map/all_to_all | solution.py:309
  53.6 17.4 %collective-permute-start.2 = (bf16[2,5,2,128,128]{4,3,2,1,0:T(8,128)(2,1)S(1)}, bf16[2,5,2,128,128]{4,3,2,1,0:T(8,128)(2,1)S(1)}, u32[]{:S(2)}, u32[]{:S(2)}) collective-permute-start(bf16[2,5,2,128,128]{4,3,2,1,0:T(8,128)(2,1)S(1)} %copy-done.9), channel_id=1, source_target_pairs={{0,2},{1,3},{2,0},{3,1},{4,6},{5,7},{6,4},{7,5},{8,10},{9,11},{10,... | collective-permute-start | bytes 1966088 | tf_op jit(solution)/shard_map/ppermute | solution.py:313
  81.7 9.2 %collective-permute-start.3 = (bf16[64,32,128]{2,1,0:T(8,128)(2,1)S(1)}, bf16[64,32,128]{2,1,0:T(8,128)(2,1)S(1)}, u32[]{:S(2)}, u32[]{:S(2)}) collective-permute-start(bf16[64,32,128]{2,1,0:T(8,128)(2,1)S(1)} %get-tuple-element.40), channel_id=1, source_target_pairs={{1,2},{3,0},{6,7},{4,5},{9,10},{11,8},{14,15},{12,13},{17,18},{19,... | collective-permute-start | bytes 1572872 | tf_op jit(solution)/shard_map/ppermute | solution.py:326
  84.8 12.5 %collective-permute-start.4 = (bf16[64,32,128]{2,1,0:T(8,128)(2,1)S(1)}, bf16[64,32,128]{2,1,0:T(8,128)(2,1)S(1)}, u32[]{:S(2)}, u32[]{:S(2)}) collective-permute-start(bf16[64,32,128]{2,1,0:T(8,128)(2,1)S(1)} %get-tuple-element.41), channel_id=1, source_target_pairs={{1,0},{3,2},{6,5},{4,7},{9,8},{11,10},{14,13},{12,15},{17,16},{19,... | collective-permute-start | bytes 1572872 | tf_op jit(solution)/shard_map/ppermute | solution.py:326
  87.4 10.0 %collective-permute-start.5 = (bf16[64,32,128]{2,1,0:T(8,128)(2,1)S(1)}, bf16[64,32,128]{2,1,0:T(8,128)(2,1)S(1)}, u32[]{:S(2)}, u32[]{:S(2)}) collective-permute-start(bf16[64,32,128]{2,1,0:T(8,128)(2,1)S(1)} %get-tuple-element.42), channel_id=1, source_target_pairs={{0,2},{2,0},{5,7},{7,5},{8,10},{10,8},{13,15},{15,13},{16,18},{18,... | collective-permute-start | bytes 1572872 | tf_op jit(solution)/shard_map/ppermute | solution.py:326
  100.6 12.1 %collective-permute-start.6 = (bf16[2,5,128,128]{3,2,1,0:T(8,128)(2,1)S(1)}, bf16[2,5,128,128]{3,2,1,0:T(8,128)(2,1)S(1)}, u32[]{:S(2)}, u32[]{:S(2)}) collective-permute-start(bf16[2,5,128,128]{3,2,1,0:T(8,128)(2,1)S(1)} %get-tuple-element.44), channel_id=1, source_target_pairs={{0,1},{2,3},{5,6},{7,4},{8,9},{10,11},{13,14},{15,12},{16,17},{18,... | collective-permute-start | bytes 983048 | tf_op jit(solution)/shard_map/ppermute | solution.py:326
  101.9 10.8 %collective-permute-start.7 = (bf16[2,5,128,128]{3,2,1,0:T(8,128)(2,1)S(1)}, bf16[2,5,128,128]{3,2,1,0:T(8,128)(2,1)S(1)}, u32[]{:S(2)}, u32[]{:S(2)}) collective-permute-start(bf16[2,5,128,128]{3,2,1,0:T(8,128)(2,1)S(1)} %get-tuple-element.45), channel_id=1, source_target_pairs={{0,2},{2,0},{5,7},{7,5},{8,10},{10,8},{13,15},{15,13},{16,18},{18,... | collective-permute-start | bytes 983048 | tf_op jit(solution)/shard_map/ppermute | solution.py:326
  102.5 16.2 %collective-permute-start.8 = (bf16[2,5,128,128]{3,2,1,0:T(8,128)(2,1)S(1)}, bf16[2,5,128,128]{3,2,1,0:T(8,128)(2,1)S(1)}, u32[]{:S(2)}, u32[]{:S(2)}) collective-permute-start(bf16[2,5,128,128]{3,2,1,0:T(8,128)(2,1)S(1)} %get-tuple-element.46), channel_id=1, source_target_pairs={{0,3},{2,1},{5,4},{7,6},{8,11},{10,9},{13,12},{15,14},{16,19},{18,... | collective-permute-start | bytes 983048 | tf_op jit(solution)/shard_map/ppermute | solution.py:326
  171.9 8.4 %collective-permute-start.9 = (bf16[4,128,128]{2,1,0:T(8,128)(2,1)S(1)}, bf16[4,128,128]{2,1,0:T(8,128)(2,1)S(1)}, u32[]{:S(2)}, u32[]{:S(2)}) collective-permute-start(bf16[4,128,128]{2,1,0:T(8,128)(2,1)S(1)} %get-tuple-element.48), channel_id=1, source_target_pairs={{0,1},{1,2},{2,3},{3,0},{4,5},{5,6},{6,7},{7,4},{8,9},{9,10},{10,1... | collective-permute-start | bytes 393224 | tf_op jit(solution)/shard_map/ppermute | solution.py:313
  173.7 6.6 %collective-permute-start.10 = (bf16[4,128,128]{2,1,0:T(8,128)(2,1)S(1)}, bf16[4,128,128]{2,1,0:T(8,128)(2,1)S(1)}, u32[]{:S(2)}, u32[]{:S(2)}) collective-permute-start(bf16[4,128,128]{2,1,0:T(8,128)(2,1)S(1)} %get-tuple-element.49), channel_id=1, source_target_pairs={{0,3},{1,0},{2,1},{3,2},{4,7},{5,4},{6,5},{7,6},{8,11},{9,8},{10,9... | collective-permute-start | bytes 393224 | tf_op jit(solution)/shard_map/ppermute | solution.py:313
  175.0 5.3 %collective-permute-start.11 = (bf16[2,128,128]{2,1,0:T(8,128)(2,1)S(1)}, bf16[2,128,128]{2,1,0:T(8,128)(2,1)S(1)}, u32[]{:S(2)}, u32[]{:S(2)}) collective-permute-start(bf16[2,128,128]{2,1,0:T(8,128)(2,1)S(1)} %get-tuple-element.50), channel_id=1, source_target_pairs={{0,2},{1,3},{2,0},{3,1},{4,6},{5,7},{6,4},{7,5},{8,10},{9,11},{10,... | collective-permute-start | bytes 196616 | tf_op jit(solution)/shard_map/ppermute | solution.py:313
  (5 other events, 4.7 us)

commit v6 on v5

--- a/solution.py
+++ b/solution.py
@@ -38,6 +38,13 @@
     return jnp.concatenate(parts, axis=0)
 
 
+def masks():
+    row = lax.broadcasted_iota(jnp.int32, (128, LANES), 0)
+    column = lax.broadcasted_iota(jnp.int32, (128, LANES), 1)
+    row_block, column_block = row >> 5, column >> 5
+    return (row_block > column_block) | ((row_block == column_block) & (row < column)), row == column
+
+
 def contract_last(a, b):
     return lax.dot_general(a, b, (((1,), (1,)), ((), ())), preferred_element_type=F32)
 
@@ -49,7 +56,7 @@
 SOURCE = ((2, 0, 0, 0, 3, 0, 1, 1), (1, 2, 0, 0, 1, 3, 1, 1))
 
 
-def pack_kernel(eta_ref, gamma_ref, out_ref, held, sems):
+def pack_kernel(eta_ref, gamma_ref, out_ref, held, ready, sems, out_sems):
     panel = lax.axis_index("panel")
     either = jnp.where(panel < 2, 0, 1)
     row = lax.broadcasted_iota(jnp.int32, (128, LANES), 0)
@@ -79,13 +86,17 @@
             pieces = []
             for j in range(part * 4, part * 4 + 4):
                 pieces += interleave([tile(ch, l, j) for ch in range(2)])
-            start = part * 32 + l * 16
-            out_ref[start : start + 16] = jnp.concatenate(pieces, axis=1).astype(BF16)
-
-
-def spread_kernel(forward_ref, back_ref, forward_out, back_out):
-    for ref, out in ((forward_ref, forward_out), (back_ref, back_out)):
-        shift = 2
+            rows = slice(part * 32 + l * 16, part * 32 + l * 16 + 16)
+            ready[rows] = jnp.concatenate(pieces, axis=1).astype(BF16)
+            copies[l, part] = pltpu.make_async_copy(ready.at[rows], out_ref.at[rows], out_sems.at[l, part])
+            copies[l, part].start()
+    for l in range(2):
+        for part in range(2):
+            copies[l, part].wait()
+
+
+def spread_kernel(forward_ref, back_ref, forward_out, back_out, edge_out):
+    for ref, out, shift in ((forward_ref, forward_out, 2), (back_ref, back_out, 2), (back_ref, edge_out, 1)):
         size = 128 << shift
         row = lax.broadcasted_iota(jnp.int32, (size, 128), 0) >> shift
         column = lax.broadcasted_iota(jnp.int32, (size, 128), 1)
@@ -159,14 +170,11 @@
             value = value * lanes[c]
         ref[r * 128 : (r + 1) * 128, c * LANES : (c + 1) * LANES] = value.astype(BF16)
 
-    row = lax.broadcasted_iota(jnp.int32, (128, LANES), 0)
-    column = lax.broadcasted_iota(jnp.int32, (128, LANES), 1)
-    row_block, column_block = row >> 5, column >> 5
-    first = (row_block > column_block) | ((row_block == column_block) & (row < column))
+    first, diagonal = masks()
     for r in range(8):
         value = tile(r, r)
         mirrored = value.T
-        put(scaled, r, r, jnp.where(row == column, F32(0.0), jnp.where(first, -value, mirrored)))
+        put(scaled, r, r, jnp.where(diagonal, F32(0.0), jnp.where(first, -value, mirrored)))
         put(plain, r, r, jnp.where(first, mirrored, value))
     for r in range(8):
         for step in (1, 2, 3, 4):
@@ -191,36 +199,56 @@
             put(plain, q, p, value.T)
     for b in range(4):
         forward[b * 256 : (b + 1) * 256, :] = contract_last(scaled[b * 256 : (b + 1) * 256], plain[...])
+
+    def product(r, offset):
+        c = (r + offset) % 8
+        value = forward[r * 128 : (r + 1) * 128, c * LANES : (c + 1) * LANES]
+        return value + forward[c * 128 : (c + 1) * 128, r * LANES : (r + 1) * LANES].T
+
+    above = lax.broadcasted_iota(jnp.int32, (128, LANES), 0) < lax.broadcasted_iota(jnp.int32, (128, LANES), 1)
     for b, ref in enumerate((own_out, plus_out, far_out, minus_out)):
+        edges = []
         for l in range(2):
-            for t, offset in enumerate(OFFSETS):
-                r, c = 2 * b + l, (2 * b + l + offset) % 8
-                value = forward[r * 128 : (r + 1) * 128, c * LANES : (c + 1) * LANES]
-                other = forward[c * 128 : (c + 1) * 128, r * LANES : (r + 1) * LANES]
-                ref[l, t] = (value + other.T).astype(BF16)
+            r = 2 * b + l
+            across = product(r, 4)
+            edges.append(jnp.sum(jnp.where(diagonal, across, F32(0.0)), axis=0, keepdims=True))
+            tiles = [jnp.where(above, across, product(r, 0))] + [product(r, offset) for offset in OFFSETS[1:4]]
+            for t, value in enumerate(tiles):
+                start = (l * 4 + t) * 128
+                ref[start : start + 128] = value.astype(BF16)
+        ref[1024:1040] = jnp.concatenate(edges + [jnp.zeros((14, LANES), F32)], axis=0).astype(BF16)
 
 
 def part_kernel(own_ref, plus_ref, far_ref, minus_ref, out_ref):
     here = place()
-
-    def pick(l, t, refs):
-        value = refs[0][l, t]
+    orders = ((own_ref, plus_ref, far_ref, minus_ref), (far_ref, minus_ref, own_ref, plus_ref))
+
+    def pick(ch, start, size):
+        value = orders[ch][0][start : start + size]
         for k in range(1, 4):
-            value = jnp.where(here == k, refs[k][l, t], value)
-        return swap_blocks(value).astype(F32).reshape(16, 8, LANES)
-
+            value = jnp.where(here == k, orders[ch][k][start : start + size], value)
+        return value
+
+    edges = [pick(ch, 1024, 16).astype(F32)[:2] for ch in range(2)]
+    edges = jnp.concatenate(edges + [jnp.zeros((4, LANES), F32)], axis=0)
+    edges = jnp.broadcast_to(edges[None], (16, 8, LANES))
     for l in range(2):
         low, high = [], []
-        for t in range(5):
-            pieces = interleave([pick(l, t, (own_ref, plus_ref, far_ref, minus_ref)), pick(l, t, (far_ref, minus_ref, own_ref, plus_ref))])
+        for t in range(4):
+            both = [swap_blocks(pick(ch, (l * 4 + t) * 128, 128)).astype(F32).reshape(16, 8, LANES) for ch in range(2)]
+            pieces = interleave(both)
             low.append(pieces[0])
             high.append(pieces[1])
-        out_ref[l * 32 : l * 32 + 16] = jnp.concatenate(low, axis=1).astype(BF16)
-        out_ref[l * 32 + 16 : l * 32 + 32] = jnp.concatenate(high, axis=1).astype(BF16)
-
-
-def recouple_back_kernel(table_ref, in_ref, out_ref):
-    out_ref[...] = jnp.concatenate(recouple_rows(table_ref, in_ref, 5), axis=1).astype(BF16)
+        out_ref[l * 32 : l * 32 + 16] = jnp.concatenate(low + [edges], axis=1).astype(BF16)
+        out_ref[l * 32 + 16 : l * 32 + 32] = jnp.concatenate(high + [edges], axis=1).astype(BF16)
+
+
+def recouple_back_kernel(table_ref, edge_table_ref, in_ref, out_ref, edge_ref, mixed):
+    out_ref[...] = jnp.concatenate(recouple_rows(table_ref, in_ref, 4), axis=1).astype(BF16)
+    edges = in_ref[:, 32:40, :].astype(F32).reshape(32, 2, 8, LANES)
+    edges = jnp.concatenate([edges[:, 0, :4], edges[:, 1, :4]], axis=1).reshape(256, LANES).astype(BF16)
+    mixed[...] = jnp.dot(edge_table_ref[...], edges, preferred_element_type=F32).astype(BF16).astype(F32)
+    edge_ref[...] = mixed[pl.ds(pl.multiple_of(lax.axis_index("chan") * 4, 4), 4), :]
 
 
 def back_tile(ref, l, t, ch):
@@ -231,25 +259,34 @@
 
 def back_mirror_kernel(in_ref, pp_ref, plus_ref, minus_ref, far_ref):
     for ch in range(2):
-        for ref, held in ((plus_ref, PLUS), (minus_ref, MINUS), (far_ref, FAR)):
+        for ref, held, size in ((plus_ref, PLUS, 2), (minus_ref, MINUS, 2), (far_ref, FAR, 3)):
             for u, (l, t) in enumerate(held):
-                ref[ch * len(held) + u] = (pp_ref[l, t, ch].T + back_tile(in_ref, l, t, ch)).astype(BF16)
-
-
-def finish_kernel(in_ref, plus_ref, minus_ref, far_ref, pp_ref, out_ref):
+                ref[ch * size + u] = (pp_ref[l, t, ch].T + back_tile(in_ref, l, t, ch)).astype(BF16)
+        for l in range(2):
+            far_ref[ch * 3 + 1 + l] = back_tile(in_ref, l, 0, ch).astype(BF16)
+
+
+def finish_kernel(in_ref, plus_ref, minus_ref, far_ref, pp_ref, edge_ref, out_ref):
     panel = lax.axis_index("panel")
+    first, diagonal = masks()
     for ch in range(2):
         for l in range(2):
 
             def put(offset, value):
                 out_ref[ch, l * 128 : (l + 1) * 128, pl.ds(tile_at(panel, l, offset), LANES)] = value.astype(BF16)
 
-            for t, offset in enumerate(OFFSETS):
-                put(offset, pp_ref[l, t, ch] + back_tile(in_ref, l, t, ch).T)
+            value = back_tile(in_ref, l, 0, ch)
+            mirrored = value.T
+            put(0, pp_ref[l, 0, ch] + jnp.where(first, mirrored, value))
+            edge = edge_ref[ch * 2 + l : ch * 2 + l + 1]
+            across = jnp.where(first, far_ref[ch * 3 + 1 + l].astype(F32), jnp.where(diagonal, edge, mirrored))
+            put(4, pp_ref[l, 4, ch] + across)
+            for t in (1, 2, 3):
+                put(OFFSETS[t], pp_ref[l, t, ch] + back_tile(in_ref, l, t, ch).T)
             put(2, minus_ref[ch * 2 + l])
             if l == 0:
                 put(-1, plus_ref[ch * 2])
-                put(-3, far_ref[ch])
+                put(-3, far_ref[ch * 3])
             else:
                 put(-1, pp_ref[0, 1, ch].T + back_tile(in_ref, 0, 1, ch))
                 put(-3, plus_ref[ch * 2 + 1])
@@ -298,6 +335,7 @@
         kernel,
         out_shape=shaped[0] if single else shaped,
         in_specs=[pl.BlockSpec(memory_space=space or pltpu.VMEM)] * len(args),
+        out_specs=jax.tree.map(lambda _: pl.BlockSpec(memory_space=space or pltpu.VMEM), shaped[0] if single else shaped),
         scratch_shapes=list(scratch),
         compiler_params=params(60 if space else 24),
         cost_estimate=cost(flops, size),
@@ -341,11 +379,16 @@
         pack_kernel,
         (64, 64, LANES),
         (eta, gamma),
-        scratch=[pltpu.VMEM((2, 2, 256, 1024), BF16), pltpu.SemaphoreType.DMA((2, 2, 2))],
+        scratch=[
+            pltpu.VMEM((2, 2, 256, 1024), BF16),
+            pltpu.VMEM((64, 64, LANES), BF16),
+            pltpu.SemaphoreType.DMA((2, 2, 2)),
+            pltpu.SemaphoreType.DMA((2, 2)),
+        ],
         name="pack",
         space=pltpu.HBM,
     )
-    forward_wide, back_wide = call(spread_kernel, [(512, 512)] * 2, (forward_table, back_table), flops=300_000_000, name="spread")
+    forward_wide, back_wide, edge_wide = call(spread_kernel, [(512, 512), (512, 512), (256, 256)], (forward_table, back_table), flops=300_000_000, name="spread")
     packed = exchange(packed, "chan")
     pp_own, *pp = call(
         pair_kernel,
@@ -366,7 +409,7 @@
     received = to_owner(*sends)
     own, *outs = call(
         product_kernel,
-        [(2, 5, 128, LANES)] * 4,
+        [(1040, LANES)] * 4,
         (mixed, *received, cc_weight),
         flops=2_200_000_000,
         scratch=[pltpu.VMEM((1024, 1024), BF16)] * 2 + [pltpu.VMEM((1024, 1024), F32)],
@@ -375,11 +418,19 @@
     outs = from_owner(*outs)
     part = call(part_kernel, (64, 40, LANES), (own, *outs), name="part")
     part = exchange(part, "chan")
-    part = call(recouple_back_kernel, (64, 40, LANES), (back_wide, part), flops=400_000_000, name="recouple_back")
+    part, edge = call(
+        recouple_back_kernel,
+        [(64, 32, LANES), (4, LANES)],
+        (back_wide, edge_wide, part),
+        flops=400_000_000,
+        scratch=[pltpu.VMEM((256, LANES), F32)],
+        name="recouple_back",
+        dtype=[BF16, F32],
+    )
     part = exchange(part, "chan")
-    back_sends = call(back_mirror_kernel, [(4, 128, LANES), (4, 128, LANES), (2, 128, LANES)], (part, pp_part), name="back_mirror")
+    back_sends = call(back_mirror_kernel, [(4, 128, LANES), (4, 128, LANES), (6, 128, LANES)], (part, pp_part), name="back_mirror")
     back_received = mirror(*back_sends)
-    return call(finish_kernel, (2, 256, 1024), (part, *back_received, pp_part), name="finish")
+    return call(finish_kernel, (2, 256, 1024), (part, *back_received, pp_part, edge), name="finish")
 
 
 def solution(mesh):

time: 182 us -> 180 us (0.989)
  blocking collectives: 51.2 us -> 48.6 us
    all_to_all x2, blocking collectives: 51.2 us -> 48.6 us  [exchange(): lax.all_to_all(operand, axis, split_axis=0, concat_axis=0, tiled=True)]
    ppermute x6, waiting for transfers between devices: 32.5 us -> 34.3 us  [step(): return lax.ppermute(value, 'panel', [(i, (i + by) % 4) for i in range(4)])]
    unnamed x30 -> x34, local copies, waits for them, and re-layouts: 4.76 us -> 5.39 us
where the time goes in v6:
time: 180 us
  waiting for transfers between devices  70.3 us (39%)
  blocking collectives  48.6 us (27%)
  starting transfers between devices  39.4 us (22%)
  Pallas kernels  15.9 us (9%)
  local copies, waits for them, and re-layouts  5.39 us (3%)
    all_to_all x2, blocking collectives, exchange(): lax.all_to_all(operand, axis, split_axis=0, concat_axis=0, tiled=True)  48.6 us
    ppermute x6, waiting for transfers between devices, step(): return lax.ppermute(value, 'panel', [(i, (i + by) % 4) for i in range(4)])  34.3 us
    ppermute x6, waiting for transfers between devices, route(): return lax.ppermute(value, ('chan', 'panel'), pairs)  22.6 us
    all_to_all x2, starting transfers between devices, exchange(): lax.all_to_all(operand, axis, split_axis=0, concat_axis=0, tiled=True)  19.9 us
    pallas_call x11, Pallas kernels, call(): pl.pallas_call(kernel, out_shape=shaped[0] if single else shaped, in_spec...  15.9 us
    all_to_all x2, waiting for transfers between devices, exchange(): lax.all_to_all(operand, axis, split_axis=0, concat_axis=0, tiled=True)  13.4 us
    ppermute x6, starting transfers between devices, route(): return lax.ppermute(value, ('chan', 'panel'), pairs)  9.84 us
    ppermute x6, starting transfers between devices, step(): return lax.ppermute(value, 'panel', [(i, (i + by) % 4) for i in range(4)])  9.71 us
  transfers between devices with their start and end apart: 14, of which 9 were waited for; matrix products, arithmetic and copies ran while one was open for 0% of the time, Pallas kernels for 2%

profile of v6, /device:TPU:1, one launch (start us, length us, event | category | flops | bytes accessed | tf_op | source)
XLA Modules:
  0.0 179.9 jit_solution(15259218671706554629)
XLA Ops:
  0.0 3.7 %pack.1 = bf16[64,64,128]{2,1,0:T(8,128)(2,1)} custom-call(bf16[2,256,1024]{2,1,0:T(8,128)(2,1)} %eta_ref.3, bf16[2,256,1024]{2,1,0:T(8,128)(2,1)} %gamma_ref.3), custom_call_target="tpu_custom_call" | custom-call | bytes 3145728 | tf_op jit(solution)/shard_map/pack/pallas_call | solution.py:334
  3.8 13.3 %all-to-all-start = ((bf16[64,64,128]{2,1,0:T(8,128)(2,1)}), bf16[64,64,128]{2,1,0:T(8,128)(2,1)S(1)}, u32[]{:S(2)}, u32[]{:S(2)}) async-start(bf16[64,64,128]{2,1,0:T(8,128)(2,1)} %pack.1), calls=%async_computation | async-start | bytes 2097152 | tf_op jit(solution)/shard_map/all_to_all | solution.py:347
  17.2 2.9 %pair.1 = (bf16[2,5,2,128,128]{4,3,2,1,0:T(8,128)(2,1)S(1)}, bf16[2,5,2,128,128]{4,3,2,1,0:T(8,128)(2,1)S(1)}, bf16[2,5,2,128,128]{4,3,2,1,0:T(8,128)(2,1)S(1)}, bf16[2,5,2,128,128]{4,3,2,1,0:T(8,128)(2,1)S(1)}) custom-call(bf16[2,256,1024]{2,1,0:T(8,128)(2,1)S(1)} %copy-done, bf16[2,256,1024]{2,1,0:T(8,128)(2,1)S(1)} %copy-done.1, ...), custom_call_target="tpu_custom_call" | custom-call | flops 2200000000 | bytes 4726784 | tf_op jit(solution)/shard_map/pair/pallas_call | solution.py:334
  22.2 1.4 collective-permute-start.1
  25.2 12.8 %collective-permute-done.plus_ref = bf16[2,5,2,128,128]{4,3,2,1,0:T(8,128)(2,1)S(1)} collective-permute-done((bf16[2,5,2,128,128]{4,3,2,1,0:T(8,128)(2,1)S(1)}, bf16[2,5,2,128,128]{4,3,2,1,0:T(8,128)(2,1)S(1)}, u32[]{:S(2)}, u32[]{:S(2)}) %collective-permute-start) | collective-permute-done | bytes 655392 | tf_op jit(solution)/shard_map/ppermute | solution.py:351
  39.8 5.3 %all-to-all-done.in_ref = bf16[64,64,128]{2,1,0:T(8,128)(2,1)S(1)} async-done(((bf16[64,64,128]{2,1,0:T(8,128)(2,1)}), bf16[64,64,128]{2,1,0:T(8,128)(2,1)S(1)}, u32[]{:S(2)}, u32[]{:S(2)}) %all-to-all-start) | async-done | bytes 1048608 | tf_op jit(solution)/shard_map/all_to_all | solution.py:347
  45.1 1.7 recouple.1
  46.8 6.6 %all-to-all-start.1 = ((bf16[64,64,128]{2,1,0:T(8,128)(2,1)}), bf16[64,64,128]{2,1,0:T(8,128)(2,1)S(1)}, u32[]{:S(2)}, u32[]{:S(2)}) async-start(bf16[64,64,128]{2,1,0:T(8,128)(2,1)} %recouple.1), calls=%async_computation.1 | async-start | bytes 2097152 | tf_op jit(solution)/shard_map/all_to_all | solution.py:347
  53.4 2.8 %collective-permute-start.2 = (bf16[2,5,2,128,128]{4,3,2,1,0:T(8,128)(2,1)S(1)}, bf16[2,5,2,128,128]{4,3,2,1,0:T(8,128)(2,1)S(1)}, u32[]{:S(2)}, u32[]{:S(2)}) collective-permute-start(bf16[2,5,2,128,128]{4,3,2,1,0:T(8,128)(2,1)S(1)} %copy-done.9), channel_id=1, source_target_pairs={{0,2},{1,3},{2,0},{3,1},{4,6},{5,7},{6,4},{7,5},{8,10},{9,11},{10,... | collective-permute-start | bytes 1966088 | tf_op jit(solution)/shard_map/ppermute | solution.py:351
  56.2 14.6 %collective-permute-done.2.far_ref = bf16[2,5,2,128,128]{4,3,2,1,0:T(8,128)(2,1)S(1)} collective-permute-done((bf16[2,5,2,128,128]{4,3,2,1,0:T(8,128)(2,1)S(1)}, bf16[2,5,2,128,128]{4,3,2,1,0:T(8,128)(2,1)S(1)}, u32[]{:S(2)}, u32[]{:S(2)}) %collective-permute-start.2) | collective-permute-done | bytes 655392 | tf_op jit(solution)/shard_map/ppermute | solution.py:351
  73.3 8.1 %all-to-all-done.1.in_ref = bf16[64,64,128]{2,1,0:T(8,128)(2,1)S(1)} async-done(((bf16[64,64,128]{2,1,0:T(8,128)(2,1)}), bf16[64,64,128]{2,1,0:T(8,128)(2,1)S(1)}, u32[]{:S(2)}, u32[]{:S(2)}) %all-to-all-start.1) | async-done | bytes 1048608 | tf_op jit(solution)/shard_map/all_to_all | solution.py:347
  81.4 3.1 %collective-permute-start.3 = (bf16[64,32,128]{2,1,0:T(8,128)(2,1)S(1)}, bf16[64,32,128]{2,1,0:T(8,128)(2,1)S(1)}, u32[]{:S(2)}, u32[]{:S(2)}) collective-permute-start(bf16[64,32,128]{2,1,0:T(8,128)(2,1)S(1)} %get-tuple-element.44), channel_id=1, source_target_pairs={{1,2},{3,0},{6,7},{4,5},{9,10},{11,8},{14,15},{12,13},{17,18},{19,... | collective-permute-start | bytes 1572872 | tf_op jit(solution)/shard_map/ppermute | solution.py:364
  84.6 2.6 %collective-permute-start.4 = (bf16[64,32,128]{2,1,0:T(8,128)(2,1)S(1)}, bf16[64,32,128]{2,1,0:T(8,128)(2,1)S(1)}, u32[]{:S(2)}, u32[]{:S(2)}) collective-permute-start(bf16[64,32,128]{2,1,0:T(8,128)(2,1)S(1)} %get-tuple-element.45), channel_id=1, source_target_pairs={{1,0},{3,2},{6,5},{4,7},{9,8},{11,10},{14,13},{12,15},{17,16},{19,... | collective-permute-start | bytes 1572872 | tf_op jit(solution)/shard_map/ppermute | solution.py:364
  88.1 2.6 %collective-permute-done.3.plus_ref = bf16[64,32,128]{2,1,0:T(8,128)(2,1)S(1)} collective-permute-done((bf16[64,32,128]{2,1,0:T(8,128)(2,1)S(1)}, bf16[64,32,128]{2,1,0:T(8,128)(2,1)S(1)}, u32[]{:S(2)}, u32[]{:S(2)}) %collective-permute-start.3) | collective-permute-done | bytes 524320 | tf_op jit(solution)/shard_map/ppermute | solution.py:364
  90.7 6.4 %collective-permute-done.4.minus_ref = bf16[64,32,128]{2,1,0:T(8,128)(2,1)S(1)} collective-permute-done((bf16[64,32,128]{2,1,0:T(8,128)(2,1)S(1)}, bf16[64,32,128]{2,1,0:T(8,128)(2,1)S(1)}, u32[]{:S(2)}, u32[]{:S(2)}) %collective-permute-start.4) | collective-permute-done | bytes 524320 | tf_op jit(solution)/shard_map/ppermute | solution.py:364
  97.1 3.2 %product.1 = (bf16[1040,128]{1,0:T(8,128)(2,1)S(1)}, bf16[1040,128]{1,0:T(8,128)(2,1)S(1)}, bf16[1040,128]{1,0:T(8,128)(2,1)S(1)}, bf16[1040,128]{1,0:T(8,128)(2,1)S(1)}) custom-call(bf16[64,64,128]{2,1,0:T(8,128)(2,1)S(1)} %all-to-all-done.1.in_ref, bf16[64,32,128]{2,1,0:T(8,128)(2,1)S(1)} %collective-permute-done.3.plus_ref, ...), custom_call_target="tpu_custom_call" | custom-call | flops 2200000000 | bytes 3694592 | tf_op jit(solution)/shard_map/product/pallas_call | solution.py:334
  103.6 8.2 %collective-permute-done.6.plus_ref = bf16[1040,128]{1,0:T(8,128)(2,1)S(1)} collective-permute-done((bf16[1040,128]{1,0:T(8,128)(2,1)S(1)}, bf16[1040,128]{1,0:T(8,128)(2,1)S(1)}, u32[]{:S(2)}, u32[]{:S(2)}) %collective-permute-start.6) | collective-permute-done | bytes 266272 | tf_op jit(solution)/shard_map/ppermute | solution.py:364
  111.8 5.4 %collective-permute-done.8.minus_ref = bf16[1040,128]{1,0:T(8,128)(2,1)S(1)} collective-permute-done((bf16[1040,128]{1,0:T(8,128)(2,1)S(1)}, bf16[1040,128]{1,0:T(8,128)(2,1)S(1)}, u32[]{:S(2)}, u32[]{:S(2)}) %collective-permute-start.8) | collective-permute-done | bytes 266272 | tf_op jit(solution)/shard_map/ppermute | solution.py:364
  117.9 25.2 %all_to_all.20.in_ref = bf16[64,40,128]{2,1,0:T(8,128)(2,1)S(1)} all-to-all(bf16[64,40,128]{2,1,0:T(8,128)(2,1)S(1)} %part.1), channel_id=1, replica_groups=mesh['chan'=64,'panel'=4] {'chan'}, dimensions={0} | all-to-all | bytes 1310720 | tf_op jit(solution)/shard_map/all_to_all | solution.py:347
  143.6 23.4 %all_to_all.21.in_ref = bf16[64,32,128]{2,1,0:T(8,128)(2,1)S(1)} all-to-all(bf16[64,32,128]{2,1,0:T(8,128)(2,1)S(1)} %get-tuple-element.51), channel_id=1, replica_groups=mesh['chan'=64,'panel'=4] {'chan'}, dimensions={0} | all-to-all | bytes 1048576 | tf_op jit(solution)/shard_map/all_to_all | solution.py:347
  167.3 1.9 %collective-permute-start.11 = (bf16[6,128,128]{2,1,0:T(8,128)(2,1)S(1)}, bf16[6,128,128]{2,1,0:T(8,128)(2,1)S(1)}, u32[]{:S(2)}, u32[]{:S(2)}) collective-permute-start(bf16[6,128,128]{2,1,0:T(8,128)(2,1)S(1)} %get-tuple-element.55), channel_id=1, source_target_pairs={{0,2},{1,3},{2,0},{3,1},{4,6},{5,7},{6,4},{7,5},{8,10},{9,11},{10,... | collective-permute-start | bytes 589832 | tf_op jit(solution)/shard_map/ppermute | solution.py:351
  169.2 2.3 %collective-permute-start.10 = (bf16[4,128,128]{2,1,0:T(8,128)(2,1)S(1)}, bf16[4,128,128]{2,1,0:T(8,128)(2,1)S(1)}, u32[]{:S(2)}, u32[]{:S(2)}) collective-permute-start(bf16[4,128,128]{2,1,0:T(8,128)(2,1)S(1)} %get-tuple-element.54), channel_id=1, source_target_pairs={{0,3},{1,0},{2,1},{3,2},{4,7},{5,4},{6,5},{7,6},{8,11},{9,8},{10,9... | collective-permute-start | bytes 393224 | tf_op jit(solution)/shard_map/ppermute | solution.py:351
  171.5 6.9 %collective-permute-done.10.minus_ref = bf16[4,128,128]{2,1,0:T(8,128)(2,1)S(1)} collective-permute-done((bf16[4,128,128]{2,1,0:T(8,128)(2,1)S(1)}, bf16[4,128,128]{2,1,0:T(8,128)(2,1)S(1)}, u32[]{:S(2)}, u32[]{:S(2)}) %collective-permute-start.10) | collective-permute-done | bytes 131104 | tf_op jit(solution)/shard_map/ppermute | solution.py:351
  178.4 1.5 finish.1
  (52 shorter events, 13.7 us)
Async XLA Ops:
  0.0 17.1 %copy-start.15 = (f32[2,1024]{1,0:T(2,128)S(1)}, f32[2,1024]{1,0:T(2,128)}, u32[]{:S(2)}) copy-start(f32[2,1024]{1,0:T(2,128)} %param.9) | copy-start | bytes 24580
  0.0 17.1 %copy-start.16 = (s32[2]{0:T(128)S(1)}, s32[2]{0:T(128)}, u32[]{:S(2)}) copy-start(s32[2]{0:T(128)} %param.11) | copy-start | bytes 28
  3.7 13.4 %copy-start = (bf16[2,256,1024]{2,1,0:T(8,128)(2,1)S(1)}, bf16[2,256,1024]{2,1,0:T(8,128)(2,1)}, u32[]{:S(2)}) copy-start(bf16[2,256,1024]{2,1,0:T(8,128)(2,1)} %eta_ref.3) | copy-start | bytes 3145732
  3.8 13.4 %copy-start.1 = (bf16[2,256,1024]{2,1,0:T(8,128)(2,1)S(1)}, bf16[2,256,1024]{2,1,0:T(8,128)(2,1)}, u32[]{:S(2)}) copy-start(bf16[2,256,1024]{2,1,0:T(8,128)(2,1)} %gamma_ref.3) | copy-start | bytes 3145732
  3.8 41.3 %all-to-all-start = ((bf16[64,64,128]{2,1,0:T(8,128)(2,1)}), bf16[64,64,128]{2,1,0:T(8,128)(2,1)S(1)}, u32[]{:S(2)}, u32[]{:S(2)}) async-start(bf16[64,64,128]{2,1,0:T(8,128)(2,1)} %pack.1), calls=%async_computation | async-start | bytes 2097152 | tf_op jit(solution)/shard_map/all_to_all | solution.py:347
  17.2 6.5 %copy-start.10 = (bf16[128,128]{1,0:T(8,128)(2,1)S(1)}, bf16[128,128]{1,0:T(8,128)(2,1)}, u32[]{:S(2)}) copy-start(bf16[128,128]{1,0:T(8,128)(2,1)} %forward_ref.1) | copy-start | bytes 98308
  21.0 17.1 %copy-start.2 = (bf16[2,5,2,128,128]{4,3,2,1,0:T(8,128)(2,1)}, bf16[2,5,2,128,128]{4,3,2,1,0:T(8,128)(2,1)S(1)}, u32[]{:S(2)}) copy-start(bf16[2,5,2,128,128]{4,3,2,1,0:T(8,128)(2,1)S(1)} %get-tuple-element.39.own_ref) | copy-start | bytes 1966084
  21.0 17.1 %collective-permute-start = (bf16[2,5,2,128,128]{4,3,2,1,0:T(8,128)(2,1)S(1)}, bf16[2,5,2,128,128]{4,3,2,1,0:T(8,128)(2,1)S(1)}, u32[]{:S(2)}, u32[]{:S(2)}) collective-permute-start(bf16[2,5,2,128,128]{4,3,2,1,0:T(8,128)(2,1)S(1)} %get-tuple-element.36), channel_id=1, source_target_pairs={{0,1},{1,2},{2,3},{3,0},{4,5},{5,6},{6,7},{7,4},{8,9},{9,10},{10,1... | collective-permute-start | bytes 1966088 | tf_op jit(solution)/shard_map/ppermute | solution.py:351
  22.2 16.7 %collective-permute-start.1 = (bf16[2,5,2,128,128]{4,3,2,1,0:T(8,128)(2,1)S(1)}, bf16[2,5,2,128,128]{4,3,2,1,0:T(8,128)(2,1)S(1)}, u32[]{:S(2)}, u32[]{:S(2)}) collective-permute-start(bf16[2,5,2,128,128]{4,3,2,1,0:T(8,128)(2,1)S(1)} %get-tuple-element.37), channel_id=1, source_target_pairs={{0,3},{1,0},{2,1},{3,2},{4,7},{5,4},{6,5},{7,6},{8,11},{9,8},{10,9... | collective-permute-start | bytes 1966088 | tf_op jit(solution)/shard_map/ppermute | solution.py:351
  46.7 6.6 %copy-start.9 = (bf16[2,5,2,128,128]{4,3,2,1,0:T(8,128)(2,1)S(1)}, bf16[2,5,2,128,128]{4,3,2,1,0:T(8,128)(2,1)}, u32[]{:S(2)}) copy-start(bf16[2,5,2,128,128]{4,3,2,1,0:T(8,128)(2,1)} %copy-done.8) | copy-start | bytes 1966084
  46.8 24.1 %copy-start.3 = (bf16[2,5,2,128,128]{4,3,2,1,0:T(8,128)(2,1)S(1)}, bf16[2,5,2,128,128]{4,3,2,1,0:T(8,128)(2,1)}, u32[]{:S(2)}) copy-start(bf16[2,5,2,128,128]{4,3,2,1,0:T(8,128)(2,1)} %copy-done.2) | copy-start | bytes 1966084
  46.8 50.4 %copy-start.12 = (f32[2,1024]{1,0:T(2,128)S(1)}, f32[2,1024]{1,0:T(2,128)}, u32[]{:S(2)}) copy-start(f32[2,1024]{1,0:T(2,128)} %weight_ref.1) | copy-start | bytes 24580
  46.8 34.6 %all-to-all-start.1 = ((bf16[64,64,128]{2,1,0:T(8,128)(2,1)}), bf16[64,64,128]{2,1,0:T(8,128)(2,1)S(1)}, u32[]{:S(2)}, u32[]{:S(2)}) async-start(bf16[64,64,128]{2,1,0:T(8,128)(2,1)} %recouple.1), calls=%async_computation.1 | async-start | bytes 2097152 | tf_op jit(solution)/shard_map/all_to_all | solution.py:347
  53.4 17.4 %collective-permute-start.2 = (bf16[2,5,2,128,128]{4,3,2,1,0:T(8,128)(2,1)S(1)}, bf16[2,5,2,128,128]{4,3,2,1,0:T(8,128)(2,1)S(1)}, u32[]{:S(2)}, u32[]{:S(2)}) collective-permute-start(bf16[2,5,2,128,128]{4,3,2,1,0:T(8,128)(2,1)S(1)} %copy-done.9), channel_id=1, source_target_pairs={{0,2},{1,3},{2,0},{3,1},{4,6},{5,7},{6,4},{7,5},{8,10},{9,11},{10,... | collective-permute-start | bytes 1966088 | tf_op jit(solution)/shard_map/ppermute | solution.py:351
  81.4 9.2 %collective-permute-start.3 = (bf16[64,32,128]{2,1,0:T(8,128)(2,1)S(1)}, bf16[64,32,128]{2,1,0:T(8,128)(2,1)S(1)}, u32[]{:S(2)}, u32[]{:S(2)}) collective-permute-start(bf16[64,32,128]{2,1,0:T(8,128)(2,1)S(1)} %get-tuple-element.44), channel_id=1, source_target_pairs={{1,2},{3,0},{6,7},{4,5},{9,10},{11,8},{14,15},{12,13},{17,18},{19,... | collective-permute-start | bytes 1572872 | tf_op jit(solution)/shard_map/ppermute | solution.py:364
  84.6 12.5 %collective-permute-start.4 = (bf16[64,32,128]{2,1,0:T(8,128)(2,1)S(1)}, bf16[64,32,128]{2,1,0:T(8,128)(2,1)S(1)}, u32[]{:S(2)}, u32[]{:S(2)}) collective-permute-start(bf16[64,32,128]{2,1,0:T(8,128)(2,1)S(1)} %get-tuple-element.45), channel_id=1, source_target_pairs={{1,0},{3,2},{6,5},{4,7},{9,8},{11,10},{14,13},{12,15},{17,16},{19,... | collective-permute-start | bytes 1572872 | tf_op jit(solution)/shard_map/ppermute | solution.py:364
  87.2 10.0 %collective-permute-start.5 = (bf16[64,32,128]{2,1,0:T(8,128)(2,1)S(1)}, bf16[64,32,128]{2,1,0:T(8,128)(2,1)S(1)}, u32[]{:S(2)}, u32[]{:S(2)}) collective-permute-start(bf16[64,32,128]{2,1,0:T(8,128)(2,1)S(1)} %get-tuple-element.46), channel_id=1, source_target_pairs={{0,2},{2,0},{5,7},{7,5},{8,10},{10,8},{13,15},{15,13},{16,18},{18,... | collective-permute-start | bytes 1572872 | tf_op jit(solution)/shard_map/ppermute | solution.py:364
  100.3 11.4 %collective-permute-start.6 = (bf16[1040,128]{1,0:T(8,128)(2,1)S(1)}, bf16[1040,128]{1,0:T(8,128)(2,1)S(1)}, u32[]{:S(2)}, u32[]{:S(2)}) collective-permute-start(bf16[1040,128]{1,0:T(8,128)(2,1)S(1)} %get-tuple-element.48), channel_id=1, source_target_pairs={{0,1},{2,3},{5,6},{7,4},{8,9},{10,11},{13,14},{15,12},{16,17},{18,... | collective-permute-start | bytes 798728 | tf_op jit(solution)/shard_map/ppermute | solution.py:364
  101.6 10.2 %collective-permute-start.7 = (bf16[1040,128]{1,0:T(8,128)(2,1)S(1)}, bf16[1040,128]{1,0:T(8,128)(2,1)S(1)}, u32[]{:S(2)}, u32[]{:S(2)}) collective-permute-start(bf16[1040,128]{1,0:T(8,128)(2,1)S(1)} %get-tuple-element.49), channel_id=1, source_target_pairs={{0,2},{2,0},{5,7},{7,5},{8,10},{10,8},{13,15},{15,13},{16,18},{18,... | collective-permute-start | bytes 798728 | tf_op jit(solution)/shard_map/ppermute | solution.py:364
  102.3 14.8 %collective-permute-start.8 = (bf16[1040,128]{1,0:T(8,128)(2,1)S(1)}, bf16[1040,128]{1,0:T(8,128)(2,1)S(1)}, u32[]{:S(2)}, u32[]{:S(2)}) collective-permute-start(bf16[1040,128]{1,0:T(8,128)(2,1)S(1)} %get-tuple-element.50), channel_id=1, source_target_pairs={{0,3},{2,1},{5,4},{7,6},{8,11},{10,9},{13,12},{15,14},{16,19},{18,... | collective-permute-start | bytes 798728 | tf_op jit(solution)/shard_map/ppermute | solution.py:364
  117.1 26.0 %copy-start.14 = (bf16[256,256]{1,0:T(8,128)(2,1)S(1)}, bf16[256,256]{1,0:T(8,128)(2,1)}, u32[]{:S(2)}) copy-start(bf16[256,256]{1,0:T(8,128)(2,1)} %copy-done.13) | copy-start | bytes 393220
  167.3 11.1 %collective-permute-start.11 = (bf16[6,128,128]{2,1,0:T(8,128)(2,1)S(1)}, bf16[6,128,128]{2,1,0:T(8,128)(2,1)S(1)}, u32[]{:S(2)}, u32[]{:S(2)}) collective-permute-start(bf16[6,128,128]{2,1,0:T(8,128)(2,1)S(1)} %get-tuple-element.55), channel_id=1, source_target_pairs={{0,2},{1,3},{2,0},{3,1},{4,6},{5,7},{6,4},{7,5},{8,10},{9,11},{10,... | collective-permute-start | bytes 589832 | tf_op jit(solution)/shard_map/ppermute | solution.py:351
  169.2 9.2 %collective-permute-start.10 = (bf16[4,128,128]{2,1,0:T(8,128)(2,1)S(1)}, bf16[4,128,128]{2,1,0:T(8,128)(2,1)S(1)}, u32[]{:S(2)}, u32[]{:S(2)}) collective-permute-start(bf16[4,128,128]{2,1,0:T(8,128)(2,1)S(1)} %get-tuple-element.54), channel_id=1, source_target_pairs={{0,3},{1,0},{2,1},{3,2},{4,7},{5,4},{6,5},{7,6},{8,11},{9,8},{10,9... | collective-permute-start | bytes 393224 | tf_op jit(solution)/shard_map/ppermute | solution.py:351
  171.5 6.9 %collective-permute-start.9 = (bf16[4,128,128]{2,1,0:T(8,128)(2,1)S(1)}, bf16[4,128,128]{2,1,0:T(8,128)(2,1)S(1)}, u32[]{:S(2)}, u32[]{:S(2)}) collective-permute-start(bf16[4,128,128]{2,1,0:T(8,128)(2,1)S(1)} %get-tuple-element.53), channel_id=1, source_target_pairs={{0,1},{1,2},{2,3},{3,0},{4,5},{5,6},{6,7},{7,4},{8,9},{9,10},{10,1... | collective-permute-start | bytes 393224 | tf_op jit(solution)/shard_map/ppermute | solution.py:351
  (7 other events, 11.9 us)

commit v7 on v6

--- a/solution.py
+++ b/solution.py
@@ -133,15 +133,18 @@
     return lax.rem(lax.axis_index("panel") + 4 - lax.rem(lax.axis_index("chan"), 2), 4)
 
 
-def send_kernel(in_ref, plus_ref, minus_ref, far_ref):
+def channel_rows(ref, ch):
+    return ref[:, pl.ds(pl.multiple_of(ch * 32, 32), 32), :]
+
+
+def send_far_kernel(in_ref, far_ref):
+    far_ref[...] = channel_rows(in_ref, jnp.where(place() == 0, 1, 0))
+
+
+def send_near_kernel(in_ref, plus_ref, minus_ref):
     here = place()
-
-    def rows(ch):
-        return in_ref[:, pl.ds(pl.multiple_of(ch * 32, 32), 32), :]
-
-    plus_ref[...] = rows(jnp.where(here == 1, 1, 0))
-    minus_ref[...] = rows(jnp.where(here == 1, 0, 1))
-    far_ref[...] = rows(jnp.where(here == 0, 1, 0))
+    plus_ref[...] = channel_rows(in_ref, jnp.where(here == 1, 1, 0))
+    minus_ref[...] = channel_rows(in_ref, jnp.where(here == 1, 0, 1))
 
 
 def tile_of(ref, l, j, first=0):
@@ -216,6 +219,8 @@
             for t, value in enumerate(tiles):
                 start = (l * 4 + t) * 128
                 ref[start : start + 128] = value.astype(BF16)
+        if b == 2:
+            ref[1040:1056] = jnp.zeros((16, LANES), BF16)
         ref[1024:1040] = jnp.concatenate(edges + [jnp.zeros((14, LANES), F32)], axis=0).astype(BF16)
 
 
@@ -257,13 +262,20 @@
     return jnp.concatenate([low, high], axis=1).reshape(128, LANES)
 
 
-def back_mirror_kernel(in_ref, pp_ref, plus_ref, minus_ref, far_ref):
+def back_far_kernel(in_ref, pp_ref, far_ref):
+    first, _ = masks()
     for ch in range(2):
-        for ref, held, size in ((plus_ref, PLUS, 2), (minus_ref, MINUS, 2), (far_ref, FAR, 3)):
+        l, t = FAR[0]
+        far_ref[ch * 256 : ch * 256 + 128] = (pp_ref[l, t, ch].T + back_tile(in_ref, l, t, ch)).astype(BF16)
+        far_ref[ch * 256 + 128 : ch * 256 + 256] = jnp.where(first, back_tile(in_ref, 0, 0, ch), back_tile(in_ref, 1, 0, ch).T).astype(BF16)
+    far_ref[512:528] = jnp.zeros((16, LANES), BF16)
+
+
+def back_near_kernel(in_ref, pp_ref, plus_ref, minus_ref):
+    for ch in range(2):
+        for ref, held in ((plus_ref, PLUS), (minus_ref, MINUS)):
             for u, (l, t) in enumerate(held):
-                ref[ch * size + u] = (pp_ref[l, t, ch].T + back_tile(in_ref, l, t, ch)).astype(BF16)
-        for l in range(2):
-            far_ref[ch * 3 + 1 + l] = back_tile(in_ref, l, 0, ch).astype(BF16)
+                ref[ch * 2 + u] = (pp_ref[l, t, ch].T + back_tile(in_ref, l, t, ch)).astype(BF16)
 
 
 def finish_kernel(in_ref, plus_ref, minus_ref, far_ref, pp_ref, edge_ref, out_ref):
@@ -279,14 +291,15 @@
             mirrored = value.T
             put(0, pp_ref[l, 0, ch] + jnp.where(first, mirrored, value))
             edge = edge_ref[ch * 2 + l : ch * 2 + l + 1]
-            across = jnp.where(first, far_ref[ch * 3 + 1 + l].astype(F32), jnp.where(diagonal, edge, mirrored))
+            far = far_ref[ch * 256 + 128 : ch * 256 + 256].astype(F32)
+            across = jnp.where(first, far if l == 0 else far.T, jnp.where(diagonal, edge, mirrored))
             put(4, pp_ref[l, 4, ch] + across)
             for t in (1, 2, 3):
                 put(OFFSETS[t], pp_ref[l, t, ch] + back_tile(in_ref, l, t, ch).T)
             put(2, minus_ref[ch * 2 + l])
             if l == 0:
                 put(-1, plus_ref[ch * 2])
-                put(-3, far_ref[ch * 3])
+                put(-3, far_ref[ch * 256 : ch * 256 + 128])
             else:
                 put(-1, pp_ref[0, 1, ch].T + back_tile(in_ref, 0, 1, ch))
                 put(-3, plus_ref[ch * 2 + 1])
@@ -405,11 +418,13 @@
     pp_far = step(pp_far, 2)
     pp_part = call(pair_sum_kernel, (2, 5, 2, 128, LANES), (pp_own, pp_plus, pp_far, pp_minus), name="pair_sum", dtype=F32)
     mixed, pp_part = lax.optimization_barrier((mixed, pp_part))
-    sends = call(send_kernel, [(64, 32, LANES)] * 3, (mixed,), name="send")
-    received = to_owner(*sends)
+    far = call(send_far_kernel, (64, 32, LANES), (mixed,), name="send_far")
+    mixed, far = lax.optimization_barrier((mixed, far))
+    near = call(send_near_kernel, [(64, 32, LANES)] * 2, (mixed,), name="send_near")
+    received = to_owner(*near, far)
     own, *outs = call(
         product_kernel,
-        [(1040, LANES)] * 4,
+        [(1040, LANES), (1040, LANES), (1056, LANES), (1040, LANES)],
         (mixed, *received, cc_weight),
         flops=2_200_000_000,
         scratch=[pltpu.VMEM((1024, 1024), BF16)] * 2 + [pltpu.VMEM((1024, 1024), F32)],
@@ -428,8 +443,10 @@
         dtype=[BF16, F32],
     )
     part = exchange(part, "chan")
-    back_sends = call(back_mirror_kernel, [(4, 128, LANES), (4, 128, LANES), (6, 128, LANES)], (part, pp_part), name="back_mirror")
-    back_received = mirror(*back_sends)
+    far = call(back_far_kernel, (528, LANES), (part, pp_part), name="back_far")
+    part, far = lax.optimization_barrier((part, far))
+    near = call(back_near_kernel, [(4, 128, LANES)] * 2, (part, pp_part), name="back_near")
+    back_received = mirror(*near, far)
     return call(finish_kernel, (2, 256, 1024), (part, *back_received, pp_part, edge), name="finish")
 
 

time: 180 us -> 178 us (0.989)
    pallas_call x11 -> x13, Pallas kernels: 15.9 us -> 16 us  [call(): pl.pallas_call(kernel, out_shape=shaped[0] if single else shaped, in_spec...]
where the time goes in v7:
time: 178 us
  waiting for transfers between devices  68.8 us (39%)
  blocking collectives  48.3 us (27%)
  starting transfers between devices  38.8 us (22%)
  Pallas kernels  16 us (9%)
  local copies, waits for them, and re-layouts  5.39 us (3%)
    all_to_all x2, blocking collectives, exchange(): lax.all_to_all(operand, axis, split_axis=0, concat_axis=0, tiled=True)  48.3 us
    ppermute x6, waiting for transfers between devices, step(): return lax.ppermute(value, 'panel', [(i, (i + by) % 4) for i in range(4)])  33.1 us
    ppermute x6, waiting for transfers between devices, route(): return lax.ppermute(value, ('chan', 'panel'), pairs)  22.4 us
    all_to_all x2, starting transfers between devices, exchange(): lax.all_to_all(operand, axis, split_axis=0, concat_axis=0, tiled=True)  19.9 us
    pallas_call x13, Pallas kernels, call(): pl.pallas_call(kernel, out_shape=shaped[0] if single else shaped, in_spec...  16 us
    all_to_all x2, waiting for transfers between devices, exchange(): lax.all_to_all(operand, axis, split_axis=0, concat_axis=0, tiled=True)  13.3 us
    ppermute x6, starting transfers between devices, route(): return lax.ppermute(value, ('chan', 'panel'), pairs)  9.84 us
    ppermute x6, starting transfers between devices, step(): return lax.ppermute(value, 'panel', [(i, (i + by) % 4) for i in range(4)])  9.03 us
  transfers between devices with their start and end apart: 14, of which 9 were waited for; matrix products, arithmetic and copies ran while one was open for 0% of the time, Pallas kernels for 2%

profile of v7, /device:TPU:1, one launch (start us, length us, event | category | flops | bytes accessed | tf_op | source)
XLA Modules:
  0.0 177.5 jit_solution(626728093441184218)
XLA Ops:
  0.0 3.7 %pack.1 = bf16[64,64,128]{2,1,0:T(8,128)(2,1)} custom-call(bf16[2,256,1024]{2,1,0:T(8,128)(2,1)} %eta_ref.3, bf16[2,256,1024]{2,1,0:T(8,128)(2,1)} %gamma_ref.3), custom_call_target="tpu_custom_call" | custom-call | bytes 3145728 | tf_op jit(solution)/shard_map/pack/pallas_call | solution.py:347
  3.8 13.3 %all-to-all-start = ((bf16[64,64,128]{2,1,0:T(8,128)(2,1)}), bf16[64,64,128]{2,1,0:T(8,128)(2,1)S(1)}, u32[]{:S(2)}, u32[]{:S(2)}) async-start(bf16[64,64,128]{2,1,0:T(8,128)(2,1)} %pack.1), calls=%async_computation | async-start | bytes 2097152 | tf_op jit(solution)/shard_map/all_to_all | solution.py:360
  17.2 2.9 %pair.1 = (bf16[2,5,2,128,128]{4,3,2,1,0:T(8,128)(2,1)S(1)}, bf16[2,5,2,128,128]{4,3,2,1,0:T(8,128)(2,1)S(1)}, bf16[2,5,2,128,128]{4,3,2,1,0:T(8,128)(2,1)S(1)}, bf16[2,5,2,128,128]{4,3,2,1,0:T(8,128)(2,1)S(1)}) custom-call(bf16[2,256,1024]{2,1,0:T(8,128)(2,1)S(1)} %copy-done, bf16[2,256,1024]{2,1,0:T(8,128)(2,1)S(1)} %copy-done.1, ...), custom_call_target="tpu_custom_call" | custom-call | flops 2200000000 | bytes 4726784 | tf_op jit(solution)/shard_map/pair/pallas_call | solution.py:347
  22.2 1.4 collective-permute-start.1
  25.2 12.8 %collective-permute-done.plus_ref = bf16[2,5,2,128,128]{4,3,2,1,0:T(8,128)(2,1)S(1)} collective-permute-done((bf16[2,5,2,128,128]{4,3,2,1,0:T(8,128)(2,1)S(1)}, bf16[2,5,2,128,128]{4,3,2,1,0:T(8,128)(2,1)S(1)}, u32[]{:S(2)}, u32[]{:S(2)}) %collective-permute-start) | collective-permute-done | bytes 655392 | tf_op jit(solution)/shard_map/ppermute | solution.py:364
  39.8 5.3 %all-to-all-done.in_ref = bf16[64,64,128]{2,1,0:T(8,128)(2,1)S(1)} async-done(((bf16[64,64,128]{2,1,0:T(8,128)(2,1)}), bf16[64,64,128]{2,1,0:T(8,128)(2,1)S(1)}, u32[]{:S(2)}, u32[]{:S(2)}) %all-to-all-start) | async-done | bytes 1048608 | tf_op jit(solution)/shard_map/all_to_all | solution.py:360
  45.1 1.7 recouple.1
  46.8 6.6 %all-to-all-start.1 = ((bf16[64,64,128]{2,1,0:T(8,128)(2,1)}), bf16[64,64,128]{2,1,0:T(8,128)(2,1)S(1)}, u32[]{:S(2)}, u32[]{:S(2)}) async-start(bf16[64,64,128]{2,1,0:T(8,128)(2,1)} %recouple.1), calls=%async_computation.1 | async-start | bytes 2097152 | tf_op jit(solution)/shard_map/all_to_all | solution.py:360
  53.4 2.8 %collective-permute-start.2 = (bf16[2,5,2,128,128]{4,3,2,1,0:T(8,128)(2,1)S(1)}, bf16[2,5,2,128,128]{4,3,2,1,0:T(8,128)(2,1)S(1)}, u32[]{:S(2)}, u32[]{:S(2)}) collective-permute-start(bf16[2,5,2,128,128]{4,3,2,1,0:T(8,128)(2,1)S(1)} %copy-done.9), channel_id=1, source_target_pairs={{0,2},{1,3},{2,0},{3,1},{4,6},{5,7},{6,4},{7,5},{8,10},{9,11},{10,... | collective-permute-start | bytes 1966088 | tf_op jit(solution)/shard_map/ppermute | solution.py:364
  56.2 14.6 %collective-permute-done.2.far_ref = bf16[2,5,2,128,128]{4,3,2,1,0:T(8,128)(2,1)S(1)} collective-permute-done((bf16[2,5,2,128,128]{4,3,2,1,0:T(8,128)(2,1)S(1)}, bf16[2,5,2,128,128]{4,3,2,1,0:T(8,128)(2,1)S(1)}, u32[]{:S(2)}, u32[]{:S(2)}) %collective-permute-start.2) | collective-permute-done | bytes 655392 | tf_op jit(solution)/shard_map/ppermute | solution.py:364
  73.3 8.0 %all-to-all-done.1.in_ref = bf16[64,64,128]{2,1,0:T(8,128)(2,1)S(1)} async-done(((bf16[64,64,128]{2,1,0:T(8,128)(2,1)}), bf16[64,64,128]{2,1,0:T(8,128)(2,1)S(1)}, u32[]{:S(2)}, u32[]{:S(2)}) %all-to-all-start.1) | async-done | bytes 1048608 | tf_op jit(solution)/shard_map/all_to_all | solution.py:360
  81.5 3.1 %collective-permute-start.3 = (bf16[64,32,128]{2,1,0:T(8,128)(2,1)S(1)}, bf16[64,32,128]{2,1,0:T(8,128)(2,1)S(1)}, u32[]{:S(2)}, u32[]{:S(2)}) collective-permute-start(bf16[64,32,128]{2,1,0:T(8,128)(2,1)S(1)} %get-tuple-element.47), channel_id=1, source_target_pairs={{1,2},{3,0},{6,7},{4,5},{9,10},{11,8},{14,15},{12,13},{17,18},{19,... | collective-permute-start | bytes 1572872 | tf_op jit(solution)/shard_map/ppermute | solution.py:377
  84.6 2.6 %collective-permute-start.4 = (bf16[64,32,128]{2,1,0:T(8,128)(2,1)S(1)}, bf16[64,32,128]{2,1,0:T(8,128)(2,1)S(1)}, u32[]{:S(2)}, u32[]{:S(2)}) collective-permute-start(bf16[64,32,128]{2,1,0:T(8,128)(2,1)S(1)} %get-tuple-element.48), channel_id=1, source_target_pairs={{1,0},{3,2},{6,5},{4,7},{9,8},{11,10},{14,13},{12,15},{17,16},{19,... | collective-permute-start | bytes 1572872 | tf_op jit(solution)/shard_map/ppermute | solution.py:377
  88.1 2.6 %collective-permute-done.3.plus_ref = bf16[64,32,128]{2,1,0:T(8,128)(2,1)S(1)} collective-permute-done((bf16[64,32,128]{2,1,0:T(8,128)(2,1)S(1)}, bf16[64,32,128]{2,1,0:T(8,128)(2,1)S(1)}, u32[]{:S(2)}, u32[]{:S(2)}) %collective-permute-start.3) | collective-permute-done | bytes 524320 | tf_op jit(solution)/shard_map/ppermute | solution.py:377
  90.7 6.4 %collective-permute-done.4.minus_ref = bf16[64,32,128]{2,1,0:T(8,128)(2,1)S(1)} collective-permute-done((bf16[64,32,128]{2,1,0:T(8,128)(2,1)S(1)}, bf16[64,32,128]{2,1,0:T(8,128)(2,1)S(1)}, u32[]{:S(2)}, u32[]{:S(2)}) %collective-permute-start.4) | collective-permute-done | bytes 524320 | tf_op jit(solution)/shard_map/ppermute | solution.py:377
  97.1 3.2 %product.1 = (bf16[1040,128]{1,0:T(8,128)(2,1)S(1)}, bf16[1040,128]{1,0:T(8,128)(2,1)S(1)}, bf16[1056,128]{1,0:T(8,128)(2,1)S(1)}, bf16[1040,128]{1,0:T(8,128)(2,1)S(1)}) custom-call(bf16[64,64,128]{2,1,0:T(8,128)(2,1)S(1)} %all-to-all-done.1.in_ref, bf16[64,32,128]{2,1,0:T(8,128)(2,1)S(1)} %collective-permute-done.3.plus_ref, ...), custom_call_target="tpu_custom_call" | custom-call | flops 2200000000 | bytes 3698688 | tf_op jit(solution)/shard_map/product/pallas_call | solution.py:347
  101.0 1.3 collective-permute-start.6
  103.6 13.3 %collective-permute-done.6.plus_ref = bf16[1040,128]{1,0:T(8,128)(2,1)S(1)} collective-permute-done((bf16[1040,128]{1,0:T(8,128)(2,1)S(1)}, bf16[1040,128]{1,0:T(8,128)(2,1)S(1)}, u32[]{:S(2)}, u32[]{:S(2)}) %collective-permute-start.6) | collective-permute-done | bytes 266272 | tf_op jit(solution)/shard_map/ppermute | solution.py:377
  117.8 24.9 %all_to_all.20.in_ref = bf16[64,40,128]{2,1,0:T(8,128)(2,1)S(1)} all-to-all(bf16[64,40,128]{2,1,0:T(8,128)(2,1)S(1)} %part.1), channel_id=1, replica_groups=mesh['chan'=64,'panel'=4] {'chan'}, dimensions={0} | all-to-all | bytes 1310720 | tf_op jit(solution)/shard_map/all_to_all | solution.py:360
  143.2 23.4 %all_to_all.21.in_ref = bf16[64,32,128]{2,1,0:T(8,128)(2,1)S(1)} all-to-all(bf16[64,32,128]{2,1,0:T(8,128)(2,1)S(1)} %get-tuple-element.54), channel_id=1, replica_groups=mesh['chan'=64,'panel'=4] {'chan'}, dimensions={0} | all-to-all | bytes 1048576 | tf_op jit(solution)/shard_map/all_to_all | solution.py:360
  166.7 1.8 %collective-permute-start.11 = (bf16[528,128]{1,0:T(8,128)(2,1)S(1)}, bf16[528,128]{1,0:T(8,128)(2,1)S(1)}, u32[]{:S(2)}, u32[]{:S(2)}) collective-permute-start(bf16[528,128]{1,0:T(8,128)(2,1)S(1)} %back_far.1), channel_id=1, source_target_pairs={{0,2},{1,3},{2,0},{3,1},{4,6},{5,7},{6,4},{7,5},{8,10},{9,11},{10,... | collective-permute-start | bytes 405512 | tf_op jit(solution)/shard_map/ppermute | solution.py:364
  168.7 1.7 collective-permute-start.10
  170.4 5.2 %collective-permute-done.10.minus_ref = bf16[4,128,128]{2,1,0:T(8,128)(2,1)S(1)} collective-permute-done((bf16[4,128,128]{2,1,0:T(8,128)(2,1)S(1)}, bf16[4,128,128]{2,1,0:T(8,128)(2,1)S(1)}, u32[]{:S(2)}, u32[]{:S(2)}) %collective-permute-start.10) | collective-permute-done | bytes 131104 | tf_op jit(solution)/shard_map/ppermute | solution.py:364
  176.0 1.5 finish.1
  (54 shorter events, 12.9 us)
Async XLA Ops:
  0.0 17.1 %copy-start.15 = (f32[2,1024]{1,0:T(2,128)S(1)}, f32[2,1024]{1,0:T(2,128)}, u32[]{:S(2)}) copy-start(f32[2,1024]{1,0:T(2,128)} %param.9) | copy-start | bytes 24580
  0.0 17.1 %copy-start.16 = (s32[2]{0:T(128)S(1)}, s32[2]{0:T(128)}, u32[]{:S(2)}) copy-start(s32[2]{0:T(128)} %param.11) | copy-start | bytes 28
  3.7 13.4 %copy-start = (bf16[2,256,1024]{2,1,0:T(8,128)(2,1)S(1)}, bf16[2,256,1024]{2,1,0:T(8,128)(2,1)}, u32[]{:S(2)}) copy-start(bf16[2,256,1024]{2,1,0:T(8,128)(2,1)} %eta_ref.3) | copy-start | bytes 3145732
  3.8 13.4 %copy-start.1 = (bf16[2,256,1024]{2,1,0:T(8,128)(2,1)S(1)}, bf16[2,256,1024]{2,1,0:T(8,128)(2,1)}, u32[]{:S(2)}) copy-start(bf16[2,256,1024]{2,1,0:T(8,128)(2,1)} %gamma_ref.3) | copy-start | bytes 3145732
  3.8 41.3 %all-to-all-start = ((bf16[64,64,128]{2,1,0:T(8,128)(2,1)}), bf16[64,64,128]{2,1,0:T(8,128)(2,1)S(1)}, u32[]{:S(2)}, u32[]{:S(2)}) async-start(bf16[64,64,128]{2,1,0:T(8,128)(2,1)} %pack.1), calls=%async_computation | async-start | bytes 2097152 | tf_op jit(solution)/shard_map/all_to_all | solution.py:360
  17.2 6.5 %copy-start.10 = (bf16[128,128]{1,0:T(8,128)(2,1)S(1)}, bf16[128,128]{1,0:T(8,128)(2,1)}, u32[]{:S(2)}) copy-start(bf16[128,128]{1,0:T(8,128)(2,1)} %forward_ref.1) | copy-start | bytes 98308
  21.0 17.1 %copy-start.2 = (bf16[2,5,2,128,128]{4,3,2,1,0:T(8,128)(2,1)}, bf16[2,5,2,128,128]{4,3,2,1,0:T(8,128)(2,1)S(1)}, u32[]{:S(2)}) copy-start(bf16[2,5,2,128,128]{4,3,2,1,0:T(8,128)(2,1)S(1)} %get-tuple-element.41.own_ref) | copy-start | bytes 1966084
  21.0 17.1 %collective-permute-start = (bf16[2,5,2,128,128]{4,3,2,1,0:T(8,128)(2,1)S(1)}, bf16[2,5,2,128,128]{4,3,2,1,0:T(8,128)(2,1)S(1)}, u32[]{:S(2)}, u32[]{:S(2)}) collective-permute-start(bf16[2,5,2,128,128]{4,3,2,1,0:T(8,128)(2,1)S(1)} %get-tuple-element.38), channel_id=1, source_target_pairs={{0,1},{1,2},{2,3},{3,0},{4,5},{5,6},{6,7},{7,4},{8,9},{9,10},{10,1... | collective-permute-start | bytes 1966088 | tf_op jit(solution)/shard_map/ppermute | solution.py:364
  22.2 16.7 %collective-permute-start.1 = (bf16[2,5,2,128,128]{4,3,2,1,0:T(8,128)(2,1)S(1)}, bf16[2,5,2,128,128]{4,3,2,1,0:T(8,128)(2,1)S(1)}, u32[]{:S(2)}, u32[]{:S(2)}) collective-permute-start(bf16[2,5,2,128,128]{4,3,2,1,0:T(8,128)(2,1)S(1)} %get-tuple-element.39), channel_id=1, source_target_pairs={{0,3},{1,0},{2,1},{3,2},{4,7},{5,4},{6,5},{7,6},{8,11},{9,8},{10,9... | collective-permute-start | bytes 1966088 | tf_op jit(solution)/shard_map/ppermute | solution.py:364
  46.7 6.6 %copy-start.9 = (bf16[2,5,2,128,128]{4,3,2,1,0:T(8,128)(2,1)S(1)}, bf16[2,5,2,128,128]{4,3,2,1,0:T(8,128)(2,1)}, u32[]{:S(2)}) copy-start(bf16[2,5,2,128,128]{4,3,2,1,0:T(8,128)(2,1)} %copy-done.8) | copy-start | bytes 1966084
  46.8 24.1 %copy-start.3 = (bf16[2,5,2,128,128]{4,3,2,1,0:T(8,128)(2,1)S(1)}, bf16[2,5,2,128,128]{4,3,2,1,0:T(8,128)(2,1)}, u32[]{:S(2)}) copy-start(bf16[2,5,2,128,128]{4,3,2,1,0:T(8,128)(2,1)} %copy-done.2) | copy-start | bytes 1966084
  46.8 34.6 %all-to-all-start.1 = ((bf16[64,64,128]{2,1,0:T(8,128)(2,1)}), bf16[64,64,128]{2,1,0:T(8,128)(2,1)S(1)}, u32[]{:S(2)}, u32[]{:S(2)}) async-start(bf16[64,64,128]{2,1,0:T(8,128)(2,1)} %recouple.1), calls=%async_computation.1 | async-start | bytes 2097152 | tf_op jit(solution)/shard_map/all_to_all | solution.py:360
  53.4 17.4 %collective-permute-start.2 = (bf16[2,5,2,128,128]{4,3,2,1,0:T(8,128)(2,1)S(1)}, bf16[2,5,2,128,128]{4,3,2,1,0:T(8,128)(2,1)S(1)}, u32[]{:S(2)}, u32[]{:S(2)}) collective-permute-start(bf16[2,5,2,128,128]{4,3,2,1,0:T(8,128)(2,1)S(1)} %copy-done.9), channel_id=1, source_target_pairs={{0,2},{1,3},{2,0},{3,1},{4,6},{5,7},{6,4},{7,5},{8,10},{9,11},{10,... | collective-permute-start | bytes 1966088 | tf_op jit(solution)/shard_map/ppermute | solution.py:364
  73.3 23.9 %copy-start.12 = (f32[2,1024]{1,0:T(2,128)S(1)}, f32[2,1024]{1,0:T(2,128)}, u32[]{:S(2)}) copy-start(f32[2,1024]{1,0:T(2,128)} %weight_ref.1) | copy-start | bytes 24580
  81.5 9.2 %collective-permute-start.3 = (bf16[64,32,128]{2,1,0:T(8,128)(2,1)S(1)}, bf16[64,32,128]{2,1,0:T(8,128)(2,1)S(1)}, u32[]{:S(2)}, u32[]{:S(2)}) collective-permute-start(bf16[64,32,128]{2,1,0:T(8,128)(2,1)S(1)} %get-tuple-element.47), channel_id=1, source_target_pairs={{1,2},{3,0},{6,7},{4,5},{9,10},{11,8},{14,15},{12,13},{17,18},{19,... | collective-permute-start | bytes 1572872 | tf_op jit(solution)/shard_map/ppermute | solution.py:377
  84.6 12.5 %collective-permute-start.4 = (bf16[64,32,128]{2,1,0:T(8,128)(2,1)S(1)}, bf16[64,32,128]{2,1,0:T(8,128)(2,1)S(1)}, u32[]{:S(2)}, u32[]{:S(2)}) collective-permute-start(bf16[64,32,128]{2,1,0:T(8,128)(2,1)S(1)} %get-tuple-element.48), channel_id=1, source_target_pairs={{1,0},{3,2},{6,5},{4,7},{9,8},{11,10},{14,13},{12,15},{17,16},{19,... | collective-permute-start | bytes 1572872 | tf_op jit(solution)/shard_map/ppermute | solution.py:377
  87.2 10.0 %collective-permute-start.5 = (bf16[64,32,128]{2,1,0:T(8,128)(2,1)S(1)}, bf16[64,32,128]{2,1,0:T(8,128)(2,1)S(1)}, u32[]{:S(2)}, u32[]{:S(2)}) collective-permute-start(bf16[64,32,128]{2,1,0:T(8,128)(2,1)S(1)} %send_far.1), channel_id=1, source_target_pairs={{0,2},{2,0},{5,7},{7,5},{8,10},{10,8},{13,15},{15,13},{16,18},{18,... | collective-permute-start | bytes 1572872 | tf_op jit(solution)/shard_map/ppermute | solution.py:377
  100.3 16.6 %collective-permute-start.7 = (bf16[1056,128]{1,0:T(8,128)(2,1)S(1)}, bf16[1056,128]{1,0:T(8,128)(2,1)S(1)}, u32[]{:S(2)}, u32[]{:S(2)}) collective-permute-start(bf16[1056,128]{1,0:T(8,128)(2,1)S(1)} %get-tuple-element.52), channel_id=1, source_target_pairs={{0,2},{2,0},{5,7},{7,5},{8,10},{10,8},{13,15},{15,13},{16,18},{18,... | collective-permute-start | bytes 811016 | tf_op jit(solution)/shard_map/ppermute | solution.py:377
  101.0 15.9 %collective-permute-start.6 = (bf16[1040,128]{1,0:T(8,128)(2,1)S(1)}, bf16[1040,128]{1,0:T(8,128)(2,1)S(1)}, u32[]{:S(2)}, u32[]{:S(2)}) collective-permute-start(bf16[1040,128]{1,0:T(8,128)(2,1)S(1)} %get-tuple-element.51), channel_id=1, source_target_pairs={{0,1},{2,3},{5,6},{7,4},{8,9},{10,11},{13,14},{15,12},{16,17},{18,... | collective-permute-start | bytes 798728 | tf_op jit(solution)/shard_map/ppermute | solution.py:377
  102.3 14.6 %collective-permute-start.8 = (bf16[1040,128]{1,0:T(8,128)(2,1)S(1)}, bf16[1040,128]{1,0:T(8,128)(2,1)S(1)}, u32[]{:S(2)}, u32[]{:S(2)}) collective-permute-start(bf16[1040,128]{1,0:T(8,128)(2,1)S(1)} %get-tuple-element.53), channel_id=1, source_target_pairs={{0,3},{2,1},{5,4},{7,6},{8,11},{10,9},{13,12},{15,14},{16,19},{18,... | collective-permute-start | bytes 798728 | tf_op jit(solution)/shard_map/ppermute | solution.py:377
  116.9 25.7 %copy-start.14 = (bf16[256,256]{1,0:T(8,128)(2,1)S(1)}, bf16[256,256]{1,0:T(8,128)(2,1)}, u32[]{:S(2)}) copy-start(bf16[256,256]{1,0:T(8,128)(2,1)} %copy-done.13) | copy-start | bytes 393220
  166.7 9.4 %collective-permute-start.11 = (bf16[528,128]{1,0:T(8,128)(2,1)S(1)}, bf16[528,128]{1,0:T(8,128)(2,1)S(1)}, u32[]{:S(2)}, u32[]{:S(2)}) collective-permute-start(bf16[528,128]{1,0:T(8,128)(2,1)S(1)} %back_far.1), channel_id=1, source_target_pairs={{0,2},{1,3},{2,0},{3,1},{4,6},{5,7},{6,4},{7,5},{8,10},{9,11},{10,... | collective-permute-start | bytes 405512 | tf_op jit(solution)/shard_map/ppermute | solution.py:364
  168.7 6.9 %collective-permute-start.10 = (bf16[4,128,128]{2,1,0:T(8,128)(2,1)S(1)}, bf16[4,128,128]{2,1,0:T(8,128)(2,1)S(1)}, u32[]{:S(2)}, u32[]{:S(2)}) collective-permute-start(bf16[4,128,128]{2,1,0:T(8,128)(2,1)S(1)} %get-tuple-element.58), channel_id=1, source_target_pairs={{0,3},{1,0},{2,1},{3,2},{4,7},{5,4},{6,5},{7,6},{8,11},{9,8},{10,9... | collective-permute-start | bytes 393224 | tf_op jit(solution)/shard_map/ppermute | solution.py:364
  170.4 5.6 %collective-permute-start.9 = (bf16[4,128,128]{2,1,0:T(8,128)(2,1)S(1)}, bf16[4,128,128]{2,1,0:T(8,128)(2,1)S(1)}, u32[]{:S(2)}, u32[]{:S(2)}) collective-permute-start(bf16[4,128,128]{2,1,0:T(8,128)(2,1)S(1)} %get-tuple-element.57), channel_id=1, source_target_pairs={{0,1},{1,2},{2,3},{3,0},{4,5},{5,6},{6,7},{7,4},{8,9},{9,10},{10,1... | collective-permute-start | bytes 393224 | tf_op jit(solution)/shard_map/ppermute | solution.py:364
  (7 other events, 11.9 us)

commit v8 on v7

--- a/solution.py
+++ b/solution.py
@@ -250,7 +250,7 @@
 
 def recouple_back_kernel(table_ref, edge_table_ref, in_ref, out_ref, edge_ref, mixed):
     out_ref[...] = jnp.concatenate(recouple_rows(table_ref, in_ref, 4), axis=1).astype(BF16)
-    edges = in_ref[:, 32:40, :].astype(F32).reshape(32, 2, 8, LANES)
+    edges = in_ref[...].astype(F32)[:, 32:40].reshape(32, 2, 8, LANES)
     edges = jnp.concatenate([edges[:, 0, :4], edges[:, 1, :4]], axis=1).reshape(256, LANES).astype(BF16)
     mixed[...] = jnp.dot(edge_table_ref[...], edges, preferred_element_type=F32).astype(BF16).astype(F32)
     edge_ref[...] = mixed[pl.ds(pl.multiple_of(lax.axis_index("chan") * 4, 4), 4), :]

time: 178 us -> 178 us (level)
  no operation moved by 1% of the time
where the time goes in v8:
time: 178 us
  waiting for transfers between devices  68.8 us (39%)
  blocking collectives  48.3 us (27%)
  starting transfers between devices  38.8 us (22%)
  Pallas kernels  16 us (9%)
  local copies, waits for them, and re-layouts  5.39 us (3%)
    all_to_all x2, blocking collectives, exchange(): lax.all_to_all(operand, axis, split_axis=0, concat_axis=0, tiled=True)  48.3 us
    ppermute x6, waiting for transfers between devices, step(): return lax.ppermute(value, 'panel', [(i, (i + by) % 4) for i in range(4)])  33.1 us
    ppermute x6, waiting for transfers between devices, route(): return lax.ppermute(value, ('chan', 'panel'), pairs)  22.4 us
    all_to_all x2, starting transfers between devices, exchange(): lax.all_to_all(operand, axis, split_axis=0, concat_axis=0, tiled=True)  19.9 us
    pallas_call x13, Pallas kernels, call(): pl.pallas_call(kernel, out_shape=shaped[0] if single else shaped, in_spec...  16 us
    all_to_all x2, waiting for transfers between devices, exchange(): lax.all_to_all(operand, axis, split_axis=0, concat_axis=0, tiled=True)  13.3 us
    ppermute x6, starting transfers between devices, route(): return lax.ppermute(value, ('chan', 'panel'), pairs)  9.84 us
    ppermute x6, starting transfers between devices, step(): return lax.ppermute(value, 'panel', [(i, (i + by) % 4) for i in range(4)])  9.03 us
  transfers between devices with their start and end apart: 14, of which 9 were waited for; matrix products, arithmetic and copies ran while one was open for 0% of the time, Pallas kernels for 2%

profile of v8, /device:TPU:1, one launch (start us, length us, event | category | flops | bytes accessed | tf_op | source)
XLA Modules:
  0.0 177.5 jit_solution(626728093441184218)
XLA Ops:
  0.0 3.7 %pack.1 = bf16[64,64,128]{2,1,0:T(8,128)(2,1)} custom-call(bf16[2,256,1024]{2,1,0:T(8,128)(2,1)} %eta_ref.3, bf16[2,256,1024]{2,1,0:T(8,128)(2,1)} %gamma_ref.3), custom_call_target="tpu_custom_call" | custom-call | bytes 3145728 | tf_op jit(solution)/shard_map/pack/pallas_call | solution.py:347
  3.8 13.3 %all-to-all-start = ((bf16[64,64,128]{2,1,0:T(8,128)(2,1)}), bf16[64,64,128]{2,1,0:T(8,128)(2,1)S(1)}, u32[]{:S(2)}, u32[]{:S(2)}) async-start(bf16[64,64,128]{2,1,0:T(8,128)(2,1)} %pack.1), calls=%async_computation | async-start | bytes 2097152 | tf_op jit(solution)/shard_map/all_to_all | solution.py:360
  17.2 2.9 %pair.1 = (bf16[2,5,2,128,128]{4,3,2,1,0:T(8,128)(2,1)S(1)}, bf16[2,5,2,128,128]{4,3,2,1,0:T(8,128)(2,1)S(1)}, bf16[2,5,2,128,128]{4,3,2,1,0:T(8,128)(2,1)S(1)}, bf16[2,5,2,128,128]{4,3,2,1,0:T(8,128)(2,1)S(1)}) custom-call(bf16[2,256,1024]{2,1,0:T(8,128)(2,1)S(1)} %copy-done, bf16[2,256,1024]{2,1,0:T(8,128)(2,1)S(1)} %copy-done.1, ...), custom_call_target="tpu_custom_call" | custom-call | flops 2200000000 | bytes 4726784 | tf_op jit(solution)/shard_map/pair/pallas_call | solution.py:347
  22.2 1.4 collective-permute-start.1
  25.2 12.8 %collective-permute-done.plus_ref = bf16[2,5,2,128,128]{4,3,2,1,0:T(8,128)(2,1)S(1)} collective-permute-done((bf16[2,5,2,128,128]{4,3,2,1,0:T(8,128)(2,1)S(1)}, bf16[2,5,2,128,128]{4,3,2,1,0:T(8,128)(2,1)S(1)}, u32[]{:S(2)}, u32[]{:S(2)}) %collective-permute-start) | collective-permute-done | bytes 655392 | tf_op jit(solution)/shard_map/ppermute | solution.py:364
  39.8 5.3 %all-to-all-done.in_ref = bf16[64,64,128]{2,1,0:T(8,128)(2,1)S(1)} async-done(((bf16[64,64,128]{2,1,0:T(8,128)(2,1)}), bf16[64,64,128]{2,1,0:T(8,128)(2,1)S(1)}, u32[]{:S(2)}, u32[]{:S(2)}) %all-to-all-start) | async-done | bytes 1048608 | tf_op jit(solution)/shard_map/all_to_all | solution.py:360
  45.1 1.7 recouple.1
  46.8 6.6 %all-to-all-start.1 = ((bf16[64,64,128]{2,1,0:T(8,128)(2,1)}), bf16[64,64,128]{2,1,0:T(8,128)(2,1)S(1)}, u32[]{:S(2)}, u32[]{:S(2)}) async-start(bf16[64,64,128]{2,1,0:T(8,128)(2,1)} %recouple.1), calls=%async_computation.1 | async-start | bytes 2097152 | tf_op jit(solution)/shard_map/all_to_all | solution.py:360
  53.4 2.8 %collective-permute-start.2 = (bf16[2,5,2,128,128]{4,3,2,1,0:T(8,128)(2,1)S(1)}, bf16[2,5,2,128,128]{4,3,2,1,0:T(8,128)(2,1)S(1)}, u32[]{:S(2)}, u32[]{:S(2)}) collective-permute-start(bf16[2,5,2,128,128]{4,3,2,1,0:T(8,128)(2,1)S(1)} %copy-done.9), channel_id=1, source_target_pairs={{0,2},{1,3},{2,0},{3,1},{4,6},{5,7},{6,4},{7,5},{8,10},{9,11},{10,... | collective-permute-start | bytes 1966088 | tf_op jit(solution)/shard_map/ppermute | solution.py:364
  56.2 14.6 %collective-permute-done.2.far_ref = bf16[2,5,2,128,128]{4,3,2,1,0:T(8,128)(2,1)S(1)} collective-permute-done((bf16[2,5,2,128,128]{4,3,2,1,0:T(8,128)(2,1)S(1)}, bf16[2,5,2,128,128]{4,3,2,1,0:T(8,128)(2,1)S(1)}, u32[]{:S(2)}, u32[]{:S(2)}) %collective-permute-start.2) | collective-permute-done | bytes 655392 | tf_op jit(solution)/shard_map/ppermute | solution.py:364
  73.3 8.0 %all-to-all-done.1.in_ref = bf16[64,64,128]{2,1,0:T(8,128)(2,1)S(1)} async-done(((bf16[64,64,128]{2,1,0:T(8,128)(2,1)}), bf16[64,64,128]{2,1,0:T(8,128)(2,1)S(1)}, u32[]{:S(2)}, u32[]{:S(2)}) %all-to-all-start.1) | async-done | bytes 1048608 | tf_op jit(solution)/shard_map/all_to_all | solution.py:360
  81.5 3.1 %collective-permute-start.3 = (bf16[64,32,128]{2,1,0:T(8,128)(2,1)S(1)}, bf16[64,32,128]{2,1,0:T(8,128)(2,1)S(1)}, u32[]{:S(2)}, u32[]{:S(2)}) collective-permute-start(bf16[64,32,128]{2,1,0:T(8,128)(2,1)S(1)} %get-tuple-element.47), channel_id=1, source_target_pairs={{1,2},{3,0},{6,7},{4,5},{9,10},{11,8},{14,15},{12,13},{17,18},{19,... | collective-permute-start | bytes 1572872 | tf_op jit(solution)/shard_map/ppermute | solution.py:377
  84.6 2.6 %collective-permute-start.4 = (bf16[64,32,128]{2,1,0:T(8,128)(2,1)S(1)}, bf16[64,32,128]{2,1,0:T(8,128)(2,1)S(1)}, u32[]{:S(2)}, u32[]{:S(2)}) collective-permute-start(bf16[64,32,128]{2,1,0:T(8,128)(2,1)S(1)} %get-tuple-element.48), channel_id=1, source_target_pairs={{1,0},{3,2},{6,5},{4,7},{9,8},{11,10},{14,13},{12,15},{17,16},{19,... | collective-permute-start | bytes 1572872 | tf_op jit(solution)/shard_map/ppermute | solution.py:377
  88.1 2.6 %collective-permute-done.3.plus_ref = bf16[64,32,128]{2,1,0:T(8,128)(2,1)S(1)} collective-permute-done((bf16[64,32,128]{2,1,0:T(8,128)(2,1)S(1)}, bf16[64,32,128]{2,1,0:T(8,128)(2,1)S(1)}, u32[]{:S(2)}, u32[]{:S(2)}) %collective-permute-start.3) | collective-permute-done | bytes 524320 | tf_op jit(solution)/shard_map/ppermute | solution.py:377
  90.7 6.4 %collective-permute-done.4.minus_ref = bf16[64,32,128]{2,1,0:T(8,128)(2,1)S(1)} collective-permute-done((bf16[64,32,128]{2,1,0:T(8,128)(2,1)S(1)}, bf16[64,32,128]{2,1,0:T(8,128)(2,1)S(1)}, u32[]{:S(2)}, u32[]{:S(2)}) %collective-permute-start.4) | collective-permute-done | bytes 524320 | tf_op jit(solution)/shard_map/ppermute | solution.py:377
  97.1 3.2 %product.1 = (bf16[1040,128]{1,0:T(8,128)(2,1)S(1)}, bf16[1040,128]{1,0:T(8,128)(2,1)S(1)}, bf16[1056,128]{1,0:T(8,128)(2,1)S(1)}, bf16[1040,128]{1,0:T(8,128)(2,1)S(1)}) custom-call(bf16[64,64,128]{2,1,0:T(8,128)(2,1)S(1)} %all-to-all-done.1.in_ref, bf16[64,32,128]{2,1,0:T(8,128)(2,1)S(1)} %collective-permute-done.3.plus_ref, ...), custom_call_target="tpu_custom_call" | custom-call | flops 2200000000 | bytes 3698688 | tf_op jit(solution)/shard_map/product/pallas_call | solution.py:347
  101.0 1.3 collective-permute-start.6
  103.6 13.3 %collective-permute-done.6.plus_ref = bf16[1040,128]{1,0:T(8,128)(2,1)S(1)} collective-permute-done((bf16[1040,128]{1,0:T(8,128)(2,1)S(1)}, bf16[1040,128]{1,0:T(8,128)(2,1)S(1)}, u32[]{:S(2)}, u32[]{:S(2)}) %collective-permute-start.6) | collective-permute-done | bytes 266272 | tf_op jit(solution)/shard_map/ppermute | solution.py:377
  117.8 24.9 %all_to_all.20.in_ref = bf16[64,40,128]{2,1,0:T(8,128)(2,1)S(1)} all-to-all(bf16[64,40,128]{2,1,0:T(8,128)(2,1)S(1)} %part.1), channel_id=1, replica_groups=mesh['chan'=64,'panel'=4] {'chan'}, dimensions={0} | all-to-all | bytes 1310720 | tf_op jit(solution)/shard_map/all_to_all | solution.py:360
  143.2 23.4 %all_to_all.21.in_ref = bf16[64,32,128]{2,1,0:T(8,128)(2,1)S(1)} all-to-all(bf16[64,32,128]{2,1,0:T(8,128)(2,1)S(1)} %get-tuple-element.54), channel_id=1, replica_groups=mesh['chan'=64,'panel'=4] {'chan'}, dimensions={0} | all-to-all | bytes 1048576 | tf_op jit(solution)/shard_map/all_to_all | solution.py:360
  166.7 1.8 %collective-permute-start.11 = (bf16[528,128]{1,0:T(8,128)(2,1)S(1)}, bf16[528,128]{1,0:T(8,128)(2,1)S(1)}, u32[]{:S(2)}, u32[]{:S(2)}) collective-permute-start(bf16[528,128]{1,0:T(8,128)(2,1)S(1)} %back_far.1), channel_id=1, source_target_pairs={{0,2},{1,3},{2,0},{3,1},{4,6},{5,7},{6,4},{7,5},{8,10},{9,11},{10,... | collective-permute-start | bytes 405512 | tf_op jit(solution)/shard_map/ppermute | solution.py:364
  168.7 1.7 collective-permute-start.10
  170.4 5.2 %collective-permute-done.10.minus_ref = bf16[4,128,128]{2,1,0:T(8,128)(2,1)S(1)} collective-permute-done((bf16[4,128,128]{2,1,0:T(8,128)(2,1)S(1)}, bf16[4,128,128]{2,1,0:T(8,128)(2,1)S(1)}, u32[]{:S(2)}, u32[]{:S(2)}) %collective-permute-start.10) | collective-permute-done | bytes 131104 | tf_op jit(solution)/shard_map/ppermute | solution.py:364
  176.0 1.5 finish.1
  (54 shorter events, 12.9 us)
Async XLA Ops:
  0.0 17.1 %copy-start.15 = (f32[2,1024]{1,0:T(2,128)S(1)}, f32[2,1024]{1,0:T(2,128)}, u32[]{:S(2)}) copy-start(f32[2,1024]{1,0:T(2,128)} %param.9) | copy-start | bytes 24580
  0.0 17.1 %copy-start.16 = (s32[2]{0:T(128)S(1)}, s32[2]{0:T(128)}, u32[]{:S(2)}) copy-start(s32[2]{0:T(128)} %param.11) | copy-start | bytes 28
  3.7 13.4 %copy-start = (bf16[2,256,1024]{2,1,0:T(8,128)(2,1)S(1)}, bf16[2,256,1024]{2,1,0:T(8,128)(2,1)}, u32[]{:S(2)}) copy-start(bf16[2,256,1024]{2,1,0:T(8,128)(2,1)} %eta_ref.3) | copy-start | bytes 3145732
  3.8 13.4 %copy-start.1 = (bf16[2,256,1024]{2,1,0:T(8,128)(2,1)S(1)}, bf16[2,256,1024]{2,1,0:T(8,128)(2,1)}, u32[]{:S(2)}) copy-start(bf16[2,256,1024]{2,1,0:T(8,128)(2,1)} %gamma_ref.3) | copy-start | bytes 3145732
  3.8 41.3 %all-to-all-start = ((bf16[64,64,128]{2,1,0:T(8,128)(2,1)}), bf16[64,64,128]{2,1,0:T(8,128)(2,1)S(1)}, u32[]{:S(2)}, u32[]{:S(2)}) async-start(bf16[64,64,128]{2,1,0:T(8,128)(2,1)} %pack.1), calls=%async_computation | async-start | bytes 2097152 | tf_op jit(solution)/shard_map/all_to_all | solution.py:360
  17.2 6.5 %copy-start.10 = (bf16[128,128]{1,0:T(8,128)(2,1)S(1)}, bf16[128,128]{1,0:T(8,128)(2,1)}, u32[]{:S(2)}) copy-start(bf16[128,128]{1,0:T(8,128)(2,1)} %forward_ref.1) | copy-start | bytes 98308
  21.0 17.1 %copy-start.2 = (bf16[2,5,2,128,128]{4,3,2,1,0:T(8,128)(2,1)}, bf16[2,5,2,128,128]{4,3,2,1,0:T(8,128)(2,1)S(1)}, u32[]{:S(2)}) copy-start(bf16[2,5,2,128,128]{4,3,2,1,0:T(8,128)(2,1)S(1)} %get-tuple-element.41.own_ref) | copy-start | bytes 1966084
  21.0 17.1 %collective-permute-start = (bf16[2,5,2,128,128]{4,3,2,1,0:T(8,128)(2,1)S(1)}, bf16[2,5,2,128,128]{4,3,2,1,0:T(8,128)(2,1)S(1)}, u32[]{:S(2)}, u32[]{:S(2)}) collective-permute-start(bf16[2,5,2,128,128]{4,3,2,1,0:T(8,128)(2,1)S(1)} %get-tuple-element.38), channel_id=1, source_target_pairs={{0,1},{1,2},{2,3},{3,0},{4,5},{5,6},{6,7},{7,4},{8,9},{9,10},{10,1... | collective-permute-start | bytes 1966088 | tf_op jit(solution)/shard_map/ppermute | solution.py:364
  22.2 16.7 %collective-permute-start.1 = (bf16[2,5,2,128,128]{4,3,2,1,0:T(8,128)(2,1)S(1)}, bf16[2,5,2,128,128]{4,3,2,1,0:T(8,128)(2,1)S(1)}, u32[]{:S(2)}, u32[]{:S(2)}) collective-permute-start(bf16[2,5,2,128,128]{4,3,2,1,0:T(8,128)(2,1)S(1)} %get-tuple-element.39), channel_id=1, source_target_pairs={{0,3},{1,0},{2,1},{3,2},{4,7},{5,4},{6,5},{7,6},{8,11},{9,8},{10,9... | collective-permute-start | bytes 1966088 | tf_op jit(solution)/shard_map/ppermute | solution.py:364
  46.7 6.6 %copy-start.9 = (bf16[2,5,2,128,128]{4,3,2,1,0:T(8,128)(2,1)S(1)}, bf16[2,5,2,128,128]{4,3,2,1,0:T(8,128)(2,1)}, u32[]{:S(2)}) copy-start(bf16[2,5,2,128,128]{4,3,2,1,0:T(8,128)(2,1)} %copy-done.8) | copy-start | bytes 1966084
  46.8 24.1 %copy-start.3 = (bf16[2,5,2,128,128]{4,3,2,1,0:T(8,128)(2,1)S(1)}, bf16[2,5,2,128,128]{4,3,2,1,0:T(8,128)(2,1)}, u32[]{:S(2)}) copy-start(bf16[2,5,2,128,128]{4,3,2,1,0:T(8,128)(2,1)} %copy-done.2) | copy-start | bytes 1966084
  46.8 34.6 %all-to-all-start.1 = ((bf16[64,64,128]{2,1,0:T(8,128)(2,1)}), bf16[64,64,128]{2,1,0:T(8,128)(2,1)S(1)}, u32[]{:S(2)}, u32[]{:S(2)}) async-start(bf16[64,64,128]{2,1,0:T(8,128)(2,1)} %recouple.1), calls=%async_computation.1 | async-start | bytes 2097152 | tf_op jit(solution)/shard_map/all_to_all | solution.py:360
  53.4 17.4 %collective-permute-start.2 = (bf16[2,5,2,128,128]{4,3,2,1,0:T(8,128)(2,1)S(1)}, bf16[2,5,2,128,128]{4,3,2,1,0:T(8,128)(2,1)S(1)}, u32[]{:S(2)}, u32[]{:S(2)}) collective-permute-start(bf16[2,5,2,128,128]{4,3,2,1,0:T(8,128)(2,1)S(1)} %copy-done.9), channel_id=1, source_target_pairs={{0,2},{1,3},{2,0},{3,1},{4,6},{5,7},{6,4},{7,5},{8,10},{9,11},{10,... | collective-permute-start | bytes 1966088 | tf_op jit(solution)/shard_map/ppermute | solution.py:364
  73.3 23.9 %copy-start.12 = (f32[2,1024]{1,0:T(2,128)S(1)}, f32[2,1024]{1,0:T(2,128)}, u32[]{:S(2)}) copy-start(f32[2,1024]{1,0:T(2,128)} %weight_ref.1) | copy-start | bytes 24580
  81.5 9.2 %collective-permute-start.3 = (bf16[64,32,128]{2,1,0:T(8,128)(2,1)S(1)}, bf16[64,32,128]{2,1,0:T(8,128)(2,1)S(1)}, u32[]{:S(2)}, u32[]{:S(2)}) collective-permute-start(bf16[64,32,128]{2,1,0:T(8,128)(2,1)S(1)} %get-tuple-element.47), channel_id=1, source_target_pairs={{1,2},{3,0},{6,7},{4,5},{9,10},{11,8},{14,15},{12,13},{17,18},{19,... | collective-permute-start | bytes 1572872 | tf_op jit(solution)/shard_map/ppermute | solution.py:377
  84.6 12.5 %collective-permute-start.4 = (bf16[64,32,128]{2,1,0:T(8,128)(2,1)S(1)}, bf16[64,32,128]{2,1,0:T(8,128)(2,1)S(1)}, u32[]{:S(2)}, u32[]{:S(2)}) collective-permute-start(bf16[64,32,128]{2,1,0:T(8,128)(2,1)S(1)} %get-tuple-element.48), channel_id=1, source_target_pairs={{1,0},{3,2},{6,5},{4,7},{9,8},{11,10},{14,13},{12,15},{17,16},{19,... | collective-permute-start | bytes 1572872 | tf_op jit(solution)/shard_map/ppermute | solution.py:377
  87.2 10.0 %collective-permute-start.5 = (bf16[64,32,128]{2,1,0:T(8,128)(2,1)S(1)}, bf16[64,32,128]{2,1,0:T(8,128)(2,1)S(1)}, u32[]{:S(2)}, u32[]{:S(2)}) collective-permute-start(bf16[64,32,128]{2,1,0:T(8,128)(2,1)S(1)} %send_far.1), channel_id=1, source_target_pairs={{0,2},{2,0},{5,7},{7,5},{8,10},{10,8},{13,15},{15,13},{16,18},{18,... | collective-permute-start | bytes 1572872 | tf_op jit(solution)/shard_map/ppermute | solution.py:377
  100.3 16.6 %collective-permute-start.7 = (bf16[1056,128]{1,0:T(8,128)(2,1)S(1)}, bf16[1056,128]{1,0:T(8,128)(2,1)S(1)}, u32[]{:S(2)}, u32[]{:S(2)}) collective-permute-start(bf16[1056,128]{1,0:T(8,128)(2,1)S(1)} %get-tuple-element.52), channel_id=1, source_target_pairs={{0,2},{2,0},{5,7},{7,5},{8,10},{10,8},{13,15},{15,13},{16,18},{18,... | collective-permute-start | bytes 811016 | tf_op jit(solution)/shard_map/ppermute | solution.py:377
  101.0 15.9 %collective-permute-start.6 = (bf16[1040,128]{1,0:T(8,128)(2,1)S(1)}, bf16[1040,128]{1,0:T(8,128)(2,1)S(1)}, u32[]{:S(2)}, u32[]{:S(2)}) collective-permute-start(bf16[1040,128]{1,0:T(8,128)(2,1)S(1)} %get-tuple-element.51), channel_id=1, source_target_pairs={{0,1},{2,3},{5,6},{7,4},{8,9},{10,11},{13,14},{15,12},{16,17},{18,... | collective-permute-start | bytes 798728 | tf_op jit(solution)/shard_map/ppermute | solution.py:377
  102.3 14.6 %collective-permute-start.8 = (bf16[1040,128]{1,0:T(8,128)(2,1)S(1)}, bf16[1040,128]{1,0:T(8,128)(2,1)S(1)}, u32[]{:S(2)}, u32[]{:S(2)}) collective-permute-start(bf16[1040,128]{1,0:T(8,128)(2,1)S(1)} %get-tuple-element.53), channel_id=1, source_target_pairs={{0,3},{2,1},{5,4},{7,6},{8,11},{10,9},{13,12},{15,14},{16,19},{18,... | collective-permute-start | bytes 798728 | tf_op jit(solution)/shard_map/ppermute | solution.py:377
  116.9 25.7 %copy-start.14 = (bf16[256,256]{1,0:T(8,128)(2,1)S(1)}, bf16[256,256]{1,0:T(8,128)(2,1)}, u32[]{:S(2)}) copy-start(bf16[256,256]{1,0:T(8,128)(2,1)} %copy-done.13) | copy-start | bytes 393220
  166.7 9.4 %collective-permute-start.11 = (bf16[528,128]{1,0:T(8,128)(2,1)S(1)}, bf16[528,128]{1,0:T(8,128)(2,1)S(1)}, u32[]{:S(2)}, u32[]{:S(2)}) collective-permute-start(bf16[528,128]{1,0:T(8,128)(2,1)S(1)} %back_far.1), channel_id=1, source_target_pairs={{0,2},{1,3},{2,0},{3,1},{4,6},{5,7},{6,4},{7,5},{8,10},{9,11},{10,... | collective-permute-start | bytes 405512 | tf_op jit(solution)/shard_map/ppermute | solution.py:364
  168.7 6.9 %collective-permute-start.10 = (bf16[4,128,128]{2,1,0:T(8,128)(2,1)S(1)}, bf16[4,128,128]{2,1,0:T(8,128)(2,1)S(1)}, u32[]{:S(2)}, u32[]{:S(2)}) collective-permute-start(bf16[4,128,128]{2,1,0:T(8,128)(2,1)S(1)} %get-tuple-element.58), channel_id=1, source_target_pairs={{0,3},{1,0},{2,1},{3,2},{4,7},{5,4},{6,5},{7,6},{8,11},{9,8},{10,9... | collective-permute-start | bytes 393224 | tf_op jit(solution)/shard_map/ppermute | solution.py:364
  170.4 5.6 %collective-permute-start.9 = (bf16[4,128,128]{2,1,0:T(8,128)(2,1)S(1)}, bf16[4,128,128]{2,1,0:T(8,128)(2,1)S(1)}, u32[]{:S(2)}, u32[]{:S(2)}) collective-permute-start(bf16[4,128,128]{2,1,0:T(8,128)(2,1)S(1)} %get-tuple-element.57), channel_id=1, source_target_pairs={{0,1},{1,2},{2,3},{3,0},{4,5},{5,6},{6,7},{7,4},{8,9},{9,10},{10,1... | collective-permute-start | bytes 393224 | tf_op jit(solution)/shard_map/ppermute | solution.py:364
  (7 other events, 11.9 us)

commit v9 on v8

--- a/solution.py
+++ b/solution.py
@@ -11,7 +11,7 @@
 LANES = 128
 
 
-def params(mib=24):
+def params(mib=16):
     return pltpu.CompilerParams(vmem_limit_bytes=mib * 1024 * 1024)
 
 
@@ -350,7 +350,7 @@
         in_specs=[pl.BlockSpec(memory_space=space or pltpu.VMEM)] * len(args),
         out_specs=jax.tree.map(lambda _: pl.BlockSpec(memory_space=space or pltpu.VMEM), shaped[0] if single else shaped),
         scratch_shapes=list(scratch),
-        compiler_params=params(60 if space else 24),
+        compiler_params=params(60 if space else 16),
         cost_estimate=cost(flops, size),
         name=name,
     )(*args)

time: 178 us -> 178 us (level)
  no operation moved by 1% of the time
where the time goes in v9:
time: 178 us
  waiting for transfers between devices  68.8 us (39%)
  blocking collectives  48.3 us (27%)
  starting transfers between devices  38.8 us (22%)
  Pallas kernels  16 us (9%)
  local copies, waits for them, and re-layouts  5.39 us (3%)
    all_to_all x2, blocking collectives, exchange(): lax.all_to_all(operand, axis, split_axis=0, concat_axis=0, tiled=True)  48.3 us
    ppermute x6, waiting for transfers between devices, step(): return lax.ppermute(value, 'panel', [(i, (i + by) % 4) for i in range(4)])  33.1 us
    ppermute x6, waiting for transfers between devices, route(): return lax.ppermute(value, ('chan', 'panel'), pairs)  22.4 us
    all_to_all x2, starting transfers between devices, exchange(): lax.all_to_all(operand, axis, split_axis=0, concat_axis=0, tiled=True)  19.9 us
    pallas_call x13, Pallas kernels, call(): pl.pallas_call(kernel, out_shape=shaped[0] if single else shaped, in_spec...  16 us
    all_to_all x2, waiting for transfers between devices, exchange(): lax.all_to_all(operand, axis, split_axis=0, concat_axis=0, tiled=True)  13.3 us
    ppermute x6, starting transfers between devices, route(): return lax.ppermute(value, ('chan', 'panel'), pairs)  9.84 us
    ppermute x6, starting transfers between devices, step(): return lax.ppermute(value, 'panel', [(i, (i + by) % 4) for i in range(4)])  9.03 us
  transfers between devices with their start and end apart: 14, of which 9 were waited for; matrix products, arithmetic and copies ran while one was open for 0% of the time, Pallas kernels for 2%

profile of v9, /device:TPU:1, one launch (start us, length us, event | category | flops | bytes accessed | tf_op | source)
XLA Modules:
  0.0 177.5 jit_solution(13681153260933628847)
XLA Ops:
  0.0 3.7 %pack.1 = bf16[64,64,128]{2,1,0:T(8,128)(2,1)} custom-call(bf16[2,256,1024]{2,1,0:T(8,128)(2,1)} %eta_ref.3, bf16[2,256,1024]{2,1,0:T(8,128)(2,1)} %gamma_ref.3), custom_call_target="tpu_custom_call" | custom-call | bytes 3145728 | tf_op jit(solution)/shard_map/pack/pallas_call | solution.py:347
  3.8 13.3 %all-to-all-start = ((bf16[64,64,128]{2,1,0:T(8,128)(2,1)}), bf16[64,64,128]{2,1,0:T(8,128)(2,1)S(1)}, u32[]{:S(2)}, u32[]{:S(2)}) async-start(bf16[64,64,128]{2,1,0:T(8,128)(2,1)} %pack.1), calls=%async_computation | async-start | bytes 2097152 | tf_op jit(solution)/shard_map/all_to_all | solution.py:360
  17.2 2.9 %pair.1 = (bf16[2,5,2,128,128]{4,3,2,1,0:T(8,128)(2,1)S(1)}, bf16[2,5,2,128,128]{4,3,2,1,0:T(8,128)(2,1)S(1)}, bf16[2,5,2,128,128]{4,3,2,1,0:T(8,128)(2,1)S(1)}, bf16[2,5,2,128,128]{4,3,2,1,0:T(8,128)(2,1)S(1)}) custom-call(bf16[2,256,1024]{2,1,0:T(8,128)(2,1)S(1)} %copy-done, bf16[2,256,1024]{2,1,0:T(8,128)(2,1)S(1)} %copy-done.1, ...), custom_call_target="tpu_custom_call" | custom-call | flops 2200000000 | bytes 4726784 | tf_op jit(solution)/shard_map/pair/pallas_call | solution.py:347
  22.2 1.4 collective-permute-start.1
  25.2 12.8 %collective-permute-done.plus_ref = bf16[2,5,2,128,128]{4,3,2,1,0:T(8,128)(2,1)S(1)} collective-permute-done((bf16[2,5,2,128,128]{4,3,2,1,0:T(8,128)(2,1)S(1)}, bf16[2,5,2,128,128]{4,3,2,1,0:T(8,128)(2,1)S(1)}, u32[]{:S(2)}, u32[]{:S(2)}) %collective-permute-start) | collective-permute-done | bytes 655392 | tf_op jit(solution)/shard_map/ppermute | solution.py:364
  39.8 5.3 %all-to-all-done.in_ref = bf16[64,64,128]{2,1,0:T(8,128)(2,1)S(1)} async-done(((bf16[64,64,128]{2,1,0:T(8,128)(2,1)}), bf16[64,64,128]{2,1,0:T(8,128)(2,1)S(1)}, u32[]{:S(2)}, u32[]{:S(2)}) %all-to-all-start) | async-done | bytes 1048608 | tf_op jit(solution)/shard_map/all_to_all | solution.py:360
  45.1 1.7 recouple.1
  46.8 6.6 %all-to-all-start.1 = ((bf16[64,64,128]{2,1,0:T(8,128)(2,1)}), bf16[64,64,128]{2,1,0:T(8,128)(2,1)S(1)}, u32[]{:S(2)}, u32[]{:S(2)}) async-start(bf16[64,64,128]{2,1,0:T(8,128)(2,1)} %recouple.1), calls=%async_computation.1 | async-start | bytes 2097152 | tf_op jit(solution)/shard_map/all_to_all | solution.py:360
  53.4 2.8 %collective-permute-start.2 = (bf16[2,5,2,128,128]{4,3,2,1,0:T(8,128)(2,1)S(1)}, bf16[2,5,2,128,128]{4,3,2,1,0:T(8,128)(2,1)S(1)}, u32[]{:S(2)}, u32[]{:S(2)}) collective-permute-start(bf16[2,5,2,128,128]{4,3,2,1,0:T(8,128)(2,1)S(1)} %copy-done.9), channel_id=1, source_target_pairs={{0,2},{1,3},{2,0},{3,1},{4,6},{5,7},{6,4},{7,5},{8,10},{9,11},{10,... | collective-permute-start | bytes 1966088 | tf_op jit(solution)/shard_map/ppermute | solution.py:364
  56.2 14.6 %collective-permute-done.2.far_ref = bf16[2,5,2,128,128]{4,3,2,1,0:T(8,128)(2,1)S(1)} collective-permute-done((bf16[2,5,2,128,128]{4,3,2,1,0:T(8,128)(2,1)S(1)}, bf16[2,5,2,128,128]{4,3,2,1,0:T(8,128)(2,1)S(1)}, u32[]{:S(2)}, u32[]{:S(2)}) %collective-permute-start.2) | collective-permute-done | bytes 655392 | tf_op jit(solution)/shard_map/ppermute | solution.py:364
  73.3 8.0 %all-to-all-done.1.in_ref = bf16[64,64,128]{2,1,0:T(8,128)(2,1)S(1)} async-done(((bf16[64,64,128]{2,1,0:T(8,128)(2,1)}), bf16[64,64,128]{2,1,0:T(8,128)(2,1)S(1)}, u32[]{:S(2)}, u32[]{:S(2)}) %all-to-all-start.1) | async-done | bytes 1048608 | tf_op jit(solution)/shard_map/all_to_all | solution.py:360
  81.5 3.1 %collective-permute-start.3 = (bf16[64,32,128]{2,1,0:T(8,128)(2,1)S(1)}, bf16[64,32,128]{2,1,0:T(8,128)(2,1)S(1)}, u32[]{:S(2)}, u32[]{:S(2)}) collective-permute-start(bf16[64,32,128]{2,1,0:T(8,128)(2,1)S(1)} %get-tuple-element.47), channel_id=1, source_target_pairs={{1,2},{3,0},{6,7},{4,5},{9,10},{11,8},{14,15},{12,13},{17,18},{19,... | collective-permute-start | bytes 1572872 | tf_op jit(solution)/shard_map/ppermute | solution.py:377
  84.6 2.6 %collective-permute-start.4 = (bf16[64,32,128]{2,1,0:T(8,128)(2,1)S(1)}, bf16[64,32,128]{2,1,0:T(8,128)(2,1)S(1)}, u32[]{:S(2)}, u32[]{:S(2)}) collective-permute-start(bf16[64,32,128]{2,1,0:T(8,128)(2,1)S(1)} %get-tuple-element.48), channel_id=1, source_target_pairs={{1,0},{3,2},{6,5},{4,7},{9,8},{11,10},{14,13},{12,15},{17,16},{19,... | collective-permute-start | bytes 1572872 | tf_op jit(solution)/shard_map/ppermute | solution.py:377
  88.1 2.6 %collective-permute-done.3.plus_ref = bf16[64,32,128]{2,1,0:T(8,128)(2,1)S(1)} collective-permute-done((bf16[64,32,128]{2,1,0:T(8,128)(2,1)S(1)}, bf16[64,32,128]{2,1,0:T(8,128)(2,1)S(1)}, u32[]{:S(2)}, u32[]{:S(2)}) %collective-permute-start.3) | collective-permute-done | bytes 524320 | tf_op jit(solution)/shard_map/ppermute | solution.py:377
  90.7 6.4 %collective-permute-done.4.minus_ref = bf16[64,32,128]{2,1,0:T(8,128)(2,1)S(1)} collective-permute-done((bf16[64,32,128]{2,1,0:T(8,128)(2,1)S(1)}, bf16[64,32,128]{2,1,0:T(8,128)(2,1)S(1)}, u32[]{:S(2)}, u32[]{:S(2)}) %collective-permute-start.4) | collective-permute-done | bytes 524320 | tf_op jit(solution)/shard_map/ppermute | solution.py:377
  97.1 3.2 %product.1 = (bf16[1040,128]{1,0:T(8,128)(2,1)S(1)}, bf16[1040,128]{1,0:T(8,128)(2,1)S(1)}, bf16[1056,128]{1,0:T(8,128)(2,1)S(1)}, bf16[1040,128]{1,0:T(8,128)(2,1)S(1)}) custom-call(bf16[64,64,128]{2,1,0:T(8,128)(2,1)S(1)} %all-to-all-done.1.in_ref, bf16[64,32,128]{2,1,0:T(8,128)(2,1)S(1)} %collective-permute-done.3.plus_ref, ...), custom_call_target="tpu_custom_call" | custom-call | flops 2200000000 | bytes 3698688 | tf_op jit(solution)/shard_map/product/pallas_call | solution.py:347
  101.0 1.3 collective-permute-start.6
  103.6 13.3 %collective-permute-done.6.plus_ref = bf16[1040,128]{1,0:T(8,128)(2,1)S(1)} collective-permute-done((bf16[1040,128]{1,0:T(8,128)(2,1)S(1)}, bf16[1040,128]{1,0:T(8,128)(2,1)S(1)}, u32[]{:S(2)}, u32[]{:S(2)}) %collective-permute-start.6) | collective-permute-done | bytes 266272 | tf_op jit(solution)/shard_map/ppermute | solution.py:377
  117.8 24.9 %all_to_all.20.in_ref = bf16[64,40,128]{2,1,0:T(8,128)(2,1)S(1)} all-to-all(bf16[64,40,128]{2,1,0:T(8,128)(2,1)S(1)} %part.1), channel_id=1, replica_groups=mesh['chan'=64,'panel'=4] {'chan'}, dimensions={0} | all-to-all | bytes 1310720 | tf_op jit(solution)/shard_map/all_to_all | solution.py:360
  143.2 23.4 %all_to_all.21.in_ref = bf16[64,32,128]{2,1,0:T(8,128)(2,1)S(1)} all-to-all(bf16[64,32,128]{2,1,0:T(8,128)(2,1)S(1)} %get-tuple-element.54), channel_id=1, replica_groups=mesh['chan'=64,'panel'=4] {'chan'}, dimensions={0} | all-to-all | bytes 1048576 | tf_op jit(solution)/shard_map/all_to_all | solution.py:360
  166.7 1.8 %collective-permute-start.11 = (bf16[528,128]{1,0:T(8,128)(2,1)S(1)}, bf16[528,128]{1,0:T(8,128)(2,1)S(1)}, u32[]{:S(2)}, u32[]{:S(2)}) collective-permute-start(bf16[528,128]{1,0:T(8,128)(2,1)S(1)} %back_far.1), channel_id=1, source_target_pairs={{0,2},{1,3},{2,0},{3,1},{4,6},{5,7},{6,4},{7,5},{8,10},{9,11},{10,... | collective-permute-start | bytes 405512 | tf_op jit(solution)/shard_map/ppermute | solution.py:364
  168.7 1.7 collective-permute-start.10
  170.4 5.2 %collective-permute-done.10.minus_ref = bf16[4,128,128]{2,1,0:T(8,128)(2,1)S(1)} collective-permute-done((bf16[4,128,128]{2,1,0:T(8,128)(2,1)S(1)}, bf16[4,128,128]{2,1,0:T(8,128)(2,1)S(1)}, u32[]{:S(2)}, u32[]{:S(2)}) %collective-permute-start.10) | collective-permute-done | bytes 131104 | tf_op jit(solution)/shard_map/ppermute | solution.py:364
  176.0 1.5 finish.1
  (54 shorter events, 12.9 us)
Async XLA Ops:
  0.0 17.1 %copy-start.15 = (f32[2,1024]{1,0:T(2,128)S(1)}, f32[2,1024]{1,0:T(2,128)}, u32[]{:S(2)}) copy-start(f32[2,1024]{1,0:T(2,128)} %param.9) | copy-start | bytes 24580
  0.0 17.1 %copy-start.16 = (s32[2]{0:T(128)S(1)}, s32[2]{0:T(128)}, u32[]{:S(2)}) copy-start(s32[2]{0:T(128)} %param.11) | copy-start | bytes 28
  3.7 13.4 %copy-start = (bf16[2,256,1024]{2,1,0:T(8,128)(2,1)S(1)}, bf16[2,256,1024]{2,1,0:T(8,128)(2,1)}, u32[]{:S(2)}) copy-start(bf16[2,256,1024]{2,1,0:T(8,128)(2,1)} %eta_ref.3) | copy-start | bytes 3145732
  3.8 13.4 %copy-start.1 = (bf16[2,256,1024]{2,1,0:T(8,128)(2,1)S(1)}, bf16[2,256,1024]{2,1,0:T(8,128)(2,1)}, u32[]{:S(2)}) copy-start(bf16[2,256,1024]{2,1,0:T(8,128)(2,1)} %gamma_ref.3) | copy-start | bytes 3145732
  3.8 41.3 %all-to-all-start = ((bf16[64,64,128]{2,1,0:T(8,128)(2,1)}), bf16[64,64,128]{2,1,0:T(8,128)(2,1)S(1)}, u32[]{:S(2)}, u32[]{:S(2)}) async-start(bf16[64,64,128]{2,1,0:T(8,128)(2,1)} %pack.1), calls=%async_computation | async-start | bytes 2097152 | tf_op jit(solution)/shard_map/all_to_all | solution.py:360
  17.2 6.5 %copy-start.10 = (bf16[128,128]{1,0:T(8,128)(2,1)S(1)}, bf16[128,128]{1,0:T(8,128)(2,1)}, u32[]{:S(2)}) copy-start(bf16[128,128]{1,0:T(8,128)(2,1)} %forward_ref.1) | copy-start | bytes 98308
  21.0 17.1 %copy-start.2 = (bf16[2,5,2,128,128]{4,3,2,1,0:T(8,128)(2,1)}, bf16[2,5,2,128,128]{4,3,2,1,0:T(8,128)(2,1)S(1)}, u32[]{:S(2)}) copy-start(bf16[2,5,2,128,128]{4,3,2,1,0:T(8,128)(2,1)S(1)} %get-tuple-element.41.own_ref) | copy-start | bytes 1966084
  21.0 17.1 %collective-permute-start = (bf16[2,5,2,128,128]{4,3,2,1,0:T(8,128)(2,1)S(1)}, bf16[2,5,2,128,128]{4,3,2,1,0:T(8,128)(2,1)S(1)}, u32[]{:S(2)}, u32[]{:S(2)}) collective-permute-start(bf16[2,5,2,128,128]{4,3,2,1,0:T(8,128)(2,1)S(1)} %get-tuple-element.38), channel_id=1, source_target_pairs={{0,1},{1,2},{2,3},{3,0},{4,5},{5,6},{6,7},{7,4},{8,9},{9,10},{10,1... | collective-permute-start | bytes 1966088 | tf_op jit(solution)/shard_map/ppermute | solution.py:364
  22.2 16.7 %collective-permute-start.1 = (bf16[2,5,2,128,128]{4,3,2,1,0:T(8,128)(2,1)S(1)}, bf16[2,5,2,128,128]{4,3,2,1,0:T(8,128)(2,1)S(1)}, u32[]{:S(2)}, u32[]{:S(2)}) collective-permute-start(bf16[2,5,2,128,128]{4,3,2,1,0:T(8,128)(2,1)S(1)} %get-tuple-element.39), channel_id=1, source_target_pairs={{0,3},{1,0},{2,1},{3,2},{4,7},{5,4},{6,5},{7,6},{8,11},{9,8},{10,9... | collective-permute-start | bytes 1966088 | tf_op jit(solution)/shard_map/ppermute | solution.py:364
  46.7 6.6 %copy-start.9 = (bf16[2,5,2,128,128]{4,3,2,1,0:T(8,128)(2,1)S(1)}, bf16[2,5,2,128,128]{4,3,2,1,0:T(8,128)(2,1)}, u32[]{:S(2)}) copy-start(bf16[2,5,2,128,128]{4,3,2,1,0:T(8,128)(2,1)} %copy-done.8) | copy-start | bytes 1966084
  46.8 24.1 %copy-start.3 = (bf16[2,5,2,128,128]{4,3,2,1,0:T(8,128)(2,1)S(1)}, bf16[2,5,2,128,128]{4,3,2,1,0:T(8,128)(2,1)}, u32[]{:S(2)}) copy-start(bf16[2,5,2,128,128]{4,3,2,1,0:T(8,128)(2,1)} %copy-done.2) | copy-start | bytes 1966084
  46.8 34.6 %all-to-all-start.1 = ((bf16[64,64,128]{2,1,0:T(8,128)(2,1)}), bf16[64,64,128]{2,1,0:T(8,128)(2,1)S(1)}, u32[]{:S(2)}, u32[]{:S(2)}) async-start(bf16[64,64,128]{2,1,0:T(8,128)(2,1)} %recouple.1), calls=%async_computation.1 | async-start | bytes 2097152 | tf_op jit(solution)/shard_map/all_to_all | solution.py:360
  53.4 17.4 %collective-permute-start.2 = (bf16[2,5,2,128,128]{4,3,2,1,0:T(8,128)(2,1)S(1)}, bf16[2,5,2,128,128]{4,3,2,1,0:T(8,128)(2,1)S(1)}, u32[]{:S(2)}, u32[]{:S(2)}) collective-permute-start(bf16[2,5,2,128,128]{4,3,2,1,0:T(8,128)(2,1)S(1)} %copy-done.9), channel_id=1, source_target_pairs={{0,2},{1,3},{2,0},{3,1},{4,6},{5,7},{6,4},{7,5},{8,10},{9,11},{10,... | collective-permute-start | bytes 1966088 | tf_op jit(solution)/shard_map/ppermute | solution.py:364
  73.3 23.9 %copy-start.12 = (f32[2,1024]{1,0:T(2,128)S(1)}, f32[2,1024]{1,0:T(2,128)}, u32[]{:S(2)}) copy-start(f32[2,1024]{1,0:T(2,128)} %weight_ref.1) | copy-start | bytes 24580
  81.5 9.2 %collective-permute-start.3 = (bf16[64,32,128]{2,1,0:T(8,128)(2,1)S(1)}, bf16[64,32,128]{2,1,0:T(8,128)(2,1)S(1)}, u32[]{:S(2)}, u32[]{:S(2)}) collective-permute-start(bf16[64,32,128]{2,1,0:T(8,128)(2,1)S(1)} %get-tuple-element.47), channel_id=1, source_target_pairs={{1,2},{3,0},{6,7},{4,5},{9,10},{11,8},{14,15},{12,13},{17,18},{19,... | collective-permute-start | bytes 1572872 | tf_op jit(solution)/shard_map/ppermute | solution.py:377
  84.6 12.5 %collective-permute-start.4 = (bf16[64,32,128]{2,1,0:T(8,128)(2,1)S(1)}, bf16[64,32,128]{2,1,0:T(8,128)(2,1)S(1)}, u32[]{:S(2)}, u32[]{:S(2)}) collective-permute-start(bf16[64,32,128]{2,1,0:T(8,128)(2,1)S(1)} %get-tuple-element.48), channel_id=1, source_target_pairs={{1,0},{3,2},{6,5},{4,7},{9,8},{11,10},{14,13},{12,15},{17,16},{19,... | collective-permute-start | bytes 1572872 | tf_op jit(solution)/shard_map/ppermute | solution.py:377
  87.2 10.0 %collective-permute-start.5 = (bf16[64,32,128]{2,1,0:T(8,128)(2,1)S(1)}, bf16[64,32,128]{2,1,0:T(8,128)(2,1)S(1)}, u32[]{:S(2)}, u32[]{:S(2)}) collective-permute-start(bf16[64,32,128]{2,1,0:T(8,128)(2,1)S(1)} %send_far.1), channel_id=1, source_target_pairs={{0,2},{2,0},{5,7},{7,5},{8,10},{10,8},{13,15},{15,13},{16,18},{18,... | collective-permute-start | bytes 1572872 | tf_op jit(solution)/shard_map/ppermute | solution.py:377
  100.3 16.6 %collective-permute-start.7 = (bf16[1056,128]{1,0:T(8,128)(2,1)S(1)}, bf16[1056,128]{1,0:T(8,128)(2,1)S(1)}, u32[]{:S(2)}, u32[]{:S(2)}) collective-permute-start(bf16[1056,128]{1,0:T(8,128)(2,1)S(1)} %get-tuple-element.52), channel_id=1, source_target_pairs={{0,2},{2,0},{5,7},{7,5},{8,10},{10,8},{13,15},{15,13},{16,18},{18,... | collective-permute-start | bytes 811016 | tf_op jit(solution)/shard_map/ppermute | solution.py:377
  101.0 15.9 %collective-permute-start.6 = (bf16[1040,128]{1,0:T(8,128)(2,1)S(1)}, bf16[1040,128]{1,0:T(8,128)(2,1)S(1)}, u32[]{:S(2)}, u32[]{:S(2)}) collective-permute-start(bf16[1040,128]{1,0:T(8,128)(2,1)S(1)} %get-tuple-element.51), channel_id=1, source_target_pairs={{0,1},{2,3},{5,6},{7,4},{8,9},{10,11},{13,14},{15,12},{16,17},{18,... | collective-permute-start | bytes 798728 | tf_op jit(solution)/shard_map/ppermute | solution.py:377
  102.3 14.6 %collective-permute-start.8 = (bf16[1040,128]{1,0:T(8,128)(2,1)S(1)}, bf16[1040,128]{1,0:T(8,128)(2,1)S(1)}, u32[]{:S(2)}, u32[]{:S(2)}) collective-permute-start(bf16[1040,128]{1,0:T(8,128)(2,1)S(1)} %get-tuple-element.53), channel_id=1, source_target_pairs={{0,3},{2,1},{5,4},{7,6},{8,11},{10,9},{13,12},{15,14},{16,19},{18,... | collective-permute-start | bytes 798728 | tf_op jit(solution)/shard_map/ppermute | solution.py:377
  116.9 25.7 %copy-start.14 = (bf16[256,256]{1,0:T(8,128)(2,1)S(1)}, bf16[256,256]{1,0:T(8,128)(2,1)}, u32[]{:S(2)}) copy-start(bf16[256,256]{1,0:T(8,128)(2,1)} %copy-done.13) | copy-start | bytes 393220
  166.7 9.4 %collective-permute-start.11 = (bf16[528,128]{1,0:T(8,128)(2,1)S(1)}, bf16[528,128]{1,0:T(8,128)(2,1)S(1)}, u32[]{:S(2)}, u32[]{:S(2)}) collective-permute-start(bf16[528,128]{1,0:T(8,128)(2,1)S(1)} %back_far.1), channel_id=1, source_target_pairs={{0,2},{1,3},{2,0},{3,1},{4,6},{5,7},{6,4},{7,5},{8,10},{9,11},{10,... | collective-permute-start | bytes 405512 | tf_op jit(solution)/shard_map/ppermute | solution.py:364
  168.7 6.9 %collective-permute-start.10 = (bf16[4,128,128]{2,1,0:T(8,128)(2,1)S(1)}, bf16[4,128,128]{2,1,0:T(8,128)(2,1)S(1)}, u32[]{:S(2)}, u32[]{:S(2)}) collective-permute-start(bf16[4,128,128]{2,1,0:T(8,128)(2,1)S(1)} %get-tuple-element.58), channel_id=1, source_target_pairs={{0,3},{1,0},{2,1},{3,2},{4,7},{5,4},{6,5},{7,6},{8,11},{9,8},{10,9... | collective-permute-start | bytes 393224 | tf_op jit(solution)/shard_map/ppermute | solution.py:364
  170.4 5.6 %collective-permute-start.9 = (bf16[4,128,128]{2,1,0:T(8,128)(2,1)S(1)}, bf16[4,128,128]{2,1,0:T(8,128)(2,1)S(1)}, u32[]{:S(2)}, u32[]{:S(2)}) collective-permute-start(bf16[4,128,128]{2,1,0:T(8,128)(2,1)S(1)} %get-tuple-element.57), channel_id=1, source_target_pairs={{0,1},{1,2},{2,3},{3,0},{4,5},{5,6},{6,7},{7,4},{8,9},{9,10},{10,1... | collective-permute-start | bytes 393224 | tf_op jit(solution)/shard_map/ppermute | solution.py:364
  (7 other events, 11.9 us)
